TPU v7x, 32 devices: a whole 2x2x4 slice. The times are simulated.
32 devices in a mesh: region: 16 (over z, y, x), dom: 2 (over core).
Axes of the slice: x: 2, y: 2, z: 4, core: 2. Of those that a mesh axis runs over, the one named last changes fastest.
Arguments:
- fine_state: float32 [16384, 128], P(('region', 'dom')), may hold values from -6 to 6
- fine_nbr: int32 [16, 16384], P(None, ('region', 'dom')), may hold values from 0 to 575
- fine_mask: int32 [16, 16384], P(None, ('region', 'dom')), may hold values 0 or 1
- send_rows: int32 [4, 512], P(None, ('region', 'dom')), may hold values from 0 to 511
- coarse_nbr: int32 [16, 4096], P(None, ('region', 'dom')), may hold values from 0 to 255
- coarse_mask: int32 [16, 4096], P(None, ('region', 'dom')), may hold values 0 or 1
- parent: int32 [16384], P(('region', 'dom')), may hold values from 0 to 4095, as said below
- interp_share: int32 [16384], P(('region', 'dom')), may hold values from 1 to 4
- edge_w: float32 [4, 3, 128, 128], replicated, may hold values from -0.375 to 0.375
- node_w: float32 [4, 3, 128, 128], replicated, may hold values from -0.375 to 0.375
- biases: float32 [4, 4, 128], replicated, may hold values from -3 to 3
Outputs:
- fine_out: float32 [16384, 128], P(('region', 'dom'))
- coarse_out: float32 [4096, 128], P(('region', 'dom'))
Inputs may be any that keep to these rules, and one draw needn't show every extreme that they name: `parent`: of the 512 fine nodes of block (r, d), 448 have parents in coarse blocks of region r, at most 384 in any one block and exactly 384 in some block; 32 have parents in blocks of region r-1 and 32 in blocks of region r+1 (periodic), at most 32 in any one block and exactly 32 in some block of each.
All inputs are finite; a program needn't handle non-finite values. No bound on the sum of `fine_mask` or of `coarse_mask` on one device may be relied on, other than what follows from the above.
Results may differ from a plain program's by a relative error of at most 0.0001.
Values sent between devices are 32-bit elements; how exact they have to be, the bound alone decides.
No kernel may reach another device: no remote copies, remote signals or barrier semaphores. Data moves between devices by JAX's collectives and lax.ppermute only.
A program may use at most 64 MiB of HBM per device.

v0:
```python
import functools

import jax
import jax.numpy as jnp
from jax import lax
from jax.experimental import pallas as pl
from jax.experimental.pallas import tpu as pltpu
from jax.sharding import PartitionSpec as P

epsilon = 1e-05
f32 = jnp.float32
bf16 = jnp.bfloat16
LANES = 128
VMEM_BYTES = 32 * 2**20


def split(values):
    high = values.astype(bf16)
    low = (values - high.astype(f32)).astype(bf16)
    return high, low


def left_factor(weight):
    high, low = split(weight.T)
    return jnp.concatenate(
        [jnp.concatenate([high, high], axis=1), jnp.concatenate([low, low], axis=1)], axis=0
    )


def folded(stacked):
    half = stacked.shape[0] // 2
    return stacked[:half] + stacked[half:]


def times(factor, columns):
    high, low = split(columns)
    stacked = jnp.concatenate([high, low], axis=0)
    return folded(jnp.dot(factor, stacked, preferred_element_type=f32))


def centered(weight):
    return weight - jnp.mean(weight, axis=-1, keepdims=True)


def bias_column(row, width):
    block = jnp.broadcast_to(row, (LANES, row.shape[-1])).T
    return jnp.concatenate([block] * (width // LANES), axis=1)


def scaled(columns):
    spread = jnp.mean(columns * columns, axis=0, keepdims=True)
    return columns * lax.rsqrt(spread + epsilon)


def lane_gather(source, index):
    features = source.shape[0]
    blocks = source.shape[1] // LANES
    pieces = []
    for start in range(0, index.shape[1], LANES):
        wide = jnp.broadcast_to(index[:, start : start + LANES], (features, LANES))
        inner = wide & (LANES - 1)
        outer = wide // LANES
        found = jnp.take_along_axis(source[:, :LANES], inner, axis=1)
        for block in range(1, blocks):
            piece = source[:, block * LANES : (block + 1) * LANES]
            found = jnp.where(outer == block, jnp.take_along_axis(piece, inner, axis=1), found)
        pieces.append(found)
    return jnp.concatenate(pieces, axis=1)


def layer_columns(own, sources, neighbours, validity, edge_ref, node_ref, bias_ref):
    count = own.shape[1]
    biases = bias_ref[0]
    own_term = times(left_factor(edge_ref[0, 0]), own) + bias_column(biases[0:1], count)
    source_proj = times(left_factor(edge_ref[0, 1]), sources)
    second = left_factor(centered(edge_ref[0, 2]))
    second_bias = bias_column(centered(biases[1:2]), count)
    gathered = jnp.zeros(own.shape, f32)
    for slot in range(neighbours.shape[0]):
        index_row = neighbours[slot : slot + 1, :]
        valid_row = validity[slot : slot + 1, :]
        hidden = jnp.maximum(own_term + lane_gather(source_proj, index_row), 0.0)
        message = times(second, hidden) + second_bias
        spread = jnp.mean(message * message, axis=0, keepdims=True)
        gathered = gathered + message * (lax.rsqrt(spread + epsilon) * valid_row.astype(f32))
    inner_act = jnp.maximum(
        times(left_factor(node_ref[0, 0]), own)
        + times(left_factor(node_ref[0, 1]), gathered)
        + bias_column(biases[2:3], count),
        0.0,
    )
    update = times(left_factor(centered(node_ref[0, 2])), inner_act)
    return own + scaled(update + bias_column(centered(biases[3:4]), count))


def iota(shape, axis):
    return lax.broadcasted_iota(jnp.int32, shape, axis)


def hot(rows, index):
    return (iota((rows, index.shape[1]), 0) == index).astype(f32)


def pick_kernel(
    rim, send_ref, parent_s, share_s, state_ref, nbr_ref, mask_ref, even_ref, odd_ref, dom_ref
):
    even = lax.rem(lax.axis_index("region"), 2) == 0
    first = jnp.where(even, 1, 0)
    lane = iota((1, LANES), 1)

    def fill(out, out_base, direction, lane_base, parents, shares):
        for k in range(rim):
            row = send_ref[direction, k]
            out[pl.ds(out_base + k, 1), :] = state_ref[pl.ds(row, 1), :]
            here = lane == lane_base + k
            parents = jnp.where(here, parent_s[row].astype(f32), parents)
            shares = jnp.where(here, share_s[row].astype(f32), shares)
        return parents, shares

    zero = jnp.zeros((1, LANES), f32)
    for out, direction in ((even_ref, first), (odd_ref, 1 - first)):
        parents, shares = fill(out, 0, direction, direction * rim, zero, zero)
        out[rim : rim + 8, :] = jnp.zeros((8, LANES), f32)
        out[rim : rim + 1, :] = parents
        out[rim + 1 : rim + 2, :] = shares
    parents, shares = fill(dom_ref, 0, 2, 2 * rim, zero, zero)
    parents, shares = fill(dom_ref, rim, 3, 3 * rim, parents, shares)
    base = 2 * rim
    dom_ref[base : base + 8, :] = jnp.zeros((8, LANES), f32)
    dom_ref[base : base + 1, :] = parents
    dom_ref[base + 1 : base + 2, :] = shares
    slots = nbr_ref.shape[0]
    dom_ref[base + 8 : base + 8 + slots, :] = nbr_ref[...].astype(f32)
    dom_ref[base + 8 + slots : base + 8 + 2 * slots, :] = mask_ref[...].astype(f32)


def rim_rows(rim, even, recv_even, recv_odd, recv_dom):
    low = jnp.where(even, recv_even, recv_odd)
    high = jnp.where(even, recv_odd, recv_even)
    pad = jnp.zeros((LANES - 4 * rim, low.shape[1]), f32)
    return jnp.concatenate([low, high, recv_dom, pad], axis=0)


def fine_kernel(
    rim,
    group,
    side,
    regions,
    send_ref,
    state_ref,
    recv_even,
    recv_odd,
    recv_dom,
    nbr_ref,
    mask_ref,
    parent_ref,
    share_ref,
    edge_ref,
    node_ref,
    bias_ref,
    fine_ref,
    even_ref,
    odd_ref,
    dom_ref,
    rows_ref,
):
    region = lax.axis_index("region")
    even = lax.rem(region, 2) == 0
    own = state_ref[...].T
    outer = rim_rows(rim, even, recv_even[:rim], recv_odd[:rim], recv_dom[: 2 * rim]).T
    sources = jnp.concatenate([own, outer], axis=1)
    fine = layer_columns(own, sources, nbr_ref, mask_ref, edge_ref, node_ref, bias_ref)
    fine_ref[...] = fine
    rows = fine.T
    rows_ref[...] = rows
    count = rows.shape[0]
    pair = jnp.concatenate(split(rows), axis=1)

    def weighted(selection):
        both = jnp.dot(selection.astype(bf16), pair, preferred_element_type=f32)
        return both[:, :LANES] + both[:, LANES:]

    parent = parent_ref[...]
    share = share_ref[...].astype(f32)
    chosen = hot(group, parent - region * group) * share
    dom_ref[0:group, :] = weighted(chosen)
    ones = jnp.ones((8, count), f32)
    totals = lax.dot_general(
        ones, chosen, (((1,), (1,)), ((), ())), preferred_element_type=f32
    )
    for block in range(group // LANES):
        dom_ref[group + 8 * block : group + 8 * (block + 1), :] = totals[
            :, block * LANES : (block + 1) * LANES
        ]
    base = group + 8 * (group // LANES)
    for k in range(2 * rim):
        row = send_ref[2 + k // rim, k % rim]
        dom_ref[base + k : base + k + 1, :] = rows_ref[pl.ds(row, 1), :]

    below = lax.rem(region + regions - 1, regions)
    above = lax.rem(region + 1, regions)
    earlier = (iota((count, count), 0) < iota((count, count), 1)).astype(bf16)
    first = jnp.where(even, 1, 0)
    for out, target, direction in (
        (even_ref, jnp.where(even, below, above), first),
        (odd_ref, jnp.where(even, above, below), 1 - first),
    ):
        local = parent - target * group
        inside = (local >= 0) & (local < group)
        member = jnp.where(inside, 1.0, 0.0)
        rank = jnp.dot(
            jnp.broadcast_to(member, (8, count)).astype(bf16), earlier, preferred_element_type=f32
        )[0:1]
        place = jnp.where(inside, rank.astype(jnp.int32), -1)
        picked = hot(LANES, place)
        out[0:side, :] = weighted((picked * share)[:side])
        facts = jnp.concatenate(
            [local.astype(f32), share, jnp.zeros((6, count), f32)], axis=0
        )
        out[side : side + 8, :] = lax.dot_general(
            facts,
            picked,
            (((1,), (1,)), ((), ())),
            precision=lax.Precision.HIGHEST,
            preferred_element_type=f32,
        )
        for k in range(rim):
            row = send_ref[direction, k]
            out[side + 8 + k : side + 9 + k, :] = rows_ref[pl.ds(row, 1), :]
        out[side + 8 + rim :, :] = jnp.zeros((out.shape[0] - side - 8 - rim, LANES), f32)


def coarse_kernel(
    rim,
    group,
    side,
    mine_ref,
    other_ref,
    even_mine,
    odd_mine,
    even_other,
    odd_other,
    nbr_ref,
    mask_ref,
    recv_dom,
    edge_one,
    node_one,
    bias_one,
    edge_two,
    node_two,
    bias_two,
    group_ref,
    out_ref,
    rows_ref,
):
    dom = lax.axis_index("dom")
    total = mine_ref[0:group, :] + other_ref[0:group, :]
    weight = [
        mine_ref[group + 8 * b : group + 8 * b + 8, :]
        + other_ref[group + 8 * b : group + 8 * b + 8, :]
        for b in range(group // LANES)
    ]
    weight = jnp.concatenate(weight, axis=1)
    for block in (even_mine, odd_mine, even_other, odd_other):
        depth = block.shape[0]
        known = iota((1, depth), 1) < side
        index = jnp.where(known, block[side : side + 1, :depth].astype(jnp.int32), -1)
        share = jnp.where(known, block[side + 1 : side + 2, :depth], 0.0)
        chosen = hot(group, index)
        both = jnp.dot(
            chosen.astype(bf16),
            jnp.concatenate(split(block[...]), axis=1),
            preferred_element_type=f32,
        )
        total = total + (both[:, :LANES] + both[:, LANES:])
        weight = weight + lax.dot_general(
            jnp.broadcast_to(share, (8, depth)),
            chosen,
            (((1,), (1,)), ((), ())),
            preferred_element_type=f32,
        )
    columns = total.T / jnp.maximum(weight[0:1], 1.0)
    base = 2 * rim + 8
    slots = nbr_ref.shape[0]
    mine_first = dom == 0

    def ordered(mine, other):
        return jnp.concatenate(
            [jnp.where(mine_first, mine, other), jnp.where(mine_first, other, mine)], axis=1
        )

    nbr = ordered(nbr_ref[...], recv_dom[base : base + slots, :].astype(jnp.int32))
    mask = ordered(mask_ref[...], recv_dom[base + slots : base + 2 * slots, :].astype(jnp.int32))
    columns = layer_columns(columns, columns, nbr, mask, edge_one, node_one, bias_one)
    columns = layer_columns(columns, columns, nbr, mask, edge_two, node_two, bias_two)
    group_ref[...] = columns
    rows_ref[...] = columns.T
    own = out_ref.shape[0]
    out_ref[...] = rows_ref[pl.ds(pl.multiple_of(dom * own, own), own), :]


def last_kernel(
    rim,
    group,
    side,
    regions,
    fine_ref,
    rim_even,
    rim_odd,
    rim_dom,
    meta_even,
    meta_odd,
    meta_dom,
    coarse_mine,
    coarse_even,
    coarse_odd,
    coarse_even_two,
    coarse_odd_two,
    nbr_ref,
    mask_ref,
    parent_ref,
    share_ref,
    edge_ref,
    node_ref,
    bias_ref,
    out_ref,
):
    region = lax.axis_index("region")
    even = lax.rem(region, 2) == 0
    even_two = lax.rem(region // 2, 2) == 0
    count = fine_ref.shape[1]
    base = side + 8
    dom_base = group + 8 * (group // LANES)
    outer = rim_rows(
        rim,
        even,
        rim_even[base : base + rim, :],
        rim_odd[base : base + rim, :],
        rim_dom[dom_base : dom_base + 2 * rim, :],
    ).T
    facts = (
        meta_even[rim : rim + 8, :]
        + meta_odd[rim : rim + 8, :]
        + meta_dom[2 * rim : 2 * rim + 8, :]
    )
    known = iota((1, LANES), 1) < 4 * rim
    outer_parent = jnp.where(known, facts[0:1].astype(jnp.int32), -1)
    outer_share = jnp.where(known, facts[1:2], 0.0)
    parent = jnp.concatenate([parent_ref[...], outer_parent], axis=1)
    share = jnp.concatenate([share_ref[...].astype(f32), outer_share], axis=1)

    def found(block, home, index):
        chosen = hot(group, index - home * group).astype(bf16)
        stacked = jnp.concatenate(split(block[...]), axis=0)
        return folded(jnp.dot(stacked, chosen, preferred_element_type=f32))

    def shifted(steps):
        return lax.rem(region + steps + regions, regions)

    added = found(coarse_mine, region, parent)
    added = added + found(coarse_even, jnp.where(even, shifted(-1), shifted(1)), parent)
    added = added + found(coarse_odd, jnp.where(even, shifted(1), shifted(-1)), parent)
    far = found(coarse_even_two, jnp.where(even_two, shifted(-2), shifted(2)), outer_parent)
    far = far + found(coarse_odd_two, jnp.where(even_two, shifted(2), shifted(-2)), outer_parent)
    added = jnp.concatenate([added[:, :count], added[:, count:] + far], axis=1)
    sources = jnp.concatenate([fine_ref[...], outer], axis=1) + (share * 0.25) * added
    result = layer_columns(
        sources[:, :count], sources, nbr_ref, mask_ref, edge_ref, node_ref, bias_ref
    )
    out_ref[...] = result.T


def whole():
    return pl.BlockSpec(memory_space=pltpu.VMEM)


def scalars():
    return pl.BlockSpec(memory_space=pltpu.SMEM)


def layer_specs(layer, feature_dim):
    return [
        pl.BlockSpec((1, 3, feature_dim, feature_dim), lambda step: (layer, 0, 0, 0)),
        pl.BlockSpec((1, 3, feature_dim, feature_dim), lambda step: (layer, 0, 0, 0)),
        pl.BlockSpec((1, 4, feature_dim), lambda step: (layer, 0, 0)),
    ]


def kernel_call(body, in_specs, outs, scratch=()):
    return pl.pallas_call(
        body,
        grid=(1,),
        in_specs=in_specs,
        out_specs=tuple(whole() for _ in outs),
        out_shape=tuple(jax.ShapeDtypeStruct(shape, f32) for shape in outs),
        scratch_shapes=list(scratch),
        compiler_params=pltpu.CompilerParams(vmem_limit_bytes=VMEM_BYTES),
    )


def swap(value, axis, partner, count):
    return lax.ppermute(value, axis, [(source, partner(source) % count) for source in range(count)])


def body(
    fine_state,
    fine_nbr,
    fine_mask,
    send_rows,
    coarse_nbr,
    coarse_mask,
    parent,
    interp_share,
    edge_w,
    node_w,
    biases,
):
    count, width = fine_state.shape
    own_coarse = coarse_nbr.shape[1]
    slots = coarse_nbr.shape[0]
    regions = lax.axis_size("region")
    domains = lax.axis_size("dom")
    group = domains * own_coarse
    rim = send_rows.shape[1]
    side = count // (8 * domains)
    weights = (edge_w, node_w, biases)

    def even_swap(value):
        return swap(value, "region", lambda r: r - 1 if r % 2 == 0 else r + 1, regions)

    def odd_swap(value):
        return swap(value, "region", lambda r: r + 1 if r % 2 == 0 else r - 1, regions)

    def even_two_swap(value):
        return swap(value, "region", lambda r: r - 2 if r // 2 % 2 == 0 else r + 2, regions)

    def odd_two_swap(value):
        return swap(value, "region", lambda r: r + 2 if r // 2 % 2 == 0 else r - 2, regions)

    def dom_swap(value):
        return swap(value, "dom", lambda d: d + 1, domains)

    even_out, odd_out, dom_out = kernel_call(
        functools.partial(pick_kernel, rim),
        [scalars(), scalars(), scalars(), whole(), whole(), whole()],
        [(rim + 8, width), (rim + 8, width), (2 * rim + 8 + 2 * slots, width)],
    )(send_rows, parent, interp_share, fine_state, coarse_nbr, coarse_mask)
    meta_even = even_swap(even_out)
    meta_odd = odd_swap(odd_out)
    meta_dom = dom_swap(dom_out)

    parent_row = parent[None, :]
    share_row = interp_share[None, :]
    block_rows = side + 8 + rim + 8
    dom_rows = group + 8 * (group // LANES) + 2 * rim
    fine_one, even_out, odd_out, mine = kernel_call(
        functools.partial(fine_kernel, rim, group, side, regions),
        [scalars()] + [whole()] * 8 + layer_specs(0, width),
        [(width, count), (block_rows, width), (block_rows, width), (dom_rows, width)],
        [pltpu.VMEM((count, width), f32)],
    )(
        send_rows,
        fine_state,
        meta_even,
        meta_odd,
        meta_dom,
        fine_nbr,
        fine_mask,
        parent_row,
        share_row,
        *weights,
    )
    even_mine = even_swap(even_out)
    odd_mine = odd_swap(odd_out)
    other = dom_swap(mine)
    even_other = dom_swap(even_mine)
    odd_other = dom_swap(odd_mine)

    coarse_group, coarse_out = kernel_call(
        functools.partial(coarse_kernel, rim, group, side),
        [whole()] * 9 + layer_specs(1, width) + layer_specs(2, width),
        [(width, group), (own_coarse, width)],
        [pltpu.VMEM((group, width), f32)],
    )(
        mine,
        other,
        even_mine,
        odd_mine,
        even_other,
        odd_other,
        coarse_nbr,
        coarse_mask,
        meta_dom,
        *weights,
        *weights,
    )
    coarse_even = even_swap(coarse_group)
    coarse_even_two = even_two_swap(coarse_group)
    coarse_odd = odd_swap(coarse_group)
    coarse_odd_two = odd_two_swap(coarse_group)

    (fine_out,) = kernel_call(
        functools.partial(last_kernel, rim, group, side, regions),
        [whole()] * 16 + layer_specs(3, width),
        [(count, width)],
    )(
        fine_one,
        even_mine,
        odd_mine,
        other,
        meta_even,
        meta_odd,
        meta_dom,
        coarse_group,
        coarse_even,
        coarse_odd,
        coarse_even_two,
        coarse_odd_two,
        fine_nbr,
        fine_mask,
        parent_row,
        share_row,
        *weights,
    )
    return (fine_out, coarse_out)


def solution(mesh):
    return jax.shard_map(
        body,
        mesh=mesh,
        in_specs=(
            P(("region", "dom"), None),
            P(None, ("region", "dom")),
            P(None, ("region", "dom")),
            P(None, ("region", "dom")),
            P(None, ("region", "dom")),
            P(None, ("region", "dom")),
            P(("region", "dom")),
            P(("region", "dom")),
            P(),
            P(),
            P(),
        ),
        out_specs=(P(("region", "dom"), None), P(("region", "dom"), None)),
        check_vma=False,
    )
```

profile of v0, /device:TPU:0, one launch (start us, length us, event | category | flops | bytes accessed | tf_op | source)
XLA Modules:
  0.0 66.9 jit_solution(16453829442034520685)
XLA Ops:
  0.6 0.0 copy-start.4
  0.6 0.9 %copy-done.4 = f32[512,128]{1,0:T(8,128)S(1)} copy-done((f32[512,128]{1,0:T(8,128)S(1)}, f32[512,128]{1,0:T(8,128)}, u32[]{:S(2)}) %copy-start.4) | copy-done | bytes 262168
  1.6 0.0 copy-start.8
  1.6 0.7 %copy-done.8 = s32[16,128]{1,0:T(8,128)S(1)} copy-done((s32[16,128]{1,0:T(8,128)S(1)}, s32[16,128]{1,0:T(8,128)}, u32[]{:S(2)}) %copy-start.8) | copy-done | bytes 8216
  2.3 0.0 copy-start.10
  2.3 0.7 %copy-done.10 = s32[16,128]{1,0:T(8,128)S(1)} copy-done((s32[16,128]{1,0:T(8,128)S(1)}, s32[16,128]{1,0:T(8,128)}, u32[]{:S(2)}) %copy-start.10) | copy-done | bytes 8216
  3.0 0.0 copy-start.12
  3.0 0.7 %copy-done.12 = s32[512]{0:T(512)S(1)} copy-done((s32[512]{0:T(512)S(1)}, s32[512]{0:T(512)}, u32[]{:S(2)}) %copy-start.12) | copy-done | bytes 2072
  3.7 0.0 copy-start.14
  3.7 0.7 %copy-done.14 = s32[512]{0:T(512)S(1)} copy-done((s32[512]{0:T(512)S(1)}, s32[512]{0:T(512)}, u32[]{:S(2)}) %copy-start.14) | copy-done | bytes 2072
  4.3 0.0 copy-start.15
  4.3 0.7 %copy-done.15 = s32[4,16]{1,0:T(4,128)S(1)} copy-done((s32[4,16]{1,0:T(4,128)S(1)}, s32[4,16]{1,0:T(4,128)}, u32[]{:S(2)}) %copy-start.15) | copy-done | bytes 280
  5.0 0.0 copy-start.5
  5.0 0.0 copy-start.6
  5.0 0.8 %shard_map.122 = (f32[24,128]{1,0:T(8,128)S(1)}, f32[24,128]{1,0:T(8,128)S(1)}, f32[72,128]{1,0:T(8,128)S(1)}) custom-call(s32[4,16]{1,0:T(4,128)S(1)} %copy-done.15, s32[512]{0:T(512)S(1)} %copy-done.12, s32[512]{0:T(512)S(1)} %copy-done.14, f32[512,128]{1,0:T(8,128)S(1)} %copy-done.4, s32[16,128]{1,0:T(8,128)S(1)} %copy-done.8, s32[16,128]{1,0:T(8,128)S(1)} %copy-done.10), custom_call_target="tpu_custom_call" | custom-call | tf_op jit(solution)/shard_map/pallas_call | solution.py:443
  5.8 0.0 copy-start.7
  5.8 0.5 collective-permute-start.2
  6.3 6.6 %collective-permute-start = (f32[24,128]{1,0:T(8,128)S(1)}, f32[24,128]{1,0:T(8,128)S(1)}, u32[]{:S(2)}, u32[]{:S(2)}) collective-permute-start(f32[24,128]{1,0:T(8,128)S(1)} %get-tuple-element.11), channel_id=1, source_target_pairs={{0,30},{2,4},{4,2},{6,8},{8,6},{10,12},{12,10},{14,16},{16,14},{18... | collective-permute-start | bytes 36872 | tf_op jit(solution)/shard_map/ppermute | solution.py:402
  12.9 0.0 collective-permute-start.1
  12.9 1.7 %collective-permute-done.recv_even.meta_even = f32[24,128]{1,0:T(8,128)S(1)} collective-permute-done((f32[24,128]{1,0:T(8,128)S(1)}, f32[24,128]{1,0:T(8,128)S(1)}, u32[]{:S(2)}, u32[]{:S(2)}) %collective-permute-start) | collective-permute-done | bytes 12320 | tf_op jit(solution)/shard_map/ppermute | solution.py:402
  14.6 2.0 %collective-permute-done.1.recv_odd.meta_odd = f32[24,128]{1,0:T(8,128)S(1)} collective-permute-done((f32[24,128]{1,0:T(8,128)S(1)}, f32[24,128]{1,0:T(8,128)S(1)}, u32[]{:S(2)}, u32[]{:S(2)}) %collective-permute-start.1) | collective-permute-done | bytes 12320 | tf_op jit(solution)/shard_map/ppermute | solution.py:402
  16.6 0.0 collective-permute-done.2.recv_dom.meta_dom
  16.6 0.0 copy-done.5
  16.6 0.0 copy-done.6
  16.6 0.0 copy-done.7
  16.6 0.0 copy-start
  16.6 1.1 %copy-done = f32[4,3,128,128]{3,2,1,0:T(8,128)S(1)} copy-done((f32[4,3,128,128]{3,2,1,0:T(8,128)S(1)}, f32[4,3,128,128]{3,2,1,0:T(8,128)}, u32[]{:S(2)}) %copy-start) | copy-done | bytes 786456
  17.8 0.0 copy-start.2
  17.8 1.1 %copy-done.2 = f32[4,3,128,128]{3,2,1,0:T(8,128)S(1)} copy-done((f32[4,3,128,128]{3,2,1,0:T(8,128)S(1)}, f32[4,3,128,128]{3,2,1,0:T(8,128)}, u32[]{:S(2)}) %copy-start.2) | copy-done | bytes 786456
  18.9 0.0 copy-start.1
  18.9 0.0 copy-start.3
  18.9 0.0 copy-start.9
  18.9 0.0 copy-start.11
  18.9 10.0 %shard_map.123 = (f32[128,512]{1,0:T(8,128)S(1)}, f32[64,128]{1,0:T(8,128)S(1)}, f32[64,128]{1,0:T(8,128)S(1)}, f32[304,128]{1,0:T(8,128)S(1)}) custom-call(s32[4,16]{1,0:T(4,128)S(1)} %copy-done.15, f32[512,128]{1,0:T(8,128)S(1)} %copy-done.4, f32[24,128]{1,0:T(8,128)S(1)} %collective-permute-done.recv_even.meta_even, ...), custom_call_target="tpu_custom_call" | custom-call | tf_op jit(solution)/shard_map/pallas_call | solution.py:456
  28.9 0.0 collective-permute-start.5
  28.9 3.6 %collective-permute-start.3 = (f32[64,128]{1,0:T(8,128)S(1)}, f32[64,128]{1,0:T(8,128)S(1)}, u32[]{:S(2)}, u32[]{:S(2)}) collective-permute-start(f32[64,128]{1,0:T(8,128)S(1)} %get-tuple-element.15), channel_id=1, source_target_pairs={{0,30},{2,4},{4,2},{6,8},{8,6},{10,12},{12,10},{14,16},{16,14},{18... | collective-permute-start | bytes 98312 | tf_op jit(solution)/shard_map/ppermute | solution.py:402
  32.6 0.0 collective-permute-start.4
  32.6 3.9 %collective-permute-done.3.even_mine.rim_even = f32[64,128]{1,0:T(8,128)S(1)} collective-permute-done((f32[64,128]{1,0:T(8,128)S(1)}, f32[64,128]{1,0:T(8,128)S(1)}, u32[]{:S(2)}, u32[]{:S(2)}) %collective-permute-start.3) | collective-permute-done | bytes 32800 | tf_op jit(solution)/shard_map/ppermute | solution.py:402
  36.5 0.0 collective-permute-start.6
  36.5 0.0 collective-permute-done.4.odd_mine.rim_odd
  36.5 0.5 collective-permute-start.7
  37.0 0.7 %collective-permute-done.6.even_other = f32[64,128]{1,0:T(8,128)S(1)} collective-permute-done((f32[64,128]{1,0:T(8,128)S(1)}, f32[64,128]{1,0:T(8,128)S(1)}, u32[]{:S(2)}, u32[]{:S(2)}) %collective-permute-start.6) | collective-permute-done | bytes 32800 | tf_op jit(solution)/shard_map/ppermute | solution.py:402
  37.7 0.2 collective-permute-done.7.odd_other
  37.8 0.0 collective-permute-done.5.other_ref.rim_dom
  37.8 0.0 copy-done.1
  37.9 0.0 copy-done.3
  37.9 0.0 copy-done.9
  37.9 0.0 copy-done.11
  37.9 7.0 %shard_map.124 = (f32[128,256]{1,0:T(8,128)S(1)}, f32[128,128]{1,0:T(8,128)}) custom-call(f32[304,128]{1,0:T(8,128)S(1)} %get-tuple-element.17.mine_ref, f32[304,128]{1,0:T(8,128)S(1)} %collective-permute-done.5.other_ref.rim_dom, f32[64,128]{1,0:T(8,128)S(1)} %collective-permute-done.3.even_mine.rim_even, ...), custom_call_target="tpu_custom_call" | custom-call | tf_op jit(solution)/shard_map/pallas_call | solution.py:479
  44.9 0.0 copy-start.13
  44.9 0.0 collective-permute-start.11
  44.9 0.4 collective-permute-start.10
  45.3 3.8 %collective-permute-start.9 = (f32[128,256]{1,0:T(8,128)S(1)}, f32[128,256]{1,0:T(8,128)S(1)}, u32[]{:S(2)}, u32[]{:S(2)}) collective-permute-start(f32[128,256]{1,0:T(8,128)S(1)} %get-tuple-element.18.coarse_mine), channel_id=1, source_target_pairs={{0,2},{2,0},{4,6},{6,4},{8,10},{10,8},{12,14},{14,12},{16,18},{18,... | collective-permute-start | bytes 393224 | tf_op jit(solution)/shard_map/ppermute | solution.py:402
  49.1 2.0 %collective-permute-start.8 = (f32[128,256]{1,0:T(8,128)S(1)}, f32[128,256]{1,0:T(8,128)S(1)}, u32[]{:S(2)}, u32[]{:S(2)}) collective-permute-start(f32[128,256]{1,0:T(8,128)S(1)} %get-tuple-element.18.coarse_mine), channel_id=1, source_target_pairs={{0,30},{2,4},{4,2},{6,8},{8,6},{10,12},{12,10},{14,16},{16,14},{18... | collective-permute-start | bytes 393224 | tf_op jit(solution)/shard_map/ppermute | solution.py:402
  51.1 2.4 %collective-permute-done.11.coarse_odd_two = f32[128,256]{1,0:T(8,128)S(1)} collective-permute-done((f32[128,256]{1,0:T(8,128)S(1)}, f32[128,256]{1,0:T(8,128)S(1)}, u32[]{:S(2)}, u32[]{:S(2)}) %collective-permute-start.11) | collective-permute-done | bytes 131104 | tf_op jit(solution)/shard_map/ppermute | solution.py:402
  53.4 0.0 collective-permute-done.10.coarse_even_two
  53.4 1.4 %collective-permute-done.9.coarse_odd = f32[128,256]{1,0:T(8,128)S(1)} collective-permute-done((f32[128,256]{1,0:T(8,128)S(1)}, f32[128,256]{1,0:T(8,128)S(1)}, u32[]{:S(2)}, u32[]{:S(2)}) %collective-permute-start.9) | collective-permute-done | bytes 131104 | tf_op jit(solution)/shard_map/ppermute | solution.py:402
  54.9 3.0 %collective-permute-done.8.coarse_even = f32[128,256]{1,0:T(8,128)S(1)} collective-permute-done((f32[128,256]{1,0:T(8,128)S(1)}, f32[128,256]{1,0:T(8,128)S(1)}, u32[]{:S(2)}, u32[]{:S(2)}) %collective-permute-start.8) | collective-permute-done | bytes 131104 | tf_op jit(solution)/shard_map/ppermute | solution.py:402
  57.9 0.0 copy-done.13
  57.9 9.0 %shard_map.125 = f32[512,128]{1,0:T(8,128)} custom-call(f32[128,512]{1,0:T(8,128)S(1)} %get-tuple-element.14.fine_ref, f32[64,128]{1,0:T(8,128)S(1)} %collective-permute-done.3.even_mine.rim_even, f32[64,128]{1,0:T(8,128)S(1)} %collective-permute-done.4.odd_mine.rim_odd, f32[304,128]{1,0:T(8,128)S(1)} %collective-permute-done.5.other_ref.rim_dom, ...), custom_call_target="tpu_custom_call" | custom-call | tf_op jit(solution)/shard_map/pallas_call | solution.py:502
Async XLA Ops:
  0.6 1.0 %copy-start.4 = (f32[512,128]{1,0:T(8,128)S(1)}, f32[512,128]{1,0:T(8,128)}, u32[]{:S(2)}) copy-start(f32[512,128]{1,0:T(8,128)} %state_ref.3) | copy-start | bytes 786436
  1.6 0.7 %copy-start.8 = (s32[16,128]{1,0:T(8,128)S(1)}, s32[16,128]{1,0:T(8,128)}, u32[]{:S(2)}) copy-start(s32[16,128]{1,0:T(8,128)} %nbr_ref.6) | copy-start | bytes 24580
  2.3 0.7 %copy-start.10 = (s32[16,128]{1,0:T(8,128)S(1)}, s32[16,128]{1,0:T(8,128)}, u32[]{:S(2)}) copy-start(s32[16,128]{1,0:T(8,128)} %mask_ref.6) | copy-start | bytes 24580
  3.0 0.7 %copy-start.12 = (s32[512]{0:T(512)S(1)}, s32[512]{0:T(512)}, u32[]{:S(2)}) copy-start(s32[512]{0:T(512)} %parent_s.1) | copy-start | bytes 6148
  3.7 0.7 %copy-start.14 = (s32[512]{0:T(512)S(1)}, s32[512]{0:T(512)}, u32[]{:S(2)}) copy-start(s32[512]{0:T(512)} %share_s.1) | copy-start | bytes 6148
  4.3 0.7 %copy-start.15 = (s32[4,16]{1,0:T(4,128)S(1)}, s32[4,16]{1,0:T(4,128)}, u32[]{:S(2)}) copy-start(s32[4,16]{1,0:T(4,128)} %send_ref.3) | copy-start | bytes 772
  5.0 11.6 %copy-start.5 = (s32[16,512]{1,0:T(8,128)S(1)}, s32[16,512]{1,0:T(8,128)}, u32[]{:S(2)}) copy-start(s32[16,512]{1,0:T(8,128)} %nbr_ref.7) | copy-start | bytes 98308
  5.0 11.6 %copy-start.6 = (s32[16,512]{1,0:T(8,128)S(1)}, s32[16,512]{1,0:T(8,128)}, u32[]{:S(2)}) copy-start(s32[16,512]{1,0:T(8,128)} %mask_ref.7) | copy-start | bytes 98308
  5.8 10.8 %copy-start.7 = (f32[4,4,128]{2,1,0:T(4,128)S(1)}, f32[4,4,128]{2,1,0:T(4,128)}, u32[]{:S(2)}) copy-start(f32[4,4,128]{2,1,0:T(4,128)} %bias_ref.3) | copy-start | bytes 24580
  5.8 10.8 %collective-permute-start.2 = (f32[72,128]{1,0:T(8,128)S(1)}, f32[72,128]{1,0:T(8,128)S(1)}, u32[]{:S(2)}, u32[]{:S(2)}) collective-permute-start(f32[72,128]{1,0:T(8,128)S(1)} %get-tuple-element.13), channel_id=1, source_target_pairs={{0,1},{1,0},{2,3},{3,2},{4,5},{5,4},{6,7},{7,6},{8,9},{9,8},{10,11... | collective-permute-start | bytes 110600 | tf_op jit(solution)/shard_map/ppermute | solution.py:402
  6.3 8.2 %collective-permute-start = (f32[24,128]{1,0:T(8,128)S(1)}, f32[24,128]{1,0:T(8,128)S(1)}, u32[]{:S(2)}, u32[]{:S(2)}) collective-permute-start(f32[24,128]{1,0:T(8,128)S(1)} %get-tuple-element.11), channel_id=1, source_target_pairs={{0,30},{2,4},{4,2},{6,8},{8,6},{10,12},{12,10},{14,16},{16,14},{18... | collective-permute-start | bytes 36872 | tf_op jit(solution)/shard_map/ppermute | solution.py:402
  12.9 3.7 %collective-permute-start.1 = (f32[24,128]{1,0:T(8,128)S(1)}, f32[24,128]{1,0:T(8,128)S(1)}, u32[]{:S(2)}, u32[]{:S(2)}) collective-permute-start(f32[24,128]{1,0:T(8,128)S(1)} %get-tuple-element.12), channel_id=1, source_target_pairs={{0,2},{2,0},{4,6},{6,4},{8,10},{10,8},{12,14},{14,12},{16,18},{18,... | collective-permute-start | bytes 36872 | tf_op jit(solution)/shard_map/ppermute | solution.py:402
  16.6 1.1 %copy-start = (f32[4,3,128,128]{3,2,1,0:T(8,128)S(1)}, f32[4,3,128,128]{3,2,1,0:T(8,128)}, u32[]{:S(2)}) copy-start(f32[4,3,128,128]{3,2,1,0:T(8,128)} %edge_ref.3) | copy-start | bytes 2359300
  17.8 1.1 %copy-start.2 = (f32[4,3,128,128]{3,2,1,0:T(8,128)S(1)}, f32[4,3,128,128]{3,2,1,0:T(8,128)}, u32[]{:S(2)}) copy-start(f32[4,3,128,128]{3,2,1,0:T(8,128)} %node_ref.3) | copy-start | bytes 2359300
  18.9 19.0 %copy-start.1 = (f32[4,3,128,128]{3,2,1,0:T(8,128)S(1)}, f32[4,3,128,128]{3,2,1,0:T(8,128)}, u32[]{:S(2)}) copy-start(f32[4,3,128,128]{3,2,1,0:T(8,128)} %edge_ref.3) | copy-start | bytes 2359300
  18.9 19.0 %copy-start.3 = (f32[4,3,128,128]{3,2,1,0:T(8,128)S(1)}, f32[4,3,128,128]{3,2,1,0:T(8,128)}, u32[]{:S(2)}) copy-start(f32[4,3,128,128]{3,2,1,0:T(8,128)} %node_ref.3) | copy-start | bytes 2359300
  18.9 19.0 %copy-start.9 = (s32[16,128]{1,0:T(8,128)S(1)}, s32[16,128]{1,0:T(8,128)}, u32[]{:S(2)}) copy-start(s32[16,128]{1,0:T(8,128)} %nbr_ref.6) | copy-start | bytes 24580
  18.9 19.0 %copy-start.11 = (s32[16,128]{1,0:T(8,128)S(1)}, s32[16,128]{1,0:T(8,128)}, u32[]{:S(2)}) copy-start(s32[16,128]{1,0:T(8,128)} %mask_ref.6) | copy-start | bytes 24580
  28.9 8.9 %collective-permute-start.5 = (f32[304,128]{1,0:T(8,128)S(1)}, f32[304,128]{1,0:T(8,128)S(1)}, u32[]{:S(2)}, u32[]{:S(2)}) collective-permute-start(f32[304,128]{1,0:T(8,128)S(1)} %get-tuple-element.17.mine_ref), channel_id=1, source_target_pairs={{0,1},{1,0},{2,3},{3,2},{4,5},{5,4},{6,7},{7,6},{8,9},{9,8},{10,11... | collective-permute-start | bytes 466952 | tf_op jit(solution)/shard_map/ppermute | solution.py:402
  28.9 7.5 %collective-permute-start.3 = (f32[64,128]{1,0:T(8,128)S(1)}, f32[64,128]{1,0:T(8,128)S(1)}, u32[]{:S(2)}, u32[]{:S(2)}) collective-permute-start(f32[64,128]{1,0:T(8,128)S(1)} %get-tuple-element.15), channel_id=1, source_target_pairs={{0,30},{2,4},{4,2},{6,8},{8,6},{10,12},{12,10},{14,16},{16,14},{18... | collective-permute-start | bytes 98312 | tf_op jit(solution)/shard_map/ppermute | solution.py:402
  32.6 3.9 %collective-permute-start.4 = (f32[64,128]{1,0:T(8,128)S(1)}, f32[64,128]{1,0:T(8,128)S(1)}, u32[]{:S(2)}, u32[]{:S(2)}) collective-permute-start(f32[64,128]{1,0:T(8,128)S(1)} %get-tuple-element.16), channel_id=1, source_target_pairs={{0,2},{2,0},{4,6},{6,4},{8,10},{10,8},{12,14},{14,12},{16,18},{18,... | collective-permute-start | bytes 98312 | tf_op jit(solution)/shard_map/ppermute | solution.py:402
  36.5 1.2 %collective-permute-start.6 = (f32[64,128]{1,0:T(8,128)S(1)}, f32[64,128]{1,0:T(8,128)S(1)}, u32[]{:S(2)}, u32[]{:S(2)}) collective-permute-start(f32[64,128]{1,0:T(8,128)S(1)} %collective-permute-done.3.even_mine.rim_even), channel_id=1, source_target_pairs={{0,1},{1,0},{2,3},{3,2},{4,5},{5,4},{6,7},{7,6},{8,9},{9,8},{10,11... | collective-permute-start | bytes 98312 | tf_op jit(solution)/shard_map/ppermute | solution.py:402
  36.5 1.4 %collective-permute-start.7 = (f32[64,128]{1,0:T(8,128)S(1)}, f32[64,128]{1,0:T(8,128)S(1)}, u32[]{:S(2)}, u32[]{:S(2)}) collective-permute-start(f32[64,128]{1,0:T(8,128)S(1)} %collective-permute-done.4.odd_mine.rim_odd), channel_id=1, source_target_pairs={{0,1},{1,0},{2,3},{3,2},{4,5},{5,4},{6,7},{7,6},{8,9},{9,8},{10,11... | collective-permute-start | bytes 98312 | tf_op jit(solution)/shard_map/ppermute | solution.py:402
  44.9 13.0 %copy-start.13 = (s32[512]{0:T(512)S(1)}, s32[512]{0:T(512)}, u32[]{:S(2)}) copy-start(s32[512]{0:T(512)} %parent_s.1) | copy-start | bytes 6148
  44.9 8.6 %collective-permute-start.11 = (f32[128,256]{1,0:T(8,128)S(1)}, f32[128,256]{1,0:T(8,128)S(1)}, u32[]{:S(2)}, u32[]{:S(2)}) collective-permute-start(f32[128,256]{1,0:T(8,128)S(1)} %get-tuple-element.18.coarse_mine), channel_id=1, source_target_pairs={{0,4},{2,6},{4,0},{6,2},{8,12},{10,14},{12,8},{14,10},{16,20},{18,... | collective-permute-start | bytes 393224 | tf_op jit(solution)/shard_map/ppermute | solution.py:402
  44.9 8.6 %collective-permute-start.10 = (f32[128,256]{1,0:T(8,128)S(1)}, f32[128,256]{1,0:T(8,128)S(1)}, u32[]{:S(2)}, u32[]{:S(2)}) collective-permute-start(f32[128,256]{1,0:T(8,128)S(1)} %get-tuple-element.18.coarse_mine), channel_id=1, source_target_pairs={{0,28},{2,30},{4,8},{6,10},{8,4},{10,6},{12,16},{14,18},{16,12},{1... | collective-permute-start | bytes 393224 | tf_op jit(solution)/shard_map/ppermute | solution.py:402
  45.3 9.6 %collective-permute-start.9 = (f32[128,256]{1,0:T(8,128)S(1)}, f32[128,256]{1,0:T(8,128)S(1)}, u32[]{:S(2)}, u32[]{:S(2)}) collective-permute-start(f32[128,256]{1,0:T(8,128)S(1)} %get-tuple-element.18.coarse_mine), channel_id=1, source_target_pairs={{0,2},{2,0},{4,6},{6,4},{8,10},{10,8},{12,14},{14,12},{16,18},{18,... | collective-permute-start | bytes 393224 | tf_op jit(solution)/shard_map/ppermute | solution.py:402
  49.1 8.8 %collective-permute-start.8 = (f32[128,256]{1,0:T(8,128)S(1)}, f32[128,256]{1,0:T(8,128)S(1)}, u32[]{:S(2)}, u32[]{:S(2)}) collective-permute-start(f32[128,256]{1,0:T(8,128)S(1)} %get-tuple-element.18.coarse_mine), channel_id=1, source_target_pairs={{0,30},{2,4},{4,2},{6,8},{8,6},{10,12},{12,10},{14,16},{16,14},{18... | collective-permute-start | bytes 393224 | tf_op jit(solution)/shard_map/ppermute | solution.py:402
where the time goes:
time: 67.3 us; the launch traced here: 66.9 us
  Pallas kernels  26.8 us (40%)
  starting transfers between devices  17.4 us (26%)
  waiting for transfers between devices  15.3 us (23%)
  local copies, waits for them, and re-layouts  6.67 us (10%)
  between operations  0.72 us (1%)
    ppermute x12, starting transfers between devices, swap(): lax.ppermute(value, axis, [(source, partner(source) % count) for source i...  17.4 us
    ppermute x12, waiting for transfers between devices, swap(): lax.ppermute(value, axis, [(source, partner(source) % count) for source i...  15.3 us
    pallas_call x1, Pallas kernels, body(): kernel_call(functools.partial(fine_kernel, rim, group, side, regions), [s...  10 us
    pallas_call x1, Pallas kernels, body(): kernel_call(functools.partial(last_kernel, rim, group, side, regions), [w...  9.04 us
    pallas_call x1, Pallas kernels, body(): kernel_call(functools.partial(coarse_kernel, rim, group, side), [whole()]...  7 us
    unnamed x32, local copies, waits for them, and re-layouts  6.67 us
  transfers between devices with their start and end apart: 12, of which 8 were waited for; matrix products, arithmetic and copies ran while one was open for 0% of the time, Pallas kernels for 0%

commit v1 on v0

v1 whole, which is shorter than its diff:
```python
import functools

import jax
import jax.numpy as jnp
from jax import lax
from jax.experimental import pallas as pl
from jax.experimental.pallas import tpu as pltpu
from jax.sharding import PartitionSpec as P

epsilon = 1e-05
f32 = jnp.float32
bf16 = jnp.bfloat16
LANES = 128
VMEM_BYTES = 32 * 2**20


def split(values):
    high = values.astype(bf16)
    low = (values - high.astype(f32)).astype(bf16)
    return high, low


def halves(weight):
    return jnp.concatenate(split(weight.T), axis=0)


def folded(stacked):
    half = stacked.shape[0] // 2
    return stacked[:half] + stacked[half:]


def times(factor, columns):
    stacked = jnp.concatenate(split(columns), axis=0)
    wide = jnp.concatenate([factor, factor], axis=1)
    return folded(jnp.dot(wide, stacked, preferred_element_type=f32))


def centered(weight):
    return weight - jnp.mean(weight, axis=-1, keepdims=True)


def bias_block(row):
    return jnp.broadcast_to(row, (LANES, row.shape[-1])).T


def spread_out(block, width):
    return jnp.concatenate([block] * (width // LANES), axis=1)


def scaled(columns):
    spread = jnp.mean(columns * columns, axis=0, keepdims=True)
    return columns * lax.rsqrt(spread + epsilon)


def iota(shape, axis):
    return lax.broadcasted_iota(jnp.int32, shape, axis)


def hot(rows, index):
    return (iota((rows, index.shape[1]), 0) == index).astype(f32)


def block_gather(block, index):
    features = block.shape[0]
    pieces = []
    for start in range(0, index.shape[1], LANES):
        wide = jnp.broadcast_to(index[:, start : start + LANES], (features, LANES))
        found = jnp.take_along_axis(block, wide & (LANES - 1), axis=1)
        pieces.append(jnp.where((wide >= 0) & (wide < LANES), found, 0.0))
    return jnp.concatenate(pieces, axis=1)


def hot_gather(stacked, index):
    chosen = hot(stacked.shape[1], index).astype(bf16)
    return folded(jnp.dot(stacked, chosen, preferred_element_type=f32))


def stacked_halves(columns):
    return jnp.concatenate(split(columns), axis=0)


def prepare(edge, node, bias, factors, columns):
    for place, weight in enumerate(
        (edge[0], edge[1], centered(edge[2]), node[0], node[1], centered(node[2]))
    ):
        factors[place] = halves(weight)
    for place in range(4):
        row = bias[place : place + 1]
        columns[place] = bias_block(centered(row) if place % 2 else row)


def edge_sum(own_term, gather, validity, factor, column):
    count = own_term.shape[1]
    second_bias = spread_out(column, count)
    total = jnp.zeros(own_term.shape, f32)
    for slot in range(validity.shape[0]):
        hidden = jnp.maximum(own_term + gather(slot), 0.0)
        message = times(factor, hidden) + second_bias
        spread = jnp.mean(message * message, axis=0, keepdims=True)
        valid = validity[slot : slot + 1, :].astype(f32)
        total = total + message * (lax.rsqrt(spread + epsilon) * valid)
    return total


def node_step(own, node_term, gathered, factors, columns):
    count = own.shape[1]
    inner_act = jnp.maximum(node_term + times(factors[4], gathered), 0.0)
    update = times(factors[5], inner_act) + spread_out(columns[3], count)
    return own + scaled(update)


def own_product(factors, columns, place, own):
    bias = spread_out(columns[0 if place == 0 else 2], own.shape[1])
    return times(factors[place], own) + bias


def fetch(copies, semaphores):
    started = []
    for place, (source, target) in enumerate(copies):
        copy = pltpu.make_async_copy(source, target, semaphores.at[place])
        copy.start()
        started.append(copy)
    return started


def pick_kernel(
    rim,
    send_hbm,
    parent_hbm,
    share_hbm,
    state_hbm,
    nbr_hbm,
    mask_hbm,
    even_ref,
    odd_ref,
    dom_ref,
    send_ref,
    parent_s,
    share_s,
    state_ref,
    nbr_ref,
    mask_ref,
    semaphores,
):
    copies = fetch(
        (
            (send_hbm, send_ref),
            (parent_hbm, parent_s),
            (share_hbm, share_s),
            (state_hbm, state_ref),
            (nbr_hbm, nbr_ref),
            (mask_hbm, mask_ref),
        ),
        semaphores,
    )
    for copy in copies:
        copy.wait()
    even = lax.rem(lax.axis_index("region"), 2) == 0
    first = jnp.where(even, 1, 0)
    lane = iota((1, LANES), 1)

    def fill(out, out_base, direction, lane_base, parents, shares):
        for k in range(rim):
            row = send_ref[direction, k]
            out[pl.ds(out_base + k, 1), :] = state_ref[pl.ds(row, 1), :]
            here = lane == lane_base + k
            parents = jnp.where(here, parent_s[row].astype(f32), parents)
            shares = jnp.where(here, share_s[row].astype(f32), shares)
        return parents, shares

    zero = jnp.zeros((1, LANES), f32)
    for out, direction in ((even_ref, first), (odd_ref, 1 - first)):
        parents, shares = fill(out, 0, direction, direction * rim, zero, zero)
        out[rim : rim + 8, :] = jnp.zeros((8, LANES), f32)
        out[rim : rim + 1, :] = parents
        out[rim + 1 : rim + 2, :] = shares
    parents, shares = fill(dom_ref, 0, 2, 2 * rim, zero, zero)
    parents, shares = fill(dom_ref, rim, 3, 3 * rim, parents, shares)
    base = 2 * rim
    dom_ref[base : base + 8, :] = jnp.zeros((8, LANES), f32)
    dom_ref[base : base + 1, :] = parents
    dom_ref[base + 1 : base + 2, :] = shares
    slots = nbr_ref.shape[0]
    dom_ref[base + 8 : base + 8 + slots, :] = nbr_ref[...].astype(f32)
    dom_ref[base + 8 + slots : base + 8 + 2 * slots, :] = mask_ref[...].astype(f32)


def rim_rows(rim, even, recv_even, recv_odd, recv_dom):
    low = jnp.where(even, recv_even, recv_odd)
    high = jnp.where(even, recv_odd, recv_even)
    pad = jnp.zeros((LANES - 4 * rim, low.shape[1]), f32)
    return jnp.concatenate([low, high, recv_dom, pad], axis=0)


def before_kernel(
    rim,
    group,
    side,
    regions,
    token_ref,
    state_hbm,
    nbr_hbm,
    mask_hbm,
    parent_hbm,
    share_hbm,
    edge_hbm,
    node_hbm,
    bias_hbm,
    own_ref,
    term_ref,
    node_term_ref,
    partial_ref,
    nbr_ref,
    valid_ref,
    factors,
    columns,
    pick_ref,
    place_ref,
    facts_ref,
    state_ref,
    mask_ref,
    parent_ref,
    share_ref,
    edge_ref,
    node_ref,
    bias_ref,
    semaphores,
):
    copies = fetch(
        (
            (state_hbm, state_ref),
            (edge_hbm.at[0], edge_ref),
            (bias_hbm.at[0], bias_ref),
            (node_hbm.at[0], node_ref),
            (nbr_hbm, nbr_ref),
            (parent_hbm, parent_ref),
            (share_hbm, share_ref),
            (mask_hbm, mask_ref),
        ),
        semaphores,
    )
    for copy in copies:
        copy.wait()
    own = state_ref[...].T
    own_ref[...] = own
    valid_ref[...] = mask_ref[...].astype(f32)
    prepare(edge_ref, node_ref, bias_ref, factors, columns)
    term_ref[...] = own_product(factors, columns, 0, own)
    node_term_ref[...] = own_product(factors, columns, 3, own)
    stacked = stacked_halves(times(factors[1], own))
    for slot in range(nbr_ref.shape[0]):
        partial_ref[slot] = hot_gather(stacked, nbr_ref[slot : slot + 1, :])
    parent = parent_ref[...]
    count = parent.shape[1]
    region = lax.axis_index("region")
    place = side_places(parent, region, regions, group, rim, side)
    place_ref[...] = jnp.broadcast_to(place, place_ref.shape)
    picked = hot(LANES, place)
    share = share_ref[...].astype(f32)
    facts = jnp.concatenate([parent.astype(f32), share, jnp.zeros((6, count), f32)], axis=0)
    facts_ref[...] = lax.dot_general(
        facts,
        picked,
        (((1,), (1,)), ((), ())),
        precision=lax.Precision.HIGHEST,
        preferred_element_type=f32,
    )
    pick_ref[...] = (picked[4 * rim : 4 * rim + 2 * side] * share).astype(bf16)


def weighted(selection, rows):
    pair = jnp.concatenate(split(rows), axis=1)
    both = jnp.dot(selection.astype(bf16), pair, preferred_element_type=f32)
    return both[:, :LANES] + both[:, LANES:]


def fine_kernel(
    rim,
    side,
    send_hbm,
    own_ref,
    term_ref,
    node_term_ref,
    partial_ref,
    nbr_ref,
    valid_ref,
    factors,
    columns,
    pick_ref,
    facts_ref,
    recv_even,
    recv_odd,
    recv_dom,
    fine_ref,
    rows_ref,
    even_ref,
    odd_ref,
    send_ref,
    semaphores,
):
    copies = fetch(((send_hbm, send_ref),), semaphores)
    even = lax.rem(lax.axis_index("region"), 2) == 0
    outer = rim_rows(rim, even, recv_even[:rim], recv_odd[:rim], recv_dom[: 2 * rim]).T
    block = times(factors[1], outer)
    count = own_ref.shape[1]

    def gather(slot):
        return partial_ref[slot] + block_gather(block, nbr_ref[slot : slot + 1, :] - count)

    gathered = edge_sum(term_ref[...], gather, valid_ref, factors[2], columns[1])
    fine = node_step(own_ref[...], node_term_ref[...], gathered, factors, columns)
    fine_ref[...] = fine
    rows = fine.T
    rows_ref[...] = rows
    late = weighted(pick_ref[...], rows)
    first = jnp.where(even, 1, 0)
    for copy in copies:
        copy.wait()
    for out, is_low in ((even_ref, even), (odd_ref, jnp.logical_not(even))):
        out[0:side, :] = jnp.where(is_low, late[:side], late[side:])
        out[side : side + 8, :] = facts_ref[...]
    for out, direction in ((even_ref, first), (odd_ref, 1 - first)):
        for k in range(rim):
            row = send_ref[direction, k]
            out[side + 8 + k : side + 9 + k, :] = rows_ref[pl.ds(row, 1), :]
        out[side + 8 + rim :, :] = jnp.zeros((out.shape[0] - side - 8 - rim, LANES), f32)


def side_places(parent, region, regions, group, rim, side):
    count = parent.shape[1]
    earlier = (iota((count, count), 0) < iota((count, count), 1)).astype(bf16)
    place = jnp.full(parent.shape, -1, jnp.int32)
    for number, steps in enumerate((regions - 1, 1)):
        local = parent - lax.rem(region + steps, regions) * group
        inside = (local >= 0) & (local < group)
        member = jnp.broadcast_to(jnp.where(inside, 1.0, 0.0), (8, count)).astype(bf16)
        rank = jnp.dot(member, earlier, preferred_element_type=f32)[0:1].astype(jnp.int32)
        place = jnp.where(inside, rank + (4 * rim + number * side), place)
    return place


def prepare_kernel(
    rim,
    group,
    token_ref,
    rows_ref,
    nbr_ref,
    place_ref,
    side_facts,
    meta_even,
    meta_odd,
    meta_dom,
    edge_hbm,
    node_hbm,
    bias_hbm,
    parent_hbm,
    share_hbm,
    send_hbm,
    coarse_nbr_hbm,
    coarse_mask_hbm,
    factors,
    columns,
    late_ref,
    mine_ref,
    group_nbr,
    group_valid,
    edge_ref,
    node_ref,
    bias_ref,
    parent_ref,
    share_ref,
    send_ref,
    coarse_nbr,
    coarse_mask,
    semaphores,
):
    copies = fetch(
        (
            (parent_hbm, parent_ref),
            (share_hbm, share_ref),
            (send_hbm, send_ref),
            (coarse_nbr_hbm, coarse_nbr),
            (coarse_mask_hbm, coarse_mask),
            (edge_hbm, edge_ref),
            (node_hbm, node_ref),
            (bias_hbm, bias_ref),
        ),
        semaphores,
    )
    index = nbr_ref[...]
    slots, count = index.shape
    for start in range(0, count, LANES):
        now = index[:, start : start + LANES]
        late = jnp.where(now >= count, now - count, -1)
        for base in range(0, count, LANES):
            table = jnp.broadcast_to(place_ref[0:1, base : base + LANES], (slots, LANES))
            inner = now - base
            found = jnp.take_along_axis(table, inner & (LANES - 1), axis=1)
            late = jnp.where((inner >= 0) & (inner < LANES), found, late)
        late_ref[:, start : start + LANES] = late
    for copy in copies:
        copy.wait()
    region = lax.axis_index("region")
    share = share_ref[...].astype(f32)
    chosen = hot(group, parent_ref[...] - region * group) * share
    mine_ref[0:group, :] = weighted(chosen, rows_ref[...])
    totals = lax.dot_general(
        jnp.ones((8, count), f32), chosen, (((1,), (1,)), ((), ())), preferred_element_type=f32
    )
    base = group
    for start in range(0, group, LANES):
        mine_ref[base : base + 8, :] = totals[:, start : start + LANES]
        base += 8
    for k in range(2 * rim):
        row = send_ref[2 + k // rim, k % rim]
        mine_ref[base + k : base + k + 1, :] = rows_ref[pl.ds(row, 1), :]
    base += 2 * rim
    facts = (
        meta_even[rim : rim + 8, :]
        + meta_odd[rim : rim + 8, :]
        + meta_dom[2 * rim : 2 * rim + 8, :]
    )
    rims = iota(facts.shape, 1) < 4 * rim
    mine_ref[base : base + 8, :] = jnp.where(rims, facts, side_facts[...])
    base = 2 * rim + 8
    mine_first = lax.axis_index("dom") == 0

    def ordered(mine, other):
        return jnp.concatenate(
            [jnp.where(mine_first, mine, other), jnp.where(mine_first, other, mine)], axis=1
        )

    group_nbr[...] = ordered(
        coarse_nbr[...], meta_dom[base : base + slots, :].astype(jnp.int32)
    )
    group_valid[...] = ordered(
        coarse_mask[...].astype(f32), meta_dom[base + slots : base + 2 * slots, :]
    )
    for layer in range(factors.shape[0]):
        prepare(
            edge_ref.at[layer + 1],
            node_ref.at[layer + 1],
            bias_ref.at[layer + 1],
            factors.at[layer],
            columns.at[layer],
        )


def gather_side_kernel(rim, group, side, regions, mine_ref, even_mine, odd_mine, sum_ref):
    region = lax.axis_index("region")
    total = mine_ref[0:group, :]
    base = group + 8 * (group // LANES)
    weight = [mine_ref[group + 8 * b : group + 8 * b + 8, :] for b in range(group // LANES)]
    weight = jnp.concatenate(weight, axis=1)
    for block in (even_mine, odd_mine):
        depth = block.shape[0]
        facts = block[side : side + 8, :]
        index = facts[0:1].astype(jnp.int32) - region * group
        chosen = hot(group, jnp.where(iota((1, LANES), 1) < 4 * rim, -1, index))
        weight = weight + lax.dot_general(
            jnp.broadcast_to(facts[1:2], (8, LANES)),
            chosen,
            (((1,), (1,)), ((), ())),
            preferred_element_type=f32,
        )
        rows = block[0:side, :]
        spread = jnp.concatenate(
            [jnp.zeros((4 * rim, LANES), f32), rows, rows]
            + [jnp.zeros((LANES - 4 * rim - 2 * side, LANES), f32)] * (LANES > 4 * rim + 2 * side),
            axis=0,
        )
        both = jnp.dot(
            chosen.astype(bf16),
            jnp.concatenate(split(spread), axis=1),
            preferred_element_type=f32,
        )
        total = total + (both[:, :LANES] + both[:, LANES:])
    sum_ref[0:group, :] = total
    for b in range(group // LANES):
        sum_ref[group + 8 * b : group + 8 * b + 8, :] = weight[:, b * LANES : (b + 1) * LANES]
    sum_ref[base:, :] = mine_ref[base:, :]


def coarse_layer(own, nbr, valid, factors, columns):
    term = own_product(factors, columns, 0, own)
    stacked = stacked_halves(times(factors[1], own))

    def gather(slot):
        return hot_gather(stacked, nbr[slot : slot + 1, :])

    gathered = edge_sum(term, gather, valid, factors[2], columns[1])
    return node_step(own, own_product(factors, columns, 3, own), gathered, factors, columns)


def coarse_kernel(
    group,
    mine_ref,
    other_ref,
    nbr_ref,
    valid_ref,
    factors,
    columns,
    group_ref,
    out_ref,
    rows_ref,
):
    dom = lax.axis_index("dom")
    total = mine_ref[0:group, :] + other_ref[0:group, :]
    weight = [
        mine_ref[group + 8 * b : group + 8 * b + 1, :]
        + other_ref[group + 8 * b : group + 8 * b + 1, :]
        for b in range(group // LANES)
    ]
    own = total.T / jnp.maximum(jnp.concatenate(weight, axis=1), 1.0)
    own = coarse_layer(own, nbr_ref, valid_ref, factors.at[0], columns.at[0])
    own = coarse_layer(own, nbr_ref, valid_ref, factors.at[1], columns.at[1])
    group_ref[...] = own
    rows_ref[...] = own.T
    rows = out_ref.shape[0]
    out_ref[...] = rows_ref[pl.ds(pl.multiple_of(dom * rows, rows), rows), :]


def between_kernel(
    rim,
    group,
    side,
    fine_ref,
    even_mine,
    odd_mine,
    mine_ref,
    other_ref,
    coarse_mine,
    nbr_ref,
    parent_hbm,
    share_hbm,
    factors,
    columns,
    own_ref,
    late_ref,
    partial_ref,
    parent_ref,
    share_ref,
    semaphores,
):
    copies = fetch(((parent_hbm, parent_ref), (share_hbm, share_ref)), semaphores)
    region = lax.axis_index("region")
    even = lax.rem(region, 2) == 0
    base = side + 8
    dom_base = group + 8 * (group // LANES)
    outer = rim_rows(
        rim,
        even,
        even_mine[base : base + rim, :],
        odd_mine[base : base + rim, :],
        other_ref[dom_base : dom_base + 2 * rim, :],
    ).T
    facts = mine_ref[dom_base + 2 * rim : dom_base + 2 * rim + 8, :]
    stacked = stacked_halves(coarse_mine[...])
    local = facts[0:1].astype(jnp.int32) - region * group
    late_ref[...] = outer + (facts[1:2] * 0.25) * hot_gather(stacked, local)
    for copy in copies:
        copy.wait()
    share = share_ref[...].astype(f32) * 0.25
    own = fine_ref[...] + share * hot_gather(stacked, parent_ref[...] - region * group)
    own_ref[...] = own
    stacked = stacked_halves(times(factors[2, 1], own))
    for slot in range(nbr_ref.shape[0]):
        partial_ref[slot] = hot_gather(stacked, nbr_ref[slot : slot + 1, :])


def side_kernel(
    rim, group, regions, late_in, mine_ref, other_ref, first_ref, second_ref, late_ref, back_ref
):
    region = lax.axis_index("region")
    near = lax.axis_index("dom") == 0
    base = group + 8 * (group // LANES) + 2 * rim
    facts = jnp.concatenate([mine_ref[base : base + 8, :], other_ref[base : base + 8, :]], axis=1)
    index = facts[0:1].astype(jnp.int32)

    def home(here, distance):
        below = (lax.rem(region // distance, 2) == 0) == here
        return lax.rem(region + jnp.where(below, regions - distance, distance), regions)

    late = None
    for block, here in ((first_ref, True), (second_ref, False)):
        place = jnp.where(near, home(here, 1), home(here, 2))
        found = hot_gather(stacked_halves(block[...]), index - place * group)
        late = found if late is None else late + found
    late = late * (facts[1:2] * 0.25)
    late_ref[...] = late_in[...] + late[:, :LANES]
    back_ref[...] = late[:, LANES:]


def last_kernel(
    own_ref,
    late_in,
    back_ref,
    partial_ref,
    late_index,
    place_ref,
    valid_ref,
    factors,
    columns,
    out_ref,
):
    late = late_in[...] + back_ref[...]
    own = own_ref[...] + block_gather(late, place_ref[0:1, :])
    factors = factors.at[2]
    columns = columns.at[2]
    block = times(factors[1], late)

    def gather(slot):
        return partial_ref[slot] + block_gather(block, late_index[slot : slot + 1, :])

    term = own_product(factors, columns, 0, own)
    gathered = edge_sum(term, gather, valid_ref, factors[2], columns[1])
    node_term = own_product(factors, columns, 3, own)
    out_ref[...] = node_step(own, node_term, gathered, factors, columns).T


def whole():
    return pl.BlockSpec(memory_space=pltpu.VMEM)


def far():
    return pl.BlockSpec(memory_space=pltpu.HBM)


def kept(value):
    return pltpu.with_memory_space_constraint(value, pltpu.HBM)


def scalars():
    return pl.BlockSpec(memory_space=pltpu.SMEM)


def kernel_call(body, in_specs, outs, scratch=(), copies=1, flops=0):
    outs = [(out, f32) if isinstance(out[0], int) else out for out in outs]
    return pl.pallas_call(
        body,
        in_specs=in_specs,
        out_specs=tuple(whole() for _ in outs),
        out_shape=tuple(jax.ShapeDtypeStruct(shape, kind) for shape, kind in outs),
        scratch_shapes=list(scratch) + [pltpu.SemaphoreType.DMA((copies,))] * (copies > 0),
        compiler_params=pltpu.CompilerParams(vmem_limit_bytes=VMEM_BYTES),
        cost_estimate=pl.CostEstimate(
            flops=flops, bytes_accessed=4 * 2**20, transcendentals=0
        ),
    )


def swap(value, axis, partner, count):
    return lax.ppermute(value, axis, [(source, partner(source) % count) for source in range(count)])


def body(
    fine_state,
    fine_nbr,
    fine_mask,
    send_rows,
    coarse_nbr,
    coarse_mask,
    parent,
    interp_share,
    edge_w,
    node_w,
    biases,
):
    count, width = fine_state.shape
    own_coarse = coarse_nbr.shape[1]
    slots = coarse_nbr.shape[0]
    regions = lax.axis_size("region")
    domains = lax.axis_size("dom")
    group = domains * own_coarse
    rim = send_rows.shape[1]
    side = count // (8 * domains)
    fine_state, fine_nbr, fine_mask, send_rows, coarse_nbr, coarse_mask = (
        kept(value)
        for value in (fine_state, fine_nbr, fine_mask, send_rows, coarse_nbr, coarse_mask)
    )
    parent_row = kept(parent[None, :])
    share_row = kept(interp_share[None, :])
    parent, interp_share = kept(parent), kept(interp_share)
    weights = (kept(edge_w), kept(node_w), kept(biases))
    i32 = jnp.int32

    def even_partner(r):
        return r - 1 if r % 2 == 0 else r + 1

    def odd_partner(r):
        return r + 1 if r % 2 == 0 else r - 1

    def even_two_partner(r):
        return r - 2 if r // 2 % 2 == 0 else r + 2

    def odd_two_partner(r):
        return r + 2 if r // 2 % 2 == 0 else r - 2

    def even_swap(value):
        return swap(value, "region", even_partner, regions)

    def odd_swap(value):
        return swap(value, "region", odd_partner, regions)

    def dom_swap(value):
        return swap(value, "dom", lambda d: d + 1, domains)

    def both_swap(value, near, distant):
        pairs = []
        for r in range(regions):
            for d in range(domains):
                target = (near(r) if d == 0 else distant(r)) % regions
                pairs.append((r * domains + d, target * domains + d))
        return lax.ppermute(value, ("region", "dom"), pairs)

    even_out, odd_out, dom_out = kernel_call(
        functools.partial(pick_kernel, rim),
        [far()] * 6,
        [(rim + 8, width), (rim + 8, width), (2 * rim + 8 + 2 * slots, width)],
        [
            pltpu.SMEM(send_rows.shape, i32),
            pltpu.SMEM(parent.shape, i32),
            pltpu.SMEM(interp_share.shape, i32),
            pltpu.VMEM(fine_state.shape, f32),
            pltpu.VMEM(coarse_nbr.shape, i32),
            pltpu.VMEM(coarse_mask.shape, i32),
        ],
        copies=6,
    )(send_rows, parent, interp_share, fine_state, coarse_nbr, coarse_mask)
    meta_even = even_swap(even_out)
    meta_odd = odd_swap(odd_out)
    meta_dom = dom_swap(dom_out)

    columns_shape = (width, count)
    weight_scratch = [
        pltpu.VMEM(edge_w.shape[1:], f32),
        pltpu.VMEM(node_w.shape[1:], f32),
        pltpu.VMEM(biases.shape[1:], f32),
    ]
    row_scratch = [pltpu.VMEM((1, count), i32), pltpu.VMEM((1, count), i32)]
    (
        own,
        term,
        node_term,
        partial,
        nbr,
        valid,
        factors,
        columns,
        pick,
        place,
        side_facts,
    ) = kernel_call(
        functools.partial(before_kernel, rim, group, side, regions),
        [whole()] + [far()] * 8,
        [
            columns_shape,
            columns_shape,
            columns_shape,
            (slots, width, count),
            (fine_nbr.shape, i32),
            fine_mask.shape,
            ((6, 2 * width, width), bf16),
            (4, width, LANES),
            ((2 * side, count), bf16),
            ((8, count), i32),
            (8, LANES),
        ],
        [pltpu.VMEM(fine_state.shape, f32), pltpu.VMEM(fine_mask.shape, i32)]
        + row_scratch
        + weight_scratch,
        copies=8,
        flops=4 * 10**9,
    )(even_out, fine_state, fine_nbr, fine_mask, parent_row, share_row, *weights)

    block_rows = side + 8 + rim + 8
    dom_rows = group + 8 * (group // LANES) + 2 * rim + 8
    fine_one, rows, even_out, odd_out = kernel_call(
        functools.partial(fine_kernel, rim, side),
        [far()] + [whole()] * 13,
        [columns_shape, (count, width), (block_rows, width), (block_rows, width)],
        [pltpu.SMEM(send_rows.shape, i32)],
    )(
        send_rows,
        own,
        term,
        node_term,
        partial,
        nbr,
        valid,
        factors,
        columns,
        pick,
        side_facts,
        meta_even,
        meta_odd,
        meta_dom,
    )
    even_mine = even_swap(even_out)
    odd_mine = odd_swap(odd_out)

    later = edge_w.shape[0] - 1
    factors, columns, late_index, mine, group_nbr, group_valid = kernel_call(
        functools.partial(prepare_kernel, rim, group),
        [whole()] * 8 + [far()] * 8,
        [
            ((later, 6, 2 * width, width), bf16),
            (later, 4, width, LANES),
            (fine_nbr.shape, i32),
            (dom_rows, width),
            ((slots, group), i32),
            (slots, group),
        ],
        [
            pltpu.VMEM(edge_w.shape, f32),
            pltpu.VMEM(node_w.shape, f32),
            pltpu.VMEM(biases.shape, f32),
        ]
        + row_scratch
        + [
            pltpu.SMEM(send_rows.shape, i32),
            pltpu.VMEM(coarse_nbr.shape, i32),
            pltpu.VMEM(coarse_mask.shape, i32),
        ],
        copies=8,
        flops=2 * 10**9,
    )(
        even_out,
        rows,
        nbr,
        place,
        side_facts,
        meta_even,
        meta_odd,
        meta_dom,
        *weights,
        parent_row,
        share_row,
        send_rows,
        coarse_nbr,
        coarse_mask,
    )
    (mine,) = kernel_call(
        functools.partial(gather_side_kernel, rim, group, side, regions),
        [whole()] * 3,
        [(dom_rows, width)],
        copies=0,
    )(mine, even_mine, odd_mine)
    other = dom_swap(mine)

    coarse_group, coarse_out = kernel_call(
        functools.partial(coarse_kernel, group),
        [whole()] * 6,
        [(width, group), (own_coarse, width)],
        [pltpu.VMEM((group, width), f32)],
        copies=0,
    )(mine, other, group_nbr, group_valid, factors, columns)
    first = both_swap(coarse_group, even_partner, even_two_partner)
    second = both_swap(coarse_group, odd_partner, odd_two_partner)

    own, late, partial = kernel_call(
        functools.partial(between_kernel, rim, group, side),
        [whole()] * 7 + [far()] * 2 + [whole()] * 2,
        [columns_shape, (width, LANES), (slots, width, count)],
        row_scratch,
        copies=2,
        flops=4 * 10**9,
    )(
        fine_one,
        even_mine,
        odd_mine,
        mine,
        other,
        coarse_group,
        nbr,
        parent_row,
        share_row,
        factors,
        columns,
    )
    late, back = kernel_call(
        functools.partial(side_kernel, rim, group, regions),
        [whole()] * 5,
        [(width, LANES), (width, LANES)],
        copies=0,
    )(late, mine, other, first, second)
    back = dom_swap(back)
    (fine_out,) = kernel_call(
        last_kernel, [whole()] * 9, [(count, width)], copies=0
    )(own, late, back, partial, late_index, place, valid, factors, columns)
    return (fine_out, coarse_out)


def solution(mesh):
    return jax.shard_map(
        body,
        mesh=mesh,
        in_specs=(
            P(("region", "dom"), None),
            P(None, ("region", "dom")),
            P(None, ("region", "dom")),
            P(None, ("region", "dom")),
            P(None, ("region", "dom")),
            P(None, ("region", "dom")),
            P(("region", "dom")),
            P(("region", "dom")),
            P(),
            P(),
            P(),
        ),
        out_specs=(P(("region", "dom"), None), P(("region", "dom"), None)),
        check_vma=False,
    )
```

time: 67.3 us -> 47.1 us (0.70)
  waiting for transfers between devices: 15.3 us -> 7.84 us
  local copies, waits for them, and re-layouts: 6.67 us -> 0 us
  starting transfers between devices: 17.4 us -> 12 us
    ppermute x12 -> x7, waiting for transfers between devices: 15.3 us -> 5.45 us  [swap(): lax.ppermute(value, axis, [(source, partner(source) % count) for source i...]
    ppermute x12 -> x7, starting transfers between devices: 17.4 us -> 9.62 us  [swap(): lax.ppermute(value, axis, [(source, partner(source) % count) for source i...]
    unnamed x32 -> x0, local copies, waits for them, and re-layouts: 6.67 us -> none
    ppermute x0 -> x2, waiting for transfers between devices: none -> 2.39 us  [both_swap(): return lax.ppermute(value, ('region', 'dom'), pairs)]
    ppermute x0 -> x2, starting transfers between devices: none -> 2.39 us  [both_swap(): return lax.ppermute(value, ('region', 'dom'), pairs)]
    pallas_call x4 -> x9, Pallas kernels: 26.8 us -> 26.3 us  [the longest x1 5.38 us: body(): kernel_call(functools.partial(coarse_kernel, group), [whole()] * 6, [(wid...]
  transfers between devices with their start and end apart: 12 -> 9, of which waited for: 8 -> 4; matrix products, arithmetic and copies ran while one was open for 0% -> 0% of each run, Pallas kernels for 0% -> 23%
where the time goes in v1:
time: 47.1 us; the launch traced here: 46.9 us
  Pallas kernels  26.3 us (56%)
  starting transfers between devices  12 us (25%)
  waiting for transfers between devices  7.84 us (17%)
  between operations  0.73 us (2%)
    ppermute x7, starting transfers between devices, swap(): lax.ppermute(value, axis, [(source, partner(source) % count) for source i...  9.62 us
    ppermute x7, waiting for transfers between devices, swap(): lax.ppermute(value, axis, [(source, partner(source) % count) for source i...  5.45 us
    pallas_call x1, Pallas kernels, body(): kernel_call(functools.partial(coarse_kernel, group), [whole()] * 6, [(wid...  5.38 us
    pallas_call x1, Pallas kernels, body(): kernel_call(functools.partial(before_kernel, rim, group, side, regions),...  4.83 us
    pallas_call x1, Pallas kernels, body(): kernel_call(last_kernel, [whole()] * 9, [(count, width)], copies=0)  4.45 us
    pallas_call x1, Pallas kernels, body(): kernel_call(functools.partial(fine_kernel, rim, side), [far()] + [whole()...  3.93 us
    pallas_call x1, Pallas kernels, body(): kernel_call(functools.partial(between_kernel, rim, group, side), [whole()...  3.78 us
    ppermute x2, waiting for transfers between devices, both_swap(): return lax.ppermute(value, ('region', 'dom'), pairs)  2.39 us
  transfers between devices with their start and end apart: 9, of which 4 were waited for; matrix products, arithmetic and copies ran while one was open for 0% of the time, Pallas kernels for 23%

profile of v1, /device:TPU:0, one launch (start us, length us, event | category | flops | bytes accessed | tf_op | source)
XLA Modules:
  0.0 46.9 jit_solution(16509745251122621215)
XLA Ops:
  0.6 1.1 %shard_map.122 = (f32[24,128]{1,0:T(8,128)S(1)}, f32[24,128]{1,0:T(8,128)S(1)}, f32[72,128]{1,0:T(8,128)S(1)}) custom-call(s32[4,16]{1,0:T(4,128)} %send_hbm.5, s32[512]{0:T(512)} %parent_hbm.1, s32[512]{0:T(512)} %share_hbm.1, f32[512,128]{1,0:T(8,128)} %state_hbm.3, s32[16,128]{1,0:T(8,128)} %coarse_nbr_hbm.1, s32[16,128]{1,0:T(8,128)} %coarse_mask_hbm.1), custom_call_target="tpu_custom_call" | custom-call | bytes 4194304 | tf_op jit(solution)/shard_map/pallas_call | solution.py:716
  1.8 7.0 %collective-permute-start = (f32[24,128]{1,0:T(8,128)S(1)}, f32[24,128]{1,0:T(8,128)S(1)}, u32[]{:S(2)}, u32[]{:S(2)}) collective-permute-start(f32[24,128]{1,0:T(8,128)S(1)} %get-tuple-element.33.token_ref), channel_id=1, source_target_pairs={{0,30},{2,4},{4,2},{6,8},{8,6},{10,12},{12,10},{14,16},{16,14},{18... | collective-permute-start | bytes 36872 | tf_op jit(solution)/shard_map/ppermute | solution.py:653
  8.8 0.0 collective-permute-start.2
  8.8 0.0 collective-permute-start.1
  8.8 4.8 %shard_map.123 = (f32[128,512]{1,0:T(8,128)S(1)}, f32[128,512]{1,0:T(8,128)S(1)}, f32[128,512]{1,0:T(8,128)S(1)}, f32[16,128,512]{2,1,0:T(8,128)S(1)}, s32[16,51...) custom-call(f32[24,128]{1,0:T(8,128)S(1)} %get-tuple-element.33.toke, ...), custom_call_target="tpu_custom_call" | custom-call | flops 4000000000 | bytes 4194304 | tf_op jit(solution)/shard_map/pallas_call | solution.py:753
  13.6 0.0 collective-permute-done.recv_even.meta_even
  13.6 0.0 collective-permute-done.1.recv_odd.meta_odd
  13.6 0.0 collective-permute-done.2.recv_dom.meta_dom
  13.6 3.9 %shard_map.124 = (f32[128,512]{1,0:T(8,128)S(1)}, f32[512,128]{1,0:T(8,128)S(1)}, f32[64,128]{1,0:T(8,128)S(1)}, f32[64,128]{1,0:T(8,128)S(1)}) custom-call(s32[4,16]{1,0:T(4,128)} %send_hbm.5, f32[128,512]{1,0:T(8,128)S(1)} %get-tuple-element.34.own_ref, f32[128,512]{1,0:T(8,128)S(1)} %get-tuple-element.35.term_ref, ...), custom_call_target="tpu_custom_call" | custom-call | bytes 4194304 | tf_op jit(solution)/shard_map/pallas_call | solution.py:778
  17.6 2.5 %collective-permute-start.3 = (f32[64,128]{1,0:T(8,128)S(1)}, f32[64,128]{1,0:T(8,128)S(1)}, u32[]{:S(2)}, u32[]{:S(2)}) collective-permute-start(f32[64,128]{1,0:T(8,128)S(1)} %get-tuple-element.47.token_ref), channel_id=1, source_target_pairs={{0,30},{2,4},{4,2},{6,8},{8,6},{10,12},{12,10},{14,16},{16,14},{18... | collective-permute-start | bytes 98312 | tf_op jit(solution)/shard_map/ppermute | solution.py:653
  20.1 0.0 collective-permute-start.4
  20.1 2.3 %shard_map.125 = (bf16[3,6,256,128]{3,2,1,0:T(8,128)(2,1)S(1)}, f32[3,4,128,128]{3,2,1,0:T(8,128)S(1)}, s32[16,512]{1,0:T(8,128)S(1)}, f32[312,128]{1,0:T(8,128)...) custom-call(f32[64,128]{1,0:T(8,128)S(1)} %get-tuple-element.47.token_ref, ...), custom_call_target="tpu_custom_call" | custom-call | flops 2000000000 | bytes 4194304 | tf_op jit(solution)/shard_map/pallas_call | solution.py:803
  22.4 2.8 %collective-permute-done.3.even_mine = f32[64,128]{1,0:T(8,128)S(1)} collective-permute-done((f32[64,128]{1,0:T(8,128)S(1)}, f32[64,128]{1,0:T(8,128)S(1)}, u32[]{:S(2)}, u32[]{:S(2)}) %collective-permute-start.3) | collective-permute-done | bytes 32800 | tf_op jit(solution)/shard_map/ppermute | solution.py:653
  25.2 0.0 collective-permute-done.4.odd_mine
  25.2 0.3 shard_map.126.mine_ref
  25.5 0.1 collective-permute-start.5
  25.5 1.4 %collective-permute-done.5.other_ref = f32[312,128]{1,0:T(8,128)S(1)} collective-permute-done((f32[312,128]{1,0:T(8,128)S(1)}, f32[312,128]{1,0:T(8,128)S(1)}, u32[]{:S(2)}, u32[]{:S(2)}) %collective-permute-start.5) | collective-permute-done | bytes 159776 | tf_op jit(solution)/shard_map/ppermute | solution.py:653
  26.9 5.4 %shard_map.127 = (f32[128,256]{1,0:T(8,128)S(1)}, f32[128,128]{1,0:T(8,128)}) custom-call(f32[312,128]{1,0:T(8,128)S(1)} %shard_map.126.mine_ref, f32[312,128]{1,0:T(8,128)S(1)} %collective-permute-done.5.other_ref, s32[16,256]{1,0:T(8,128)S(1)} %get-tuple-element.52.nbr_ref, f32[16,256]{1,0:T(8,128)S(1)} %get-tuple-element.53.valid_ref, ...), custom_call_target="tpu_custom_call" | custom-call | bytes 4194304 | tf_op jit(solution)/shard_map/pallas_call | solution.py:851
  32.3 2.4 %collective-permute-start.6 = (f32[128,256]{1,0:T(8,128)S(1)}, f32[128,256]{1,0:T(8,128)S(1)}, u32[]{:S(2)}, u32[]{:S(2)}) collective-permute-start(f32[128,256]{1,0:T(8,128)S(1)} %get-tuple-element.56.coarse_mine), channel_id=1, source_target_pairs={{0,30},{1,29},{2,4},{3,31},{4,2},{5,9},{6,8},{7,11},{8,6},{9,5},{1... | collective-permute-start | bytes 393224 | tf_op jit(solution)/shard_map/ppermute | solution.py:714
  34.7 0.0 collective-permute-start.7
  34.7 3.8 %shard_map.128 = (f32[128,512]{1,0:T(8,128)S(1)}, f32[128,128]{1,0:T(8,128)S(1)}, f32[16,128,512]{2,1,0:T(8,128)S(1)}) custom-call(f32[128,512]{1,0:T(8,128)S(1)} %get-tuple-element.46.fine_ref, f32[64,128]{1,0:T(8,128)S(1)} %collective-permute-done.3.even_mine, f32[64,128]{1,0:T(8,128)S(1)} %collective-permute-done.4.odd_mine, ...), custom_call_target="tpu_custom_call" | custom-call | flops 4000000000 | bytes 4194304 | tf_op jit(solution)/shard_map/pallas_call | solution.py:861
  38.5 2.4 %collective-permute-done.6.first_ref = f32[128,256]{1,0:T(8,128)S(1)} collective-permute-done((f32[128,256]{1,0:T(8,128)S(1)}, f32[128,256]{1,0:T(8,128)S(1)}, u32[]{:S(2)}, u32[]{:S(2)}) %collective-permute-start.6) | collective-permute-done | bytes 131104 | tf_op jit(solution)/shard_map/ppermute | solution.py:714
  40.8 0.0 collective-permute-done.7.second_ref
  40.9 0.3 shard_map.129
  41.1 0.1 collective-permute-start.8
  41.2 1.2 %collective-permute-done.8.back_ref = f32[128,128]{1,0:T(8,128)S(1)} collective-permute-done((f32[128,128]{1,0:T(8,128)S(1)}, f32[128,128]{1,0:T(8,128)S(1)}, u32[]{:S(2)}, u32[]{:S(2)}) %collective-permute-start.8) | collective-permute-done | bytes 65568 | tf_op jit(solution)/shard_map/ppermute | solution.py:653
  42.4 4.5 %shard_map.130 = f32[512,128]{1,0:T(8,128)} custom-call(f32[128,512]{1,0:T(8,128)S(1)} %get-tuple-element.57.own_ref, f32[128,128]{1,0:T(8,128)S(1)} %get-tuple-element.59.late_in, f32[128,128]{1,0:T(8,128)S(1)} %collective-permute-done.8.back_ref, f32[16,128,512]{2,1,0:T(8,128)S(1)} %get-tuple-element.61.partial_ref, ...), custom_call_target="tpu_custom_call" | custom-call | bytes 4194304 | tf_op jit(solution)/shard_map/pallas_call | solution.py:888
Async XLA Ops:
  1.8 11.8 %collective-permute-start = (f32[24,128]{1,0:T(8,128)S(1)}, f32[24,128]{1,0:T(8,128)S(1)}, u32[]{:S(2)}, u32[]{:S(2)}) collective-permute-start(f32[24,128]{1,0:T(8,128)S(1)} %get-tuple-element.33.token_ref), channel_id=1, source_target_pairs={{0,30},{2,4},{4,2},{6,8},{8,6},{10,12},{12,10},{14,16},{16,14},{18... | collective-permute-start | bytes 36872 | tf_op jit(solution)/shard_map/ppermute | solution.py:653
  8.8 4.9 %collective-permute-start.2 = (f32[72,128]{1,0:T(8,128)S(1)}, f32[72,128]{1,0:T(8,128)S(1)}, u32[]{:S(2)}, u32[]{:S(2)}) collective-permute-start(f32[72,128]{1,0:T(8,128)S(1)} %get-tuple-element.45), channel_id=1, source_target_pairs={{0,1},{1,0},{2,3},{3,2},{4,5},{5,4},{6,7},{7,6},{8,9},{9,8},{10,11... | collective-permute-start | bytes 110600 | tf_op jit(solution)/shard_map/ppermute | solution.py:653
  8.8 4.9 %collective-permute-start.1 = (f32[24,128]{1,0:T(8,128)S(1)}, f32[24,128]{1,0:T(8,128)S(1)}, u32[]{:S(2)}, u32[]{:S(2)}) collective-permute-start(f32[24,128]{1,0:T(8,128)S(1)} %get-tuple-element.44), channel_id=1, source_target_pairs={{0,2},{2,0},{4,6},{6,4},{8,10},{10,8},{12,14},{14,12},{16,18},{18,... | collective-permute-start | bytes 36872 | tf_op jit(solution)/shard_map/ppermute | solution.py:653
  17.6 7.6 %collective-permute-start.3 = (f32[64,128]{1,0:T(8,128)S(1)}, f32[64,128]{1,0:T(8,128)S(1)}, u32[]{:S(2)}, u32[]{:S(2)}) collective-permute-start(f32[64,128]{1,0:T(8,128)S(1)} %get-tuple-element.47.token_ref), channel_id=1, source_target_pairs={{0,30},{2,4},{4,2},{6,8},{8,6},{10,12},{12,10},{14,16},{16,14},{18... | collective-permute-start | bytes 98312 | tf_op jit(solution)/shard_map/ppermute | solution.py:653
  20.1 5.1 %collective-permute-start.4 = (f32[64,128]{1,0:T(8,128)S(1)}, f32[64,128]{1,0:T(8,128)S(1)}, u32[]{:S(2)}, u32[]{:S(2)}) collective-permute-start(f32[64,128]{1,0:T(8,128)S(1)} %get-tuple-element.48), channel_id=1, source_target_pairs={{0,2},{2,0},{4,6},{6,4},{8,10},{10,8},{12,14},{14,12},{16,18},{18,... | collective-permute-start | bytes 98312 | tf_op jit(solution)/shard_map/ppermute | solution.py:653
  25.5 1.5 %collective-permute-start.5 = (f32[312,128]{1,0:T(8,128)S(1)}, f32[312,128]{1,0:T(8,128)S(1)}, u32[]{:S(2)}, u32[]{:S(2)}) collective-permute-start(f32[312,128]{1,0:T(8,128)S(1)} %shard_map.126.mine_ref), channel_id=1, source_target_pairs={{0,1},{1,0},{2,3},{3,2},{4,5},{5,4},{6,7},{7,6},{8,9},{9,8},{10,11... | collective-permute-start | bytes 479240 | tf_op jit(solution)/shard_map/ppermute | solution.py:653
  32.3 8.6 %collective-permute-start.6 = (f32[128,256]{1,0:T(8,128)S(1)}, f32[128,256]{1,0:T(8,128)S(1)}, u32[]{:S(2)}, u32[]{:S(2)}) collective-permute-start(f32[128,256]{1,0:T(8,128)S(1)} %get-tuple-element.56.coarse_mine), channel_id=1, source_target_pairs={{0,30},{1,29},{2,4},{3,31},{4,2},{5,9},{6,8},{7,11},{8,6},{9,5},{1... | collective-permute-start | bytes 393224 | tf_op jit(solution)/shard_map/ppermute | solution.py:714
  34.7 6.2 %collective-permute-start.7 = (f32[128,256]{1,0:T(8,128)S(1)}, f32[128,256]{1,0:T(8,128)S(1)}, u32[]{:S(2)}, u32[]{:S(2)}) collective-permute-start(f32[128,256]{1,0:T(8,128)S(1)} %get-tuple-element.56.coarse_mine), channel_id=1, source_target_pairs={{0,2},{1,5},{2,0},{3,7},{4,6},{5,1},{6,4},{7,3},{8,10},{9,13},{10,... | collective-permute-start | bytes 393224 | tf_op jit(solution)/shard_map/ppermute | solution.py:714
  41.1 1.3 %collective-permute-start.8 = (f32[128,128]{1,0:T(8,128)S(1)}, f32[128,128]{1,0:T(8,128)S(1)}, u32[]{:S(2)}, u32[]{:S(2)}) collective-permute-start(f32[128,128]{1,0:T(8,128)S(1)} %get-tuple-element.60), channel_id=1, source_target_pairs={{0,1},{1,0},{2,3},{3,2},{4,5},{5,4},{6,7},{7,6},{8,9},{9,8},{10,11... | collective-permute-start | bytes 196616 | tf_op jit(solution)/shard_map/ppermute | solution.py:653

commit v2 on v1

v2 whole, which is shorter than its diff:
```python
import functools

import jax
import jax.numpy as jnp
from jax import lax
from jax.experimental import pallas as pl
from jax.experimental.pallas import tpu as pltpu
from jax.sharding import PartitionSpec as P

epsilon = 1e-05
f32 = jnp.float32
bf16 = jnp.bfloat16
LANES = 128
WIDE = 512
VMEM_BYTES = 32 * 2**20


def split(values):
    high = values.astype(bf16)
    low = (values - high.astype(f32)).astype(bf16)
    return high, low


def halves(weight):
    return jnp.concatenate(split(weight.T), axis=0)


def folded(stacked):
    half = stacked.shape[0] // 2
    return stacked[:half] + stacked[half:]


def times(factor, columns):
    stacked = jnp.concatenate(split(columns), axis=0)
    wide = jnp.concatenate([factor, factor], axis=1)
    return folded(jnp.dot(wide, stacked, preferred_element_type=f32))


def centered(weight):
    return weight - jnp.mean(weight, axis=-1, keepdims=True)


def bias_block(row):
    return jnp.broadcast_to(row, (LANES, row.shape[-1])).T


def spread_out(block, width):
    return jnp.concatenate([block] * (width // LANES), axis=1)


def scaled(columns):
    spread = jnp.mean(columns * columns, axis=0, keepdims=True)
    return columns * lax.rsqrt(spread + epsilon)


def iota(shape, axis):
    return lax.broadcasted_iota(jnp.int32, shape, axis)


def hot(rows, index):
    return (iota((rows, index.shape[1]), 0) == index).astype(f32)


def block_gather(block, index):
    features = block.shape[0]
    pieces = []
    for start in range(0, index.shape[1], LANES):
        wide = jnp.broadcast_to(index[:, start : start + LANES], (features, LANES))
        found = jnp.take_along_axis(block, wide & (LANES - 1), axis=1)
        pieces.append(jnp.where((wide >= 0) & (wide < LANES), found, 0.0))
    return jnp.concatenate(pieces, axis=1)


def hot_gather(stacked, index):
    chosen = hot(stacked.shape[1], index).astype(bf16)
    return folded(jnp.dot(stacked, chosen, preferred_element_type=f32))


def stacked_halves(columns):
    return jnp.concatenate(split(columns), axis=0)


def prepare(edge, node, bias, factors, columns):
    for place, weight in enumerate(
        (edge[0], edge[1], centered(edge[2]), node[0], node[1], centered(node[2]))
    ):
        factors[place] = halves(weight)
    for place in range(4):
        row = bias[place : place + 1]
        columns[place] = bias_block(centered(row) if place % 2 else row)


def edge_sum(before, validity, factor, column):
    slots, count = validity.shape
    second_bias = spread_out(column, count)
    total = None
    for slot in range(slots):
        message = times(factor, jnp.maximum(before(slot), 0.0)) + second_bias
        spread = jnp.mean(message * message, axis=0, keepdims=True)
        message = message * (lax.rsqrt(spread + epsilon) * validity[slot : slot + 1, :])
        total = message if total is None else total + message
    return total


def node_step(own, node_term, gathered, factors, columns):
    count = own.shape[1]
    inner_act = jnp.maximum(node_term + times(factors[4], gathered), 0.0)
    update = times(factors[5], inner_act) + spread_out(columns[3], count)
    return own + scaled(update)


def own_products(factors, columns, places, own):
    stacked = stacked_halves(own)
    rows = [jnp.concatenate([factors[place]] * 2, axis=1) for place in places]
    both = jnp.dot(jnp.concatenate(rows, axis=0), stacked, preferred_element_type=f32)
    results = []
    for number, place in enumerate(places):
        rows = 2 * own.shape[0]
        result = folded(both[number * rows : (number + 1) * rows])
        if place in (0, 3):
            result = result + spread_out(columns[0 if place == 0 else 2], own.shape[1])
        results.append(result)
    return results


def pick_columns(columns, index):
    picked = None
    for start in range(0, columns.shape[1], LANES):
        block = columns[:, start : start + LANES]
        wide = jnp.broadcast_to(index - start, block.shape)
        found = jnp.take_along_axis(block, wide & (LANES - 1), axis=1)
        picked = found if picked is None else jnp.where(wide >= 0, found, picked)
    return picked


def wide_row(rows, first, number):
    return jnp.concatenate([rows[slot : slot + 1, :] for slot in range(first, first + number)], axis=1)


def fetch(copies, semaphores):
    started = []
    for place, (source, target) in enumerate(copies):
        copy = pltpu.make_async_copy(source, target, semaphores.at[place])
        copy.start()
        started.append(copy)
    return started


def pick_kernel(
    rim,
    send_hbm,
    parent_hbm,
    share_hbm,
    state_hbm,
    coarse_nbr_hbm,
    coarse_mask_hbm,
    parent_row_hbm,
    share_row_hbm,
    nbr_hbm,
    mask_hbm,
    edge_hbm,
    node_hbm,
    bias_hbm,
    even_ref,
    odd_ref,
    dom_ref,
    rows_ref,
    state_ref,
    parent_ref,
    share_ref,
    nbr_ref,
    mask_ref,
    edge_ref,
    node_ref,
    bias_ref,
    send_s,
    parent_s,
    share_s,
    coarse_nbr,
    coarse_mask,
    semaphores,
):
    copies = fetch(
        (
            (send_hbm, send_s),
            (parent_hbm, parent_s),
            (share_hbm, share_s),
            (state_hbm, state_ref),
            (coarse_nbr_hbm, coarse_nbr),
            (coarse_mask_hbm, coarse_mask),
            (nbr_hbm, nbr_ref),
            (parent_row_hbm, parent_ref),
            (share_row_hbm, share_ref),
            (edge_hbm.at[0], edge_ref),
            (node_hbm.at[0], node_ref),
            (bias_hbm.at[0], bias_ref),
            (mask_hbm, mask_ref),
        ),
        semaphores,
    )
    for copy in copies[:4]:
        copy.wait()
    even = lax.rem(lax.axis_index("region"), 2) == 0
    first = jnp.where(even, 1, 0)
    lane = iota((1, LANES), 1)

    def fill(out, out_base, direction, lane_base, facts):
        for k in range(rim):
            row = send_s[direction, k]
            out[pl.ds(out_base + k, 1), :] = state_ref[pl.ds(row, 1), :]
            here = lane == lane_base + k
            new = (parent_s[row], share_s[row], row)
            facts = [jnp.where(here, value, fact) for value, fact in zip(new, facts)]
        return facts

    def put(out, base, facts):
        out[base : base + 8, :] = jnp.zeros((8, LANES), f32)
        out[base : base + 1, :] = facts[0].astype(f32)
        out[base + 1 : base + 2, :] = facts[1].astype(f32)

    zero = jnp.zeros((1, LANES), jnp.int32)
    own_rows = zero
    for out, direction in ((even_ref, first), (odd_ref, 1 - first)):
        facts = fill(out, 0, direction, direction * rim, [zero] * 3)
        put(out, rim, facts)
        own_rows = own_rows + facts[2]
    facts = fill(dom_ref, 0, 2, 2 * rim, [zero] * 3)
    facts = fill(dom_ref, rim, 3, 3 * rim, facts)
    base = 2 * rim
    put(dom_ref, base, facts)
    rows_ref[...] = jnp.broadcast_to(own_rows + facts[2], rows_ref.shape)
    for copy in copies[4:]:
        copy.wait()
    slots = coarse_nbr.shape[0]
    dom_ref[base + 8 : base + 8 + slots, :] = coarse_nbr[...].astype(f32)
    dom_ref[base + 8 + slots : base + 8 + 2 * slots, :] = coarse_mask[...].astype(f32)


def rim_rows(rim, even, recv_even, recv_odd, recv_dom):
    low = jnp.where(even, recv_even, recv_odd)
    high = jnp.where(even, recv_odd, recv_even)
    pad = jnp.zeros((LANES - 4 * rim, low.shape[1]), f32)
    return jnp.concatenate([low, high, recv_dom, pad], axis=0)


def before_kernel(
    rim,
    group,
    side,
    regions,
    state_ref,
    rows_ref,
    parent_ref,
    share_ref,
    nbr_ref,
    mask_ref,
    edge_ref,
    node_ref,
    bias_ref,
    edge_hbm,
    node_hbm,
    bias_hbm,
    own_ref,
    node_term_ref,
    partial_ref,
    valid_ref,
    factors,
    columns,
    place_ref,
    facts_ref,
    own_first,
    node_term_first,
    partial_first,
    nbr_first,
    valid_first,
    later_edge,
    later_node,
    later_bias,
    semaphores,
):
    later = later_edge.shape[0]
    copies = fetch(
        (
            (edge_hbm.at[pl.ds(1, later)], later_edge),
            (node_hbm.at[pl.ds(1, later)], later_node),
            (bias_hbm.at[pl.ds(1, later)], later_bias),
        ),
        semaphores,
    )
    parent = parent_ref[...]
    count = parent.shape[1]
    region = lax.axis_index("region")
    place = side_places(parent, region, regions, group, rim, side)
    place_ref[...] = jnp.broadcast_to(place, place_ref.shape)
    facts = jnp.concatenate(
        [
            parent.astype(f32),
            share_ref[...].astype(f32),
            iota((1, count), 1).astype(f32),
            jnp.zeros((5, count), f32),
        ],
        axis=0,
    )
    facts = lax.dot_general(
        facts,
        hot(LANES, place),
        (((1,), (1,)), ((), ())),
        precision=lax.Precision.HIGHEST,
        preferred_element_type=f32,
    )
    facts_ref[...] = facts
    rims = iota((1, LANES), 1) < 4 * rim
    chosen = jnp.where(rims, rows_ref[0:1, :], facts[2:3].astype(jnp.int32))
    own = state_ref[...].T
    own_ref[...] = own
    valid = mask_ref[...].astype(f32)
    valid_ref[...] = valid
    prepare(edge_ref, node_ref, bias_ref, factors, columns)
    term, source, node_term = own_products(factors, columns, (0, 1, 3), own)
    node_term_ref[...] = node_term
    stacked = stacked_halves(source)
    slots = nbr_ref.shape[0]
    for slot in range(slots):
        partial_ref[slot] = term + hot_gather(stacked, nbr_ref[slot : slot + 1, :])
    own = pick_columns(own, chosen)
    own_first[...] = own
    term, node_term = own_products(factors, columns, (0, 3), own)
    node_term_first[...] = node_term
    valid_first[...] = pick_columns(valid, chosen)
    nbr = pick_columns(nbr_ref[...], chosen)
    nbr_first[...] = nbr
    together = WIDE // LANES
    for slot in range(0, slots, together):
        found = hot_gather(stacked, wide_row(nbr, slot, together))
        for number in range(together):
            partial_first[slot + number] = (
                term + found[:, number * LANES : (number + 1) * LANES]
            )
    for copy in copies:
        copy.wait()


def weighted(selection, rows):
    pair = jnp.concatenate(split(rows), axis=1)
    both = jnp.dot(selection.astype(bf16), pair, preferred_element_type=f32)
    return both[:, :LANES] + both[:, LANES:]


def first_kernel(
    rim,
    side,
    own_ref,
    node_term_ref,
    partial_ref,
    nbr_ref,
    valid_ref,
    count,
    factors,
    columns,
    facts_ref,
    recv_even,
    recv_odd,
    recv_dom,
    even_ref,
    odd_ref,
    dom_ref,
    block_ref,
):
    even = lax.rem(lax.axis_index("region"), 2) == 0
    outer = rim_rows(rim, even, recv_even[:rim], recv_odd[:rim], recv_dom[: 2 * rim]).T
    block = times(factors[1], outer)
    block_ref[...] = block

    def before(slot):
        return partial_ref[slot] + block_gather(block, nbr_ref[slot : slot + 1, :] - count)

    gathered = edge_sum(before, valid_ref, factors[2], columns[1])
    fine = node_step(own_ref[...], node_term_ref[...], gathered, factors, columns)
    rows = fine.T
    dom_ref[...] = rows[2 * rim : 4 * rim, :]
    late = (fine * facts_ref[1:2, :]).T
    low, high = late[4 * rim : 4 * rim + side], late[4 * rim + side : 4 * rim + 2 * side]
    up, down = rows[:rim], rows[rim : 2 * rim]
    for out, is_low in ((even_ref, even), (odd_ref, jnp.logical_not(even))):
        out[0:side, :] = jnp.where(is_low, low, high)
        out[side : side + 8, :] = facts_ref[...]
        out[side + 8 : side + 8 + rim, :] = jnp.where(is_low, down, up)
        out[side + 8 + rim :, :] = jnp.zeros((out.shape[0] - side - 8 - rim, LANES), f32)


def fine_kernel(
    rim,
    group,
    own_ref,
    node_term_ref,
    partial_ref,
    nbr_ref,
    valid_ref,
    factors,
    columns,
    block_ref,
    parent_ref,
    share_ref,
    dom_rows,
    side_facts,
    meta_even,
    meta_odd,
    meta_dom,
    fine_ref,
    mine_ref,
):
    block = block_ref[...]
    count = own_ref.shape[1]

    def before(slot):
        return partial_ref[slot] + block_gather(block, nbr_ref[slot : slot + 1, :] - count)

    gathered = edge_sum(before, valid_ref, factors[2], columns[1])
    fine = node_step(own_ref[...], node_term_ref[...], gathered, factors, columns)
    fine_ref[...] = fine
    region = lax.axis_index("region")
    share = share_ref[...].astype(f32)
    chosen = hot(group, parent_ref[...] - region * group) * share
    mine_ref[0:group, :] = weighted(chosen, fine.T)
    totals = lax.dot_general(
        jnp.ones((8, count), f32), chosen, (((1,), (1,)), ((), ())), preferred_element_type=f32
    )
    base = group
    for start in range(0, group, LANES):
        mine_ref[base : base + 8, :] = totals[:, start : start + LANES]
        base += 8
    mine_ref[base : base + 2 * rim, :] = dom_rows[...]
    base += 2 * rim
    facts = (
        meta_even[rim : rim + 8, :]
        + meta_odd[rim : rim + 8, :]
        + meta_dom[2 * rim : 2 * rim + 8, :]
    )
    rims = iota(facts.shape, 1) < 4 * rim
    mine_ref[base : base + 8, :] = jnp.where(rims, facts, side_facts[...])


def side_places(parent, region, regions, group, rim, side):
    count = parent.shape[1]
    earlier = (iota((count, count), 0) < iota((count, count), 1)).astype(bf16)
    place = jnp.full(parent.shape, -1, jnp.int32)
    for number, steps in enumerate((regions - 1, 1)):
        local = parent - lax.rem(region + steps, regions) * group
        inside = (local >= 0) & (local < group)
        member = jnp.broadcast_to(jnp.where(inside, 1.0, 0.0), (8, count)).astype(bf16)
        rank = jnp.dot(member, earlier, preferred_element_type=f32)[0:1].astype(jnp.int32)
        place = jnp.where(inside, rank + (4 * rim + number * side), place)
    return place


def prepare_kernel(
    rim,
    token_ref,
    sent_dom,
    meta_dom,
    edge_ref,
    node_ref,
    bias_ref,
    factors,
    columns,
    chosen_ref,
    valid_ref,
):
    slots, group = valid_ref.shape
    first = lax.axis_index("dom") == 0
    sent, received = sent_dom[2 * rim + 8 :, :], meta_dom[2 * rim + 8 :, :]
    tiles = jnp.concatenate(
        [jnp.where(first, sent, received), jnp.where(first, received, sent)], axis=1
    )
    valid_ref[...] = tiles[slots:]
    for slot in range(slots):
        chosen_ref[slot] = hot(group, tiles[slot : slot + 1].astype(jnp.int32)).astype(bf16)
    for layer in range(factors.shape[0]):
        prepare(
            edge_ref.at[layer],
            node_ref.at[layer],
            bias_ref.at[layer],
            factors.at[layer],
            columns.at[layer],
        )


def late_places(nbr_ref, place_ref, late_ref):
    index = nbr_ref[...]
    slots, count = index.shape
    for start in range(0, count, LANES):
        now = index[:, start : start + LANES]
        late = jnp.where(now >= count, now - count, -1)
        for base in range(0, count, LANES):
            table = jnp.broadcast_to(place_ref[0:1, base : base + LANES], (slots, LANES))
            inner = now - base
            found = jnp.take_along_axis(table, inner & (LANES - 1), axis=1)
            late = jnp.where((inner >= 0) & (inner < LANES), found, late)
        late_ref[:, start : start + LANES] = late


def gather_side_kernel(rim, group, side, regions, mine_ref, even_mine, odd_mine, sum_ref):
    region = lax.axis_index("region")
    total = mine_ref[0:group, :]
    base = group + 8 * (group // LANES)
    weight = [mine_ref[group + 8 * b : group + 8 * b + 8, :] for b in range(group // LANES)]
    weight = jnp.concatenate(weight, axis=1)
    for block in (even_mine, odd_mine):
        depth = block.shape[0]
        facts = block[side : side + 8, :]
        index = facts[0:1].astype(jnp.int32) - region * group
        chosen = hot(group, jnp.where(iota((1, LANES), 1) < 4 * rim, -1, index))
        weight = weight + lax.dot_general(
            jnp.broadcast_to(facts[1:2], (8, LANES)),
            chosen,
            (((1,), (1,)), ((), ())),
            preferred_element_type=f32,
        )
        rows = block[0:side, :]
        spread = jnp.concatenate(
            [jnp.zeros((4 * rim, LANES), f32), rows, rows]
            + [jnp.zeros((LANES - 4 * rim - 2 * side, LANES), f32)] * (LANES > 4 * rim + 2 * side),
            axis=0,
        )
        both = jnp.dot(
            chosen.astype(bf16),
            jnp.concatenate(split(spread), axis=1),
            preferred_element_type=f32,
        )
        total = total + (both[:, :LANES] + both[:, LANES:])
    sum_ref[0:group, :] = total
    for b in range(group // LANES):
        sum_ref[group + 8 * b : group + 8 * b + 8, :] = weight[:, b * LANES : (b + 1) * LANES]
    sum_ref[base:, :] = mine_ref[base:, :]


def coarse_layer(own, chosen, valid, factors, columns):
    (term,) = own_products(factors, columns, (0,), own)
    (node_term,) = own_products(factors, columns, (3,), own)
    stacked = stacked_halves(times(factors[1], own))
    found = jnp.dot(stacked, chosen, preferred_element_type=f32)
    count = own.shape[1]

    def before(slot):
        return folded(found[:, slot * count : (slot + 1) * count]) + term

    gathered = edge_sum(before, valid, factors[2], columns[1])
    return node_step(own, node_term, gathered, factors, columns)


def coarse_kernel(
    group,
    mine_ref,
    other_ref,
    chosen_ref,
    valid_ref,
    factors,
    columns,
    group_ref,
    out_ref,
    rows_ref,
):
    dom = lax.axis_index("dom")
    total = mine_ref[0:group, :] + other_ref[0:group, :]
    weight = [
        mine_ref[group + 8 * b : group + 8 * b + 1, :]
        + other_ref[group + 8 * b : group + 8 * b + 1, :]
        for b in range(group // LANES)
    ]
    own = total.T / jnp.maximum(jnp.concatenate(weight, axis=1), 1.0)
    chosen = jnp.concatenate([chosen_ref[slot] for slot in range(chosen_ref.shape[0])], axis=1)
    valid = valid_ref[...]
    own = coarse_layer(own, chosen, valid, factors.at[0], columns.at[0])
    own = coarse_layer(own, chosen, valid, factors.at[1], columns.at[1])
    group_ref[...] = own
    rows_ref[...] = own.T
    rows = out_ref.shape[0]
    out_ref[...] = rows_ref[pl.ds(pl.multiple_of(dom * rows, rows), rows), :]


def between_kernel(
    rim,
    group,
    side,
    fine_ref,
    even_mine,
    odd_mine,
    mine_ref,
    other_ref,
    coarse_mine,
    nbr_ref,
    place_ref,
    parent_ref,
    share_ref,
    edge_ref,
    node_ref,
    bias_ref,
    own_ref,
    late_ref,
    partial_ref,
    late_index,
    factors,
    columns,
):
    last = edge_ref.shape[0] - 1
    prepare(edge_ref.at[last], node_ref.at[last], bias_ref.at[last], factors, columns)
    region = lax.axis_index("region")
    even = lax.rem(region, 2) == 0
    base = side + 8
    dom_base = group + 8 * (group // LANES)
    outer = rim_rows(
        rim,
        even,
        even_mine[base : base + rim, :],
        odd_mine[base : base + rim, :],
        other_ref[dom_base : dom_base + 2 * rim, :],
    ).T
    facts = mine_ref[dom_base + 2 * rim : dom_base + 2 * rim + 8, :]
    stacked = stacked_halves(coarse_mine[...])
    local = facts[0:1].astype(jnp.int32) - region * group
    late_ref[...] = outer + (facts[1:2] * 0.25) * hot_gather(stacked, local)
    share = share_ref[...].astype(f32) * 0.25
    own = fine_ref[...] + share * hot_gather(stacked, parent_ref[...] - region * group)
    own_ref[...] = own
    stacked = stacked_halves(times(factors[1], own))
    for slot in range(nbr_ref.shape[0]):
        partial_ref[slot] = hot_gather(stacked, nbr_ref[slot : slot + 1, :])
    late_places(nbr_ref, place_ref, late_index)


def side_kernel(
    rim, group, regions, late_in, mine_ref, other_ref, first_ref, second_ref, late_ref, back_ref
):
    region = lax.axis_index("region")
    near = lax.axis_index("dom") == 0
    base = group + 8 * (group // LANES) + 2 * rim
    facts = jnp.concatenate([mine_ref[base : base + 8, :], other_ref[base : base + 8, :]], axis=1)
    index = facts[0:1].astype(jnp.int32)

    def home(here, distance):
        below = (lax.rem(region // distance, 2) == 0) == here
        return lax.rem(region + jnp.where(below, regions - distance, distance), regions)

    late = None
    for block, here in ((first_ref, True), (second_ref, False)):
        place = jnp.where(near, home(here, 1), home(here, 2))
        found = hot_gather(stacked_halves(block[...]), index - place * group)
        late = found if late is None else late + found
    late = late * (facts[1:2] * 0.25)
    late_ref[...] = late_in[...] + late[:, :LANES]
    back_ref[...] = late[:, LANES:]


def last_kernel(
    own_ref,
    late_in,
    back_ref,
    partial_ref,
    late_index,
    place_ref,
    valid_ref,
    factors,
    columns,
    out_ref,
):
    late = late_in[...] + back_ref[...]
    own = own_ref[...] + block_gather(late, place_ref[0:1, :])
    block = times(factors[1], late)
    term, node_term = own_products(factors, columns, (0, 3), own)

    def before(slot):
        return partial_ref[slot] + block_gather(block, late_index[slot : slot + 1, :]) + term

    gathered = edge_sum(before, valid_ref, factors[2], columns[1])
    out_ref[...] = node_step(own, node_term, gathered, factors, columns).T


def whole():
    return pl.BlockSpec(memory_space=pltpu.VMEM)


def far():
    return pl.BlockSpec(memory_space=pltpu.HBM)


def kept(value):
    return pltpu.with_memory_space_constraint(value, pltpu.HBM)


def scalars():
    return pl.BlockSpec(memory_space=pltpu.SMEM)


def kernel_call(body, in_specs, outs, scratch=(), copies=0, flops=0):
    outs = [(out, f32) if isinstance(out[0], int) else out for out in outs]
    return pl.pallas_call(
        body,
        in_specs=in_specs,
        out_specs=tuple(whole() for _ in outs),
        out_shape=tuple(jax.ShapeDtypeStruct(shape, kind) for shape, kind in outs),
        scratch_shapes=list(scratch) + [pltpu.SemaphoreType.DMA((copies,))] * (copies > 0),
        compiler_params=pltpu.CompilerParams(vmem_limit_bytes=VMEM_BYTES),
        cost_estimate=pl.CostEstimate(
            flops=flops, bytes_accessed=4 * 2**20, transcendentals=0
        ),
    )


def swap(value, axis, partner, count):
    return lax.ppermute(value, axis, [(source, partner(source) % count) for source in range(count)])


def body(
    fine_state,
    fine_nbr,
    fine_mask,
    send_rows,
    coarse_nbr,
    coarse_mask,
    parent,
    interp_share,
    edge_w,
    node_w,
    biases,
):
    count, width = fine_state.shape
    own_coarse = coarse_nbr.shape[1]
    slots = coarse_nbr.shape[0]
    regions = lax.axis_size("region")
    domains = lax.axis_size("dom")
    group = domains * own_coarse
    rim = send_rows.shape[1]
    side = count // (8 * domains)
    fine_state, fine_nbr, fine_mask, send_rows, coarse_nbr, coarse_mask = (
        kept(value)
        for value in (fine_state, fine_nbr, fine_mask, send_rows, coarse_nbr, coarse_mask)
    )
    parent_row = kept(parent[None, :])
    share_row = kept(interp_share[None, :])
    parent, interp_share = kept(parent), kept(interp_share)
    weights = (kept(edge_w), kept(node_w), kept(biases))
    i32 = jnp.int32

    def even_partner(r):
        return r - 1 if r % 2 == 0 else r + 1

    def odd_partner(r):
        return r + 1 if r % 2 == 0 else r - 1

    def even_two_partner(r):
        return r - 2 if r // 2 % 2 == 0 else r + 2

    def odd_two_partner(r):
        return r + 2 if r // 2 % 2 == 0 else r - 2

    def even_swap(value):
        return swap(value, "region", even_partner, regions)

    def odd_swap(value):
        return swap(value, "region", odd_partner, regions)

    def dom_swap(value):
        return swap(value, "dom", lambda d: d + 1, domains)

    def both_swap(value, near, distant):
        pairs = []
        for r in range(regions):
            for d in range(domains):
                target = (near(r) if d == 0 else distant(r)) % regions
                pairs.append((r * domains + d, target * domains + d))
        return lax.ppermute(value, ("region", "dom"), pairs)

    columns_shape = (width, count)
    row_shape = ((1, count), i32)
    fine_slots = (fine_nbr.shape, i32)
    (
        even_out,
        odd_out,
        dom_out,
        sent_rows,
        state,
        parents,
        shares,
        nbr,
        mask,
        edge_first,
        node_first,
        bias_first,
    ) = kernel_call(
        functools.partial(pick_kernel, rim),
        [far()] * 13,
        [
            (rim + 8, width),
            (rim + 8, width),
            (2 * rim + 8 + 2 * slots, width),
            ((8, LANES), i32),
            fine_state.shape,
            row_shape,
            row_shape,
            fine_slots,
            fine_slots,
            edge_w.shape[1:],
            node_w.shape[1:],
            biases.shape[1:],
        ],
        [
            pltpu.SMEM(send_rows.shape, i32),
            pltpu.SMEM(parent.shape, i32),
            pltpu.SMEM(interp_share.shape, i32),
            pltpu.VMEM(coarse_nbr.shape, i32),
            pltpu.VMEM(coarse_mask.shape, i32),
        ],
        copies=13,
    )(
        send_rows,
        parent,
        interp_share,
        fine_state,
        coarse_nbr,
        coarse_mask,
        parent_row,
        share_row,
        fine_nbr,
        fine_mask,
        *weights,
    )
    meta_even = even_swap(even_out)
    meta_odd = odd_swap(odd_out)
    meta_dom = dom_swap(dom_out)

    later = edge_w.shape[0] - 1
    (
        own,
        node_term,
        partial,
        valid,
        factors,
        columns,
        place,
        side_facts,
        own_some,
        node_term_some,
        partial_some,
        nbr_some,
        valid_some,
        edge_later,
        node_later,
        bias_later,
    ) = kernel_call(
        functools.partial(before_kernel, rim, group, side, regions),
        [whole()] * 9 + [far()] * 3,
        [
            columns_shape,
            columns_shape,
            (slots, width, count),
            fine_mask.shape,
            ((6, 2 * width, width), bf16),
            (4, width, LANES),
            ((8, count), i32),
            (8, LANES),
            (width, LANES),
            (width, LANES),
            (slots, width, LANES),
            ((slots, LANES), i32),
            (slots, LANES),
            (later,) + edge_w.shape[1:],
            (later,) + node_w.shape[1:],
            (later,) + biases.shape[1:],
        ],
        copies=3,
        flops=4 * 10**9,
    )(
        state,
        sent_rows,
        parents,
        shares,
        nbr,
        mask,
        edge_first,
        node_first,
        bias_first,
        *weights,
    )

    block_rows = side + 8 + rim + 8
    dom_rows = group + 8 * (group // LANES) + 2 * rim + 8

    def first_body(*refs):
        first_kernel(rim, side, *refs[:5], count, *refs[5:])

    even_out, odd_out, dom_some, block = kernel_call(
        first_body,
        [whole()] * 11,
        [(block_rows, width), (block_rows, width), (2 * rim, width), (width, LANES)],
    )(
        own_some,
        node_term_some,
        partial_some,
        nbr_some,
        valid_some,
        factors,
        columns,
        side_facts,
        meta_even,
        meta_odd,
        meta_dom,
    )
    even_mine = even_swap(even_out)
    odd_mine = odd_swap(odd_out)

    fine_one, mine = kernel_call(
        functools.partial(fine_kernel, rim, group),
        [whole()] * 15,
        [columns_shape, (dom_rows, width)],
        flops=4 * 10**9,
    )(
        own,
        node_term,
        partial,
        nbr,
        valid,
        factors,
        columns,
        block,
        parents,
        shares,
        dom_some,
        side_facts,
        meta_even,
        meta_odd,
        meta_dom,
    )
    (mine,) = kernel_call(
        functools.partial(gather_side_kernel, rim, group, side, regions),
        [whole()] * 3,
        [(dom_rows, width)],
    )(mine, even_mine, odd_mine)
    other = dom_swap(mine)

    factors, columns, group_chosen, group_valid = kernel_call(
        functools.partial(prepare_kernel, rim),
        [whole()] * 6,
        [
            ((later - 1, 6, 2 * width, width), bf16),
            (later - 1, 4, width, LANES),
            ((slots, group, group), bf16),
            (slots, group),
        ],
        flops=10**9,
    )(mine, dom_out, meta_dom, edge_later, node_later, bias_later)

    coarse_group, coarse_out = kernel_call(
        functools.partial(coarse_kernel, group),
        [whole()] * 6,
        [(width, group), (own_coarse, width)],
        [pltpu.VMEM((group, width), f32)],
    )(mine, other, group_chosen, group_valid, factors, columns)
    first = both_swap(coarse_group, even_partner, even_two_partner)
    second = both_swap(coarse_group, odd_partner, odd_two_partner)

    own, late, partial, late_index, factors, columns = kernel_call(
        functools.partial(between_kernel, rim, group, side),
        [whole()] * 13,
        [
            columns_shape,
            (width, LANES),
            (slots, width, count),
            fine_slots,
            ((6, 2 * width, width), bf16),
            (4, width, LANES),
        ],
        flops=4 * 10**9,
    )(
        fine_one,
        even_mine,
        odd_mine,
        mine,
        other,
        coarse_group,
        nbr,
        place,
        parents,
        shares,
        edge_later,
        node_later,
        bias_later,
    )
    late, back = kernel_call(
        functools.partial(side_kernel, rim, group, regions),
        [whole()] * 5,
        [(width, LANES), (width, LANES)],
    )(late, mine, other, first, second)
    back = dom_swap(back)
    (fine_out,) = kernel_call(last_kernel, [whole()] * 9, [(count, width)])(
        own, late, back, partial, late_index, place, valid, factors, columns
    )
    return (fine_out, coarse_out)


def solution(mesh):
    return jax.shard_map(
        body,
        mesh=mesh,
        in_specs=(
            P(("region", "dom"), None),
            P(None, ("region", "dom")),
            P(None, ("region", "dom")),
            P(None, ("region", "dom")),
            P(None, ("region", "dom")),
            P(None, ("region", "dom")),
            P(("region", "dom")),
            P(("region", "dom")),
            P(),
            P(),
            P(),
        ),
        out_specs=(P(("region", "dom"), None), P(("region", "dom"), None)),
        check_vma=False,
    )
```

time: 47.1 us -> 45.2 us (0.960)
  waiting for transfers between devices: 7.84 us -> 5.15 us
  starting transfers between devices: 12 us -> 13.7 us
  Pallas kernels: 26.3 us -> 25.5 us
    ppermute x7, waiting for transfers between devices: 5.45 us -> 1.73 us  [swap(): lax.ppermute(value, axis, [(source, partner(source) % count) for source i...]
    ppermute x2, waiting for transfers between devices: 2.39 us -> 3.42 us  [both_swap(): return lax.ppermute(value, ('region', 'dom'), pairs)]
    pallas_call x4 -> x5, Pallas kernels: 11.8 us -> 12.8 us  [the longest x1 4.43 us: body(): kernel_call(last_kernel, [whole()] * 9, [(count, width)])]
    ppermute x7, starting transfers between devices: 9.62 us -> 10.5 us  [swap(): lax.ppermute(value, axis, [(source, partner(source) % count) for source i...]
    ppermute x2, starting transfers between devices: 2.39 us -> 3.21 us  [both_swap(): return lax.ppermute(value, ('region', 'dom'), pairs)]
    pallas_call x1, Pallas kernels: 3.78 us -> 2.98 us  [body(): kernel_call(functools.partial(between_kernel, rim, group, side), [whole()...]
    pallas_call x1, Pallas kernels: 4.83 us -> 4.04 us  [body(): kernel_call(functools.partial(before_kernel, rim, group, side, regions),...]
  transfers between devices with their start and end apart: 9 -> 9, of which waited for: 4 -> 4; matrix products, arithmetic and copies ran while one was open for 0% -> 0% of each run, Pallas kernels for 23% -> 27%
where the time goes in v2:
time: 45.2 us; the launch traced here: 45 us
  Pallas kernels  25.5 us (56%)
  starting transfers between devices  13.7 us (30%)
  waiting for transfers between devices  5.15 us (11%)
  between operations  0.73 us (2%)
    ppermute x7, starting transfers between devices, swap(): lax.ppermute(value, axis, [(source, partner(source) % count) for source i...  10.5 us
    pallas_call x1, Pallas kernels, body(): kernel_call(functools.partial(coarse_kernel, group), [whole()] * 6, [(wid...  5.14 us
    pallas_call x1, Pallas kernels, body(): kernel_call(last_kernel, [whole()] * 9, [(count, width)])  4.43 us
    pallas_call x1, Pallas kernels, body(): kernel_call(functools.partial(before_kernel, rim, group, side, regions),...  4.04 us
    pallas_call x1, Pallas kernels, body(): kernel_call(functools.partial(fine_kernel, rim, group), [whole()] * 15, [...  3.94 us
    ppermute x2, waiting for transfers between devices, both_swap(): return lax.ppermute(value, ('region', 'dom'), pairs)  3.42 us
    ppermute x2, starting transfers between devices, both_swap(): return lax.ppermute(value, ('region', 'dom'), pairs)  3.21 us
    pallas_call x1, Pallas kernels, body(): kernel_call(functools.partial(between_kernel, rim, group, side), [whole()...  2.98 us
  transfers between devices with their start and end apart: 9, of which 4 were waited for; matrix products, arithmetic and copies ran while one was open for 0% of the time, Pallas kernels for 27%

profile of v2, /device:TPU:0, one launch (start us, length us, event | category | flops | bytes accessed | tf_op | source)
XLA Modules:
  0.0 45.0 jit_solution(12068301181810532604)
XLA Ops:
  0.6 1.3 %shard_map.122 = (f32[24,128]{1,0:T(8,128)S(1)}, f32[24,128]{1,0:T(8,128)S(1)}, f32[72,128]{1,0:T(8,128)S(1)}, s32[8,128]{1,0:T(8,128)S(1)}, f32[512,128]{1,0:T(...) custom-call(s32[4,16]{1,0:T(4,128)} %send_hbm.1, ...), custom_call_target="tpu_custom_call" | custom-call | bytes 4194304 | tf_op jit(solution)/shard_map/pallas_call | solution.py:789
  2.0 0.5 %collective-permute-start.2 = (f32[72,128]{1,0:T(8,128)S(1)}, f32[72,128]{1,0:T(8,128)S(1)}, u32[]{:S(2)}, u32[]{:S(2)}) collective-permute-start(f32[72,128]{1,0:T(8,128)S(1)} %get-tuple-element.73.sent_dom), channel_id=1, source_target_pairs={{0,1},{1,0},{2,3},{3,2},{4,5},{5,4},{6,7},{7,6},{8,9},{9,8},{10,11... | collective-permute-start | bytes 110600 | tf_op jit(solution)/shard_map/ppermute | solution.py:710
  2.5 6.6 %collective-permute-start = (f32[24,128]{1,0:T(8,128)S(1)}, f32[24,128]{1,0:T(8,128)S(1)}, u32[]{:S(2)}, u32[]{:S(2)}) collective-permute-start(f32[24,128]{1,0:T(8,128)S(1)} %get-tuple-element.71), channel_id=1, source_target_pairs={{0,30},{2,4},{4,2},{6,8},{8,6},{10,12},{12,10},{14,16},{16,14},{18... | collective-permute-start | bytes 36872 | tf_op jit(solution)/shard_map/ppermute | solution.py:710
  9.0 0.0 collective-permute-start.1
  9.0 4.0 %shard_map.123 = (f32[128,512]{1,0:T(8,128)S(1)}, f32[128,512]{1,0:T(8,128)S(1)}, f32[16,128,512]{2,1,0:T(8,128)S(1)}, f32[16,512]{1,0:T(8,128)S(1)}, bf16[6,256...) custom-call(f32[512,128]{1,0:T(8,128)S(1)} %get-tuple-element.50.sta, ...), custom_call_target="tpu_custom_call" | custom-call | flops 4000000000 | bytes 4194304 | tf_op jit(solution)/shard_map/pallas_call | solution.py:849
  13.1 0.0 collective-permute-done.refs_8_.meta_even
  13.1 0.0 collective-permute-done.1.refs_9_.meta_odd
  13.1 0.0 collective-permute-done.2.refs_10_.meta_dom
  13.1 1.8 %shard_map.124 = (f32[64,128]{1,0:T(8,128)S(1)}, f32[64,128]{1,0:T(8,128)S(1)}, f32[32,128]{1,0:T(8,128)S(1)}, f32[128,128]{1,0:T(8,128)S(1)}) custom-call(f32[128,128]{1,0:T(8,128)S(1)} %get-tuple-element.65.refs_0_, f32[128,128]{1,0:T(8,128)S(1)} %get-tuple-element.66.refs_1_, f32[16,128,128]{2,1,0:T(8,128)S(1)} %get-tuple-element.67.refs_2_, ...), custom_call_target="tpu_custom_call" | custom-call | bytes 4194304 | tf_op jit(solution)/shard_map/pallas_call | solution.py:891
  15.0 3.3 %collective-permute-start.3 = (f32[64,128]{1,0:T(8,128)S(1)}, f32[64,128]{1,0:T(8,128)S(1)}, u32[]{:S(2)}, u32[]{:S(2)}) collective-permute-start(f32[64,128]{1,0:T(8,128)S(1)} %get-tuple-element.77), channel_id=1, source_target_pairs={{0,30},{2,4},{4,2},{6,8},{8,6},{10,12},{12,10},{14,16},{16,14},{18... | collective-permute-start | bytes 98312 | tf_op jit(solution)/shard_map/ppermute | solution.py:710
  18.2 0.0 collective-permute-start.4
  18.2 3.9 %shard_map.125 = (f32[128,512]{1,0:T(8,128)S(1)}, f32[312,128]{1,0:T(8,128)S(1)}) custom-call(f32[128,512]{1,0:T(8,128)S(1)} %get-tuple-element.59.own_ref, f32[128,512]{1,0:T(8,128)S(1)} %get-tuple-element.60.node_term_ref, f32[16,128,512]{2,1,0:T(8,128)S(1)} %get-tuple-element.61.partial_ref, s32[16,512]{1,0:T(8,128)S(1)} %get-tuple-element.54.nbr_ref, ...), custom_call_target="tpu_custom_call" | custom-call | flops 4000000000 | bytes 4194304 | tf_op jit(solution)/shard_map/pallas_call | solution.py:911
  22.2 0.4 collective-permute-done.3.even_mine
  22.5 0.0 collective-permute-done.4.odd_mine
  22.5 0.3 shard_map.126.token_ref.mine_ref
  22.8 0.1 collective-permute-start.5
  22.9 1.3 %shard_map.127 = (bf16[2,6,256,128]{3,2,1,0:T(8,128)(2,1)S(1)}, f32[2,4,128,128]{3,2,1,0:T(8,128)S(1)}, bf16[16,256,256]{2,1,0:T(8,128)(2,1)S(1)}, f32[16,256]{1,0:T(8,128)S(1)}) custom-call(f32[312,128]{1,0:T(8,128)S(1)} %shard_map.126.token_ref.mine_ref, f32[72,128]{1,0:T(8,128)S(1)} %get-tuple-element.73.sent_dom, ...), custom_call_target="tpu_custom_call" | custom-call | flops 1000000000 | bytes 4194304 | tf_op jit(solution)/shard_map/pallas_call | solution.py:940
  24.2 0.1 collective-permute-done.5.other_ref
  24.3 5.1 %shard_map.128 = (f32[128,256]{1,0:T(8,128)S(1)}, f32[128,128]{1,0:T(8,128)}) custom-call(f32[312,128]{1,0:T(8,128)S(1)} %shard_map.126.token_ref.mine_ref, f32[312,128]{1,0:T(8,128)S(1)} %collective-permute-done.5.other_ref, bf16[16,256,256]{2,1,0:T(8,128)(2,1)S(1)} %get-tuple-element.83.chosen_ref, f32[16,256]{1,0:T(8,128)S(1)} %get-tuple-element.84.valid_ref, ...), custom_call_target="tpu_custom_call" | custom-call | bytes 4194304 | tf_op jit(solution)/shard_map/pallas_call | solution.py:952
  29.4 3.2 %collective-permute-start.6 = (f32[128,256]{1,0:T(8,128)S(1)}, f32[128,256]{1,0:T(8,128)S(1)}, u32[]{:S(2)}, u32[]{:S(2)}) collective-permute-start(f32[128,256]{1,0:T(8,128)S(1)} %get-tuple-element.87.coarse_mine), channel_id=1, source_target_pairs={{0,30},{1,29},{2,4},{3,31},{4,2},{5,9},{6,8},{7,11},{8,6},{9,5},{1... | collective-permute-start | bytes 393224 | tf_op jit(solution)/shard_map/ppermute | solution.py:771
  32.6 0.0 collective-permute-start.7
  32.6 3.0 %shard_map.129 = (f32[128,512]{1,0:T(8,128)S(1)}, f32[128,128]{1,0:T(8,128)S(1)}, f32[16,128,512]{2,1,0:T(8,128)S(1)}, s32[16,512]{1,0:T(8,128)S(1)}, bf16[6,256...) custom-call(f32[128,512]{1,0:T(8,128)S(1)} %get-tuple-element.76.fine_ref, ...), custom_call_target="tpu_custom_call" | custom-call | flops 4000000000 | bytes 4194304 | tf_op jit(solution)/shard_map/pallas_call | solution.py:961
  35.6 3.4 %collective-permute-done.6.first_ref = f32[128,256]{1,0:T(8,128)S(1)} collective-permute-done((f32[128,256]{1,0:T(8,128)S(1)}, f32[128,256]{1,0:T(8,128)S(1)}, u32[]{:S(2)}, u32[]{:S(2)}) %collective-permute-start.6) | collective-permute-done | bytes 131104 | tf_op jit(solution)/shard_map/ppermute | solution.py:771
  39.0 0.0 collective-permute-done.7.second_ref
  39.0 0.3 shard_map.130
  39.3 0.1 collective-permute-start.8
  39.4 1.2 %collective-permute-done.8.back_ref = f32[128,128]{1,0:T(8,128)S(1)} collective-permute-done((f32[128,128]{1,0:T(8,128)S(1)}, f32[128,128]{1,0:T(8,128)S(1)}, u32[]{:S(2)}, u32[]{:S(2)}) %collective-permute-start.8) | collective-permute-done | bytes 65568 | tf_op jit(solution)/shard_map/ppermute | solution.py:710
  40.6 4.4 %shard_map.131 = f32[512,128]{1,0:T(8,128)} custom-call(f32[128,512]{1,0:T(8,128)S(1)} %get-tuple-element.89.own_ref, f32[128,128]{1,0:T(8,128)S(1)} %get-tuple-element.91.late_in, f32[128,128]{1,0:T(8,128)S(1)} %collective-permute-done.8.back_ref, f32[16,128,512]{2,1,0:T(8,128)S(1)} %get-tuple-element.93.partial_ref, ...), custom_call_target="tpu_custom_call" | custom-call | bytes 4194304 | tf_op jit(solution)/shard_map/pallas_call | solution.py:994
Async XLA Ops:
  2.0 11.2 %collective-permute-start.2 = (f32[72,128]{1,0:T(8,128)S(1)}, f32[72,128]{1,0:T(8,128)S(1)}, u32[]{:S(2)}, u32[]{:S(2)}) collective-permute-start(f32[72,128]{1,0:T(8,128)S(1)} %get-tuple-element.73.sent_dom), channel_id=1, source_target_pairs={{0,1},{1,0},{2,3},{3,2},{4,5},{5,4},{6,7},{7,6},{8,9},{9,8},{10,11... | collective-permute-start | bytes 110600 | tf_op jit(solution)/shard_map/ppermute | solution.py:710
  2.5 10.6 %collective-permute-start = (f32[24,128]{1,0:T(8,128)S(1)}, f32[24,128]{1,0:T(8,128)S(1)}, u32[]{:S(2)}, u32[]{:S(2)}) collective-permute-start(f32[24,128]{1,0:T(8,128)S(1)} %get-tuple-element.71), channel_id=1, source_target_pairs={{0,30},{2,4},{4,2},{6,8},{8,6},{10,12},{12,10},{14,16},{16,14},{18... | collective-permute-start | bytes 36872 | tf_op jit(solution)/shard_map/ppermute | solution.py:710
  9.0 4.1 %collective-permute-start.1 = (f32[24,128]{1,0:T(8,128)S(1)}, f32[24,128]{1,0:T(8,128)S(1)}, u32[]{:S(2)}, u32[]{:S(2)}) collective-permute-start(f32[24,128]{1,0:T(8,128)S(1)} %get-tuple-element.72), channel_id=1, source_target_pairs={{0,2},{2,0},{4,6},{6,4},{8,10},{10,8},{12,14},{14,12},{16,18},{18,... | collective-permute-start | bytes 36872 | tf_op jit(solution)/shard_map/ppermute | solution.py:710
  15.0 7.6 %collective-permute-start.3 = (f32[64,128]{1,0:T(8,128)S(1)}, f32[64,128]{1,0:T(8,128)S(1)}, u32[]{:S(2)}, u32[]{:S(2)}) collective-permute-start(f32[64,128]{1,0:T(8,128)S(1)} %get-tuple-element.77), channel_id=1, source_target_pairs={{0,30},{2,4},{4,2},{6,8},{8,6},{10,12},{12,10},{14,16},{16,14},{18... | collective-permute-start | bytes 98312 | tf_op jit(solution)/shard_map/ppermute | solution.py:710
  18.2 4.3 %collective-permute-start.4 = (f32[64,128]{1,0:T(8,128)S(1)}, f32[64,128]{1,0:T(8,128)S(1)}, u32[]{:S(2)}, u32[]{:S(2)}) collective-permute-start(f32[64,128]{1,0:T(8,128)S(1)} %get-tuple-element.78), channel_id=1, source_target_pairs={{0,2},{2,0},{4,6},{6,4},{8,10},{10,8},{12,14},{14,12},{16,18},{18,... | collective-permute-start | bytes 98312 | tf_op jit(solution)/shard_map/ppermute | solution.py:710
  22.8 1.5 %collective-permute-start.5 = (f32[312,128]{1,0:T(8,128)S(1)}, f32[312,128]{1,0:T(8,128)S(1)}, u32[]{:S(2)}, u32[]{:S(2)}) collective-permute-start(f32[312,128]{1,0:T(8,128)S(1)} %shard_map.126.token_ref.mine_ref), channel_id=1, source_target_pairs={{0,1},{1,0},{2,3},{3,2},{4,5},{5,4},{6,7},{7,6},{8,9},{9,8},{10,11... | collective-permute-start | bytes 479240 | tf_op jit(solution)/shard_map/ppermute | solution.py:710
  29.4 9.6 %collective-permute-start.6 = (f32[128,256]{1,0:T(8,128)S(1)}, f32[128,256]{1,0:T(8,128)S(1)}, u32[]{:S(2)}, u32[]{:S(2)}) collective-permute-start(f32[128,256]{1,0:T(8,128)S(1)} %get-tuple-element.87.coarse_mine), channel_id=1, source_target_pairs={{0,30},{1,29},{2,4},{3,31},{4,2},{5,9},{6,8},{7,11},{8,6},{9,5},{1... | collective-permute-start | bytes 393224 | tf_op jit(solution)/shard_map/ppermute | solution.py:771
  32.6 6.4 %collective-permute-start.7 = (f32[128,256]{1,0:T(8,128)S(1)}, f32[128,256]{1,0:T(8,128)S(1)}, u32[]{:S(2)}, u32[]{:S(2)}) collective-permute-start(f32[128,256]{1,0:T(8,128)S(1)} %get-tuple-element.87.coarse_mine), channel_id=1, source_target_pairs={{0,2},{1,5},{2,0},{3,7},{4,6},{5,1},{6,4},{7,3},{8,10},{9,13},{10,... | collective-permute-start | bytes 393224 | tf_op jit(solution)/shard_map/ppermute | solution.py:771
  39.3 1.3 %collective-permute-start.8 = (f32[128,128]{1,0:T(8,128)S(1)}, f32[128,128]{1,0:T(8,128)S(1)}, u32[]{:S(2)}, u32[]{:S(2)}) collective-permute-start(f32[128,128]{1,0:T(8,128)S(1)} %get-tuple-element.92), channel_id=1, source_target_pairs={{0,1},{1,0},{2,3},{3,2},{4,5},{5,4},{6,7},{7,6},{8,9},{9,8},{10,11... | collective-permute-start | bytes 196616 | tf_op jit(solution)/shard_map/ppermute | solution.py:710

commit v3 on v2

--- a/solution.py
+++ b/solution.py
@@ -149,13 +149,11 @@
 def pick_kernel(
     rim,
     send_hbm,
-    parent_hbm,
-    share_hbm,
     state_hbm,
     coarse_nbr_hbm,
     coarse_mask_hbm,
-    parent_row_hbm,
-    share_row_hbm,
+    parent_hbm,
+    share_hbm,
     nbr_hbm,
     mask_hbm,
     edge_hbm,
@@ -174,8 +172,6 @@
     node_ref,
     bias_ref,
     send_s,
-    parent_s,
-    share_s,
     coarse_nbr,
     coarse_mask,
     semaphores,
@@ -183,57 +179,43 @@
     copies = fetch(
         (
             (send_hbm, send_s),
-            (parent_hbm, parent_s),
-            (share_hbm, share_s),
             (state_hbm, state_ref),
             (coarse_nbr_hbm, coarse_nbr),
             (coarse_mask_hbm, coarse_mask),
-            (nbr_hbm, nbr_ref),
-            (parent_row_hbm, parent_ref),
-            (share_row_hbm, share_ref),
             (edge_hbm.at[0], edge_ref),
             (node_hbm.at[0], node_ref),
+            (nbr_hbm, nbr_ref),
+            (parent_hbm, parent_ref),
+            (share_hbm, share_ref),
             (bias_hbm.at[0], bias_ref),
             (mask_hbm, mask_ref),
         ),
         semaphores,
     )
-    for copy in copies[:4]:
+    for copy in copies[:2]:
         copy.wait()
     even = lax.rem(lax.axis_index("region"), 2) == 0
     first = jnp.where(even, 1, 0)
     lane = iota((1, LANES), 1)
 
-    def fill(out, out_base, direction, lane_base, facts):
+    def fill(out, out_base, direction, lane_base, rows):
         for k in range(rim):
             row = send_s[direction, k]
             out[pl.ds(out_base + k, 1), :] = state_ref[pl.ds(row, 1), :]
-            here = lane == lane_base + k
-            new = (parent_s[row], share_s[row], row)
-            facts = [jnp.where(here, value, fact) for value, fact in zip(new, facts)]
-        return facts
-
-    def put(out, base, facts):
-        out[base : base + 8, :] = jnp.zeros((8, LANES), f32)
-        out[base : base + 1, :] = facts[0].astype(f32)
-        out[base + 1 : base + 2, :] = facts[1].astype(f32)
-
-    zero = jnp.zeros((1, LANES), jnp.int32)
-    own_rows = zero
-    for out, direction in ((even_ref, first), (odd_ref, 1 - first)):
-        facts = fill(out, 0, direction, direction * rim, [zero] * 3)
-        put(out, rim, facts)
-        own_rows = own_rows + facts[2]
-    facts = fill(dom_ref, 0, 2, 2 * rim, [zero] * 3)
-    facts = fill(dom_ref, rim, 3, 3 * rim, facts)
-    base = 2 * rim
-    put(dom_ref, base, facts)
-    rows_ref[...] = jnp.broadcast_to(own_rows + facts[2], rows_ref.shape)
-    for copy in copies[4:]:
+            rows = jnp.where(lane == lane_base + k, row, rows)
+        return rows
+
+    rows = fill(even_ref, 0, first, first * rim, jnp.zeros((1, LANES), jnp.int32))
+    rows = fill(odd_ref, 0, 1 - first, (1 - first) * rim, rows)
+    rows = fill(dom_ref, 0, 2, 2 * rim, rows)
+    rows = fill(dom_ref, rim, 3, 3 * rim, rows)
+    rows_ref[...] = jnp.broadcast_to(rows, rows_ref.shape)
+    for copy in copies[2:]:
         copy.wait()
     slots = coarse_nbr.shape[0]
-    dom_ref[base + 8 : base + 8 + slots, :] = coarse_nbr[...].astype(f32)
-    dom_ref[base + 8 + slots : base + 8 + 2 * slots, :] = coarse_mask[...].astype(f32)
+    base = 2 * rim
+    dom_ref[base : base + slots, :] = coarse_nbr[...].astype(f32)
+    dom_ref[base + slots : base + 2 * slots, :] = coarse_mask[...].astype(f32)
 
 
 def rim_rows(rim, even, recv_even, recv_odd, recv_dom):
@@ -292,25 +274,18 @@
     region = lax.axis_index("region")
     place = side_places(parent, region, regions, group, rim, side)
     place_ref[...] = jnp.broadcast_to(place, place_ref.shape)
-    facts = jnp.concatenate(
-        [
-            parent.astype(f32),
-            share_ref[...].astype(f32),
-            iota((1, count), 1).astype(f32),
-            jnp.zeros((5, count), f32),
-        ],
-        axis=0,
-    )
-    facts = lax.dot_general(
-        facts,
+    numbers = lax.dot_general(
+        jnp.broadcast_to(iota((1, count), 1).astype(f32), (8, count)),
         hot(LANES, place),
         (((1,), (1,)), ((), ())),
         precision=lax.Precision.HIGHEST,
         preferred_element_type=f32,
     )
-    facts_ref[...] = facts
     rims = iota((1, LANES), 1) < 4 * rim
-    chosen = jnp.where(rims, rows_ref[0:1, :], facts[2:3].astype(jnp.int32))
+    chosen = jnp.where(rims, rows_ref[0:1, :], numbers[0:1].astype(jnp.int32))
+    facts = [parent.astype(f32), share_ref[...].astype(f32), place.astype(f32)]
+    facts = jnp.concatenate(facts + [jnp.zeros((5, count), f32)], axis=0)
+    facts_ref[...] = pick_columns(facts, chosen)
     own = state_ref[...].T
     own_ref[...] = own
     valid = mask_ref[...].astype(f32)
@@ -403,9 +378,6 @@
     share_ref,
     dom_rows,
     side_facts,
-    meta_even,
-    meta_odd,
-    meta_dom,
     fine_ref,
     mine_ref,
 ):
@@ -431,13 +403,7 @@
         base += 8
     mine_ref[base : base + 2 * rim, :] = dom_rows[...]
     base += 2 * rim
-    facts = (
-        meta_even[rim : rim + 8, :]
-        + meta_odd[rim : rim + 8, :]
-        + meta_dom[2 * rim : 2 * rim + 8, :]
-    )
-    rims = iota(facts.shape, 1) < 4 * rim
-    mine_ref[base : base + 8, :] = jnp.where(rims, facts, side_facts[...])
+    mine_ref[base : base + 8, :] = side_facts[...]
 
 
 def side_places(parent, region, regions, group, rim, side):
@@ -468,7 +434,7 @@
 ):
     slots, group = valid_ref.shape
     first = lax.axis_index("dom") == 0
-    sent, received = sent_dom[2 * rim + 8 :, :], meta_dom[2 * rim + 8 :, :]
+    sent, received = sent_dom[2 * rim :, :], meta_dom[2 * rim :, :]
     tiles = jnp.concatenate(
         [jnp.where(first, sent, received), jnp.where(first, received, sent)], axis=1
     )
@@ -531,7 +497,76 @@
     sum_ref[0:group, :] = total
     for b in range(group // LANES):
         sum_ref[group + 8 * b : group + 8 * b + 8, :] = weight[:, b * LANES : (b + 1) * LANES]
-    sum_ref[base:, :] = mine_ref[base:, :]
+    count = mine_ref.shape[0]
+    sum_ref[base:count, :] = mine_ref[base:, :]
+    even = lax.rem(region, 2) == 0
+    below, above = even_mine[side : side + 8, :], odd_mine[side : side + 8, :]
+    sum_ref[count : count + 8, :] = jnp.where(even, below, above)
+    sum_ref[count + 8 : count + 16, :] = jnp.where(even, above, below)
+
+
+def known_facts(group, rim, dom, mine_ref, other_ref):
+    base = group + 8 * (group // LANES) + 2 * rim
+    first = dom == 0
+    facts = []
+    for place in range(3):
+        rows = slice(base + 8 * place, base + 8 * place + 8)
+        mine, other = mine_ref[rows, :], other_ref[rows, :]
+        facts.append((jnp.where(first, mine, other), jnp.where(first, other, mine)))
+    return facts
+
+
+def moved(rows, steps):
+    index = (iota(rows.shape, 1) - steps) & (LANES - 1)
+    return jnp.take_along_axis(rows, index, axis=1)
+
+
+def first_is_below(region, near):
+    return lax.rem(jnp.where(near, region, region // 2), 2) == 0
+
+
+def asked_columns(rim, side, region, dom, facts):
+    own, below, above = facts
+    near = dom == 0
+    lane = iota((8, LANES), 1)
+    base = 4 * rim
+    up = [jnp.where(near, mine, theirs) for mine, theirs in zip(own, above)]
+    down = [jnp.where(near, mine, theirs) for mine, theirs in zip(own, below)]
+    up_rims = jnp.where(lane < rim, up[0], moved(up[1], rim))
+    down_rims = jnp.where(lane < rim, moved(down[0], -rim), down[1])
+    up_sides = jnp.where(lane < base + side, above[0], moved(above[1], side))
+    down_sides = jnp.where(lane < base + side, moved(below[0], -side), below[1])
+    asked = []
+    for rims, sides in ((up_rims, up_sides), (down_rims, down_sides)):
+        sides = jnp.where((lane >= base) & near, sides, -1.0)
+        asked.append(jnp.where(lane < 2 * rim, rims, sides)[0:1].astype(jnp.int32))
+    first_below = first_is_below(region, near)
+    up, down = asked
+    return jnp.where(first_below, down, up), jnp.where(first_below, up, down)
+
+
+def answer_lanes(rim, side, dom, core, place):
+    lane = iota((1, LANES), 1)
+    base = 4 * rim
+    near = dom == 0
+    second = core == 1
+    from_dom = (lane >= 2 * rim) & (lane < base)
+    low_place = (place >= base) & (place < base + side)
+    low = jnp.where(lane < rim, lane + jnp.where(second, rim, 0), -1)
+    high = jnp.where((lane >= rim) & (lane < 2 * rim), lane - jnp.where(second, 0, rim), -1)
+    near_low = jnp.where(
+        from_dom,
+        jnp.where(low_place, place + jnp.where(second, 0, side), -1),
+        jnp.where(
+            (lane >= base) & (lane < base + side), lane + jnp.where(second, side, 0), low
+        ),
+    )
+    near_high = jnp.where(
+        from_dom,
+        jnp.where(place >= base + side, place - jnp.where(second, side, 0), -1),
+        jnp.where(lane >= base + side, lane - jnp.where(second, 0, side), high),
+    )
+    return jnp.where(near, near_low, low), jnp.where(near, near_high, high)
 
 
 def coarse_layer(own, chosen, valid, factors, columns):
@@ -549,7 +584,9 @@
 
 
 def coarse_kernel(
+    rim,
     group,
+    side,
     mine_ref,
     other_ref,
     chosen_ref,
@@ -558,9 +595,14 @@
     columns,
     group_ref,
     out_ref,
+    first_ref,
+    second_ref,
     rows_ref,
 ):
-    dom = lax.axis_index("dom")
+    region, dom = lax.axis_index("region"), lax.axis_index("dom")
+    facts = known_facts(group, rim, dom, mine_ref, other_ref)
+    asked = asked_columns(rim, side, region, dom, facts)
+    asked = jnp.concatenate(asked, axis=1) - region * group
     total = mine_ref[0:group, :] + other_ref[0:group, :]
     weight = [
         mine_ref[group + 8 * b : group + 8 * b + 1, :]
@@ -573,6 +615,9 @@
     own = coarse_layer(own, chosen, valid, factors.at[0], columns.at[0])
     own = coarse_layer(own, chosen, valid, factors.at[1], columns.at[1])
     group_ref[...] = own
+    answers = hot_gather(stacked_halves(own), asked)
+    first_ref[...] = answers[:, :LANES]
+    second_ref[...] = answers[:, LANES:]
     rows_ref[...] = own.T
     rows = out_ref.shape[0]
     out_ref[...] = rows_ref[pl.ds(pl.multiple_of(dom * rows, rows), rows), :]
@@ -599,6 +644,8 @@
     late_ref,
     partial_ref,
     late_index,
+    weight_ref,
+    lanes_ref,
     factors,
     columns,
 ):
@@ -615,10 +662,30 @@
         odd_mine[base : base + rim, :],
         other_ref[dom_base : dom_base + 2 * rim, :],
     ).T
-    facts = mine_ref[dom_base + 2 * rim : dom_base + 2 * rim + 8, :]
+    dom = lax.axis_index("dom")
+    facts = known_facts(group, rim, dom, mine_ref, other_ref)
+    own_facts, below, above = facts
+    lane = iota((8, LANES), 1)
+    late_facts = []
+    for core in range(2):
+        rims = jnp.where(lane < rim, below[core], above[core])
+        sides = jnp.where(lane < 4 * rim, own_facts[1 - core], own_facts[core])
+        late_facts.append(jnp.where(lane < 2 * rim, rims, sides))
+    first = dom == 0
+    mine = jnp.where(first, late_facts[0], late_facts[1])
+    theirs = jnp.where(first, late_facts[1], late_facts[0])
+    weight_ref[...] = jnp.concatenate([mine, theirs], axis=1) * 0.25
+    places = [own_facts[1 - core][2:3].astype(jnp.int32) for core in range(2)]
+    lanes = [
+        answer_lanes(rim, side, dom, core, jnp.where(core == 0, places[0], places[1]))
+        for core in (dom, 1 - dom)
+    ]
+    for row in range(2):
+        pair = jnp.concatenate([lanes[0][row], lanes[1][row]], axis=1)
+        lanes_ref[8 * row : 8 * row + 8, :] = jnp.broadcast_to(pair, (8, 2 * LANES))
     stacked = stacked_halves(coarse_mine[...])
-    local = facts[0:1].astype(jnp.int32) - region * group
-    late_ref[...] = outer + (facts[1:2] * 0.25) * hot_gather(stacked, local)
+    local = mine[0:1].astype(jnp.int32) - region * group
+    late_ref[...] = outer + (mine[1:2] * 0.25) * hot_gather(stacked, local)
     share = share_ref[...].astype(f32) * 0.25
     own = fine_ref[...] + share * hot_gather(stacked, parent_ref[...] - region * group)
     own_ref[...] = own
@@ -628,25 +695,12 @@
     late_places(nbr_ref, place_ref, late_index)
 
 
-def side_kernel(
-    rim, group, regions, late_in, mine_ref, other_ref, first_ref, second_ref, late_ref, back_ref
-):
-    region = lax.axis_index("region")
-    near = lax.axis_index("dom") == 0
-    base = group + 8 * (group // LANES) + 2 * rim
-    facts = jnp.concatenate([mine_ref[base : base + 8, :], other_ref[base : base + 8, :]], axis=1)
-    index = facts[0:1].astype(jnp.int32)
-
-    def home(here, distance):
-        below = (lax.rem(region // distance, 2) == 0) == here
-        return lax.rem(region + jnp.where(below, regions - distance, distance), regions)
-
-    late = None
-    for block, here in ((first_ref, True), (second_ref, False)):
-        place = jnp.where(near, home(here, 1), home(here, 2))
-        found = hot_gather(stacked_halves(block[...]), index - place * group)
-        late = found if late is None else late + found
-    late = late * (facts[1:2] * 0.25)
+def side_kernel(weight_ref, lanes_ref, late_in, first_in, second_in, late_ref, back_ref):
+    first_below = first_is_below(lax.axis_index("region"), lax.axis_index("dom") == 0)
+    first, second = first_in[...], second_in[...]
+    low, high = jnp.where(first_below, first, second), jnp.where(first_below, second, first)
+    late = block_gather(low, lanes_ref[0:1, :]) + block_gather(high, lanes_ref[8:9, :])
+    late = late * weight_ref[1:2, :]
     late_ref[...] = late_in[...] + late[:, :LANES]
     back_ref[...] = late[:, LANES:]
 
@@ -737,7 +791,6 @@
     )
     parent_row = kept(parent[None, :])
     share_row = kept(interp_share[None, :])
-    parent, interp_share = kept(parent), kept(interp_share)
     weights = (kept(edge_w), kept(node_w), kept(biases))
     i32 = jnp.int32
 
@@ -788,11 +841,11 @@
         bias_first,
     ) = kernel_call(
         functools.partial(pick_kernel, rim),
-        [far()] * 13,
+        [far()] * 11,
         [
-            (rim + 8, width),
-            (rim + 8, width),
-            (2 * rim + 8 + 2 * slots, width),
+            (rim, width),
+            (rim, width),
+            (2 * rim + 2 * slots, width),
             ((8, LANES), i32),
             fine_state.shape,
             row_shape,
@@ -805,16 +858,12 @@
         ],
         [
             pltpu.SMEM(send_rows.shape, i32),
-            pltpu.SMEM(parent.shape, i32),
-            pltpu.SMEM(interp_share.shape, i32),
             pltpu.VMEM(coarse_nbr.shape, i32),
             pltpu.VMEM(coarse_mask.shape, i32),
         ],
-        copies=13,
+        copies=11,
     )(
         send_rows,
-        parent,
-        interp_share,
         fine_state,
         coarse_nbr,
         coarse_mask,
@@ -910,7 +959,7 @@
 
     fine_one, mine = kernel_call(
         functools.partial(fine_kernel, rim, group),
-        [whole()] * 15,
+        [whole()] * 12,
         [columns_shape, (dom_rows, width)],
         flops=4 * 10**9,
     )(
@@ -926,14 +975,11 @@
         shares,
         dom_some,
         side_facts,
-        meta_even,
-        meta_odd,
-        meta_dom,
     )
     (mine,) = kernel_call(
         functools.partial(gather_side_kernel, rim, group, side, regions),
         [whole()] * 3,
-        [(dom_rows, width)],
+        [(dom_rows + 16, width)],
     )(mine, even_mine, odd_mine)
     other = dom_swap(mine)
 
@@ -949,16 +995,16 @@
         flops=10**9,
     )(mine, dom_out, meta_dom, edge_later, node_later, bias_later)
 
-    coarse_group, coarse_out = kernel_call(
-        functools.partial(coarse_kernel, group),
+    coarse_group, coarse_out, first_out, second_out = kernel_call(
+        functools.partial(coarse_kernel, rim, group, side),
         [whole()] * 6,
-        [(width, group), (own_coarse, width)],
+        [(width, group), (own_coarse, width), (width, LANES), (width, LANES)],
         [pltpu.VMEM((group, width), f32)],
     )(mine, other, group_chosen, group_valid, factors, columns)
-    first = both_swap(coarse_group, even_partner, even_two_partner)
-    second = both_swap(coarse_group, odd_partner, odd_two_partner)
-
-    own, late, partial, late_index, factors, columns = kernel_call(
+    first = both_swap(first_out, even_partner, even_two_partner)
+    second = both_swap(second_out, odd_partner, odd_two_partner)
+
+    own, late, partial, late_index, weight, lanes, factors, columns = kernel_call(
         functools.partial(between_kernel, rim, group, side),
         [whole()] * 13,
         [
@@ -966,6 +1012,8 @@
             (width, LANES),
             (slots, width, count),
             fine_slots,
+            (8, 2 * LANES),
+            ((16, 2 * LANES), i32),
             ((6, 2 * width, width), bf16),
             (4, width, LANES),
         ],
@@ -986,10 +1034,8 @@
         bias_later,
     )
     late, back = kernel_call(
-        functools.partial(side_kernel, rim, group, regions),
-        [whole()] * 5,
-        [(width, LANES), (width, LANES)],
-    )(late, mine, other, first, second)
+        side_kernel, [whole()] * 5, [(width, LANES), (width, LANES)]
+    )(weight, lanes, late, first, second)
     back = dom_swap(back)
     (fine_out,) = kernel_call(last_kernel, [whole()] * 9, [(count, width)])(
         own, late, back, partial, late_index, place, valid, factors, columns

time: 45.2 us -> 43.4 us (0.960)
  waiting for transfers between devices: 5.15 us -> 3.83 us
    ppermute x2, waiting for transfers between devices: 3.42 us -> 2 us  [both_swap(): return lax.ppermute(value, ('region', 'dom'), pairs)]
  transfers between devices with their start and end apart: 9 -> 9, of which waited for: 4 -> 4; matrix products, arithmetic and copies ran while one was open for 0% -> 0% of each run, Pallas kernels for 27% -> 28%
where the time goes in v3:
time: 43.4 us; the launch traced here: 43.3 us
  Pallas kernels  25.1 us (58%)
  starting transfers between devices  13.6 us (31%)
  waiting for transfers between devices  3.83 us (9%)
  between operations  0.73 us (2%)
    ppermute x7, starting transfers between devices, swap(): lax.ppermute(value, axis, [(source, partner(source) % count) for source i...  10.4 us
    pallas_call x1, Pallas kernels, body(): kernel_call(functools.partial(coarse_kernel, rim, group, side), [whole()]...  5.13 us
    pallas_call x1, Pallas kernels, body(): kernel_call(last_kernel, [whole()] * 9, [(count, width)])  4.32 us
    pallas_call x1, Pallas kernels, body(): kernel_call(functools.partial(before_kernel, rim, group, side, regions),...  4.05 us
    pallas_call x1, Pallas kernels, body(): kernel_call(functools.partial(fine_kernel, rim, group), [whole()] * 12, [...  3.91 us
    ppermute x2, starting transfers between devices, both_swap(): return lax.ppermute(value, ('region', 'dom'), pairs)  3.15 us
    pallas_call x1, Pallas kernels, body(): kernel_call(functools.partial(between_kernel, rim, group, side), [whole()...  2.95 us
    ppermute x2, waiting for transfers between devices, both_swap(): return lax.ppermute(value, ('region', 'dom'), pairs)  2 us
  transfers between devices with their start and end apart: 9, of which 4 were waited for; matrix products, arithmetic and copies ran while one was open for 0% of the time, Pallas kernels for 28%

profile of v3, /device:TPU:0, one launch (start us, length us, event | category | flops | bytes accessed | tf_op | source)
XLA Modules:
  0.0 43.3 jit_solution(8335614086946738077)
XLA Ops:
  0.6 1.3 %shard_map.122 = (f32[16,128]{1,0:T(8,128)S(1)}, f32[16,128]{1,0:T(8,128)S(1)}, f32[64,128]{1,0:T(8,128)S(1)}, s32[8,128]{1,0:T(8,128)S(1)}, f32[512,128]{1,0:T(...) custom-call(s32[4,16]{1,0:T(4,128)} %send_hbm.1, ...), custom_call_target="tpu_custom_call" | custom-call | bytes 4194304 | tf_op jit(solution)/shard_map/pallas_call | solution.py:842
  1.9 0.5 %collective-permute-start.2 = (f32[64,128]{1,0:T(8,128)S(1)}, f32[64,128]{1,0:T(8,128)S(1)}, u32[]{:S(2)}, u32[]{:S(2)}) collective-permute-start(f32[64,128]{1,0:T(8,128)S(1)} %get-tuple-element.77.sent_dom), channel_id=1, source_target_pairs={{0,1},{1,0},{2,3},{3,2},{4,5},{5,4},{6,7},{7,6},{8,9},{9,8},{10,11... | collective-permute-start | bytes 98312 | tf_op jit(solution)/shard_map/ppermute | solution.py:764
  2.4 6.6 %collective-permute-start = (f32[16,128]{1,0:T(8,128)S(1)}, f32[16,128]{1,0:T(8,128)S(1)}, u32[]{:S(2)}, u32[]{:S(2)}) collective-permute-start(f32[16,128]{1,0:T(8,128)S(1)} %get-tuple-element.75), channel_id=1, source_target_pairs={{0,30},{2,4},{4,2},{6,8},{8,6},{10,12},{12,10},{14,16},{16,14},{18... | collective-permute-start | bytes 24584 | tf_op jit(solution)/shard_map/ppermute | solution.py:764
  9.0 0.0 collective-permute-start.1
  9.0 4.1 %shard_map.123 = (f32[128,512]{1,0:T(8,128)S(1)}, f32[128,512]{1,0:T(8,128)S(1)}, f32[16,128,512]{2,1,0:T(8,128)S(1)}, f32[16,512]{1,0:T(8,128)S(1)}, bf16[6,256...) custom-call(f32[512,128]{1,0:T(8,128)S(1)} %get-tuple-element.54.sta, ...), custom_call_target="tpu_custom_call" | custom-call | flops 4000000000 | bytes 4194304 | tf_op jit(solution)/shard_map/pallas_call | solution.py:898
  13.0 0.0 collective-permute-done.refs_8_
  13.0 0.0 collective-permute-done.1.refs_9_
  13.1 0.0 collective-permute-done.2.refs_10_.meta_dom
  13.1 1.8 %shard_map.124 = (f32[64,128]{1,0:T(8,128)S(1)}, f32[64,128]{1,0:T(8,128)S(1)}, f32[32,128]{1,0:T(8,128)S(1)}, f32[128,128]{1,0:T(8,128)S(1)}) custom-call(f32[128,128]{1,0:T(8,128)S(1)} %get-tuple-element.69.refs_0_, f32[128,128]{1,0:T(8,128)S(1)} %get-tuple-element.70.refs_1_, f32[16,128,128]{2,1,0:T(8,128)S(1)} %get-tuple-element.71.refs_2_, ...), custom_call_target="tpu_custom_call" | custom-call | bytes 4194304 | tf_op jit(solution)/shard_map/pallas_call | solution.py:940
  14.9 3.2 %collective-permute-start.3 = (f32[64,128]{1,0:T(8,128)S(1)}, f32[64,128]{1,0:T(8,128)S(1)}, u32[]{:S(2)}, u32[]{:S(2)}) collective-permute-start(f32[64,128]{1,0:T(8,128)S(1)} %get-tuple-element.81), channel_id=1, source_target_pairs={{0,30},{2,4},{4,2},{6,8},{8,6},{10,12},{12,10},{14,16},{16,14},{18... | collective-permute-start | bytes 98312 | tf_op jit(solution)/shard_map/ppermute | solution.py:764
  18.1 0.0 collective-permute-start.4
  18.1 3.9 %shard_map.125 = (f32[128,512]{1,0:T(8,128)S(1)}, f32[312,128]{1,0:T(8,128)S(1)}) custom-call(f32[128,512]{1,0:T(8,128)S(1)} %get-tuple-element.63.own_ref, f32[128,512]{1,0:T(8,128)S(1)} %get-tuple-element.64.node_term_ref, f32[16,128,512]{2,1,0:T(8,128)S(1)} %get-tuple-element.65.partial_ref, s32[16,512]{1,0:T(8,128)S(1)} %get-tuple-element.58.nbr_ref, ...), custom_call_target="tpu_custom_call" | custom-call | flops 4000000000 | bytes 4194304 | tf_op jit(solution)/shard_map/pallas_call | solution.py:960
  22.0 0.4 %collective-permute-done.3.even_mine = f32[64,128]{1,0:T(8,128)S(1)} collective-permute-done((f32[64,128]{1,0:T(8,128)S(1)}, f32[64,128]{1,0:T(8,128)S(1)}, u32[]{:S(2)}, u32[]{:S(2)}) %collective-permute-start.3) | collective-permute-done | bytes 32800 | tf_op jit(solution)/shard_map/ppermute | solution.py:764
  22.5 0.0 collective-permute-done.4.odd_mine
  22.5 0.3 shard_map.126.token_ref.mine_ref
  22.8 0.1 collective-permute-start.5
  22.8 1.3 %shard_map.127 = (bf16[2,6,256,128]{3,2,1,0:T(8,128)(2,1)S(1)}, f32[2,4,128,128]{3,2,1,0:T(8,128)S(1)}, bf16[16,256,256]{2,1,0:T(8,128)(2,1)S(1)}, f32[16,256]{1,0:T(8,128)S(1)}) custom-call(f32[328,128]{1,0:T(8,128)S(1)} %shard_map.126.token_ref.mine_ref, f32[64,128]{1,0:T(8,128)S(1)} %get-tuple-element.77.sent_dom, ...), custom_call_target="tpu_custom_call" | custom-call | flops 1000000000 | bytes 4194304 | tf_op jit(solution)/shard_map/pallas_call | solution.py:986
  24.1 0.1 collective-permute-done.5.other_ref
  24.2 5.1 %shard_map.128 = (f32[128,256]{1,0:T(8,128)S(1)}, f32[128,128]{1,0:T(8,128)}, f32[128,128]{1,0:T(8,128)S(1)}, f32[128,128]{1,0:T(8,128)S(1)}) custom-call(f32[328,128]{1,0:T(8,128)S(1)} %shard_map.126.token_ref.mine_ref, f32[328,128]{1,0:T(8,128)S(1)} %collective-permute-done.5.other_ref, bf16[16,256,256]{2,1,0:T(8,128)(2,1)S(1)} %get-tuple-element.87.chosen_ref, ...), custom_call_target="tpu_custom_call" | custom-call | bytes 4194304 | tf_op jit(solution)/shard_map/pallas_call | solution.py:998
  29.4 3.1 %collective-permute-start.6 = (f32[128,128]{1,0:T(8,128)S(1)}, f32[128,128]{1,0:T(8,128)S(1)}, u32[]{:S(2)}, u32[]{:S(2)}) collective-permute-start(f32[128,128]{1,0:T(8,128)S(1)} %get-tuple-element.97), channel_id=1, source_target_pairs={{0,30},{1,29},{2,4},{3,31},{4,2},{5,9},{6,8},{7,11},{8,6},{9,5},{1... | collective-permute-start | bytes 196616 | tf_op jit(solution)/shard_map/ppermute | solution.py:824
  32.5 0.0 collective-permute-start.7
  32.5 3.0 %shard_map.129 = (f32[128,512]{1,0:T(8,128)S(1)}, f32[128,128]{1,0:T(8,128)S(1)}, f32[16,128,512]{2,1,0:T(8,128)S(1)}, s32[16,512]{1,0:T(8,128)S(1)}, f32[8,256]...) custom-call(f32[128,512]{1,0:T(8,128)S(1)} %get-tuple-element.80.fine_ref, ...), custom_call_target="tpu_custom_call" | custom-call | flops 4000000000 | bytes 4194304 | tf_op jit(solution)/shard_map/pallas_call | solution.py:1007
  35.5 2.0 %collective-permute-done.6.first_in = f32[128,128]{1,0:T(8,128)S(1)} collective-permute-done((f32[128,128]{1,0:T(8,128)S(1)}, f32[128,128]{1,0:T(8,128)S(1)}, u32[]{:S(2)}, u32[]{:S(2)}) %collective-permute-start.6) | collective-permute-done | bytes 65568 | tf_op jit(solution)/shard_map/ppermute | solution.py:824
  37.5 0.0 collective-permute-done.7.second_in
  37.5 0.2 shard_map.130
  37.6 0.1 collective-permute-start.8
  37.7 1.2 %collective-permute-done.8.back_ref = f32[128,128]{1,0:T(8,128)S(1)} collective-permute-done((f32[128,128]{1,0:T(8,128)S(1)}, f32[128,128]{1,0:T(8,128)S(1)}, u32[]{:S(2)}, u32[]{:S(2)}) %collective-permute-start.8) | collective-permute-done | bytes 65568 | tf_op jit(solution)/shard_map/ppermute | solution.py:764
  38.9 4.3 %shard_map.131 = f32[512,128]{1,0:T(8,128)} custom-call(f32[128,512]{1,0:T(8,128)S(1)} %get-tuple-element.93.own_ref, f32[128,128]{1,0:T(8,128)S(1)} %get-tuple-element.99.late_in, f32[128,128]{1,0:T(8,128)S(1)} %collective-permute-done.8.back_ref, f32[16,128,512]{2,1,0:T(8,128)S(1)} %get-tuple-element.101.partial_ref, ...), custom_call_target="tpu_custom_call" | custom-call | bytes 4194304 | tf_op jit(solution)/shard_map/pallas_call | solution.py:1040
Async XLA Ops:
  1.9 11.2 %collective-permute-start.2 = (f32[64,128]{1,0:T(8,128)S(1)}, f32[64,128]{1,0:T(8,128)S(1)}, u32[]{:S(2)}, u32[]{:S(2)}) collective-permute-start(f32[64,128]{1,0:T(8,128)S(1)} %get-tuple-element.77.sent_dom), channel_id=1, source_target_pairs={{0,1},{1,0},{2,3},{3,2},{4,5},{5,4},{6,7},{7,6},{8,9},{9,8},{10,11... | collective-permute-start | bytes 98312 | tf_op jit(solution)/shard_map/ppermute | solution.py:764
  2.4 10.6 %collective-permute-start = (f32[16,128]{1,0:T(8,128)S(1)}, f32[16,128]{1,0:T(8,128)S(1)}, u32[]{:S(2)}, u32[]{:S(2)}) collective-permute-start(f32[16,128]{1,0:T(8,128)S(1)} %get-tuple-element.75), channel_id=1, source_target_pairs={{0,30},{2,4},{4,2},{6,8},{8,6},{10,12},{12,10},{14,16},{16,14},{18... | collective-permute-start | bytes 24584 | tf_op jit(solution)/shard_map/ppermute | solution.py:764
  9.0 4.1 %collective-permute-start.1 = (f32[16,128]{1,0:T(8,128)S(1)}, f32[16,128]{1,0:T(8,128)S(1)}, u32[]{:S(2)}, u32[]{:S(2)}) collective-permute-start(f32[16,128]{1,0:T(8,128)S(1)} %get-tuple-element.76), channel_id=1, source_target_pairs={{0,2},{2,0},{4,6},{6,4},{8,10},{10,8},{12,14},{14,12},{16,18},{18,... | collective-permute-start | bytes 24584 | tf_op jit(solution)/shard_map/ppermute | solution.py:764
  14.9 7.6 %collective-permute-start.3 = (f32[64,128]{1,0:T(8,128)S(1)}, f32[64,128]{1,0:T(8,128)S(1)}, u32[]{:S(2)}, u32[]{:S(2)}) collective-permute-start(f32[64,128]{1,0:T(8,128)S(1)} %get-tuple-element.81), channel_id=1, source_target_pairs={{0,30},{2,4},{4,2},{6,8},{8,6},{10,12},{12,10},{14,16},{16,14},{18... | collective-permute-start | bytes 98312 | tf_op jit(solution)/shard_map/ppermute | solution.py:764
  18.1 4.4 %collective-permute-start.4 = (f32[64,128]{1,0:T(8,128)S(1)}, f32[64,128]{1,0:T(8,128)S(1)}, u32[]{:S(2)}, u32[]{:S(2)}) collective-permute-start(f32[64,128]{1,0:T(8,128)S(1)} %get-tuple-element.82), channel_id=1, source_target_pairs={{0,2},{2,0},{4,6},{6,4},{8,10},{10,8},{12,14},{14,12},{16,18},{18,... | collective-permute-start | bytes 98312 | tf_op jit(solution)/shard_map/ppermute | solution.py:764
  22.8 1.5 %collective-permute-start.5 = (f32[328,128]{1,0:T(8,128)S(1)}, f32[328,128]{1,0:T(8,128)S(1)}, u32[]{:S(2)}, u32[]{:S(2)}) collective-permute-start(f32[328,128]{1,0:T(8,128)S(1)} %shard_map.126.token_ref.mine_ref), channel_id=1, source_target_pairs={{0,1},{1,0},{2,3},{3,2},{4,5},{5,4},{6,7},{7,6},{8,9},{9,8},{10,11... | collective-permute-start | bytes 503816 | tf_op jit(solution)/shard_map/ppermute | solution.py:764
  29.4 8.1 %collective-permute-start.6 = (f32[128,128]{1,0:T(8,128)S(1)}, f32[128,128]{1,0:T(8,128)S(1)}, u32[]{:S(2)}, u32[]{:S(2)}) collective-permute-start(f32[128,128]{1,0:T(8,128)S(1)} %get-tuple-element.97), channel_id=1, source_target_pairs={{0,30},{1,29},{2,4},{3,31},{4,2},{5,9},{6,8},{7,11},{8,6},{9,5},{1... | collective-permute-start | bytes 196616 | tf_op jit(solution)/shard_map/ppermute | solution.py:824
  32.5 5.0 %collective-permute-start.7 = (f32[128,128]{1,0:T(8,128)S(1)}, f32[128,128]{1,0:T(8,128)S(1)}, u32[]{:S(2)}, u32[]{:S(2)}) collective-permute-start(f32[128,128]{1,0:T(8,128)S(1)} %get-tuple-element.98), channel_id=1, source_target_pairs={{0,2},{1,5},{2,0},{3,7},{4,6},{5,1},{6,4},{7,3},{8,10},{9,13},{10,... | collective-permute-start | bytes 196616 | tf_op jit(solution)/shard_map/ppermute | solution.py:824
  37.6 1.3 %collective-permute-start.8 = (f32[128,128]{1,0:T(8,128)S(1)}, f32[128,128]{1,0:T(8,128)S(1)}, u32[]{:S(2)}, u32[]{:S(2)}) collective-permute-start(f32[128,128]{1,0:T(8,128)S(1)} %get-tuple-element.100), channel_id=1, source_target_pairs={{0,1},{1,0},{2,3},{3,2},{4,5},{5,4},{6,7},{7,6},{8,9},{9,8},{10,11... | collective-permute-start | bytes 196616 | tf_op jit(solution)/shard_map/ppermute | solution.py:764

commit v4 on v3

--- a/solution.py
+++ b/solution.py
@@ -11,6 +11,7 @@
 f32 = jnp.float32
 bf16 = jnp.bfloat16
 LANES = 128
+PARTS = 2
 WIDE = 512
 VMEM_BYTES = 32 * 2**20
 
@@ -430,6 +431,7 @@
     factors,
     columns,
     chosen_ref,
+    nbr_ref,
     valid_ref,
 ):
     slots, group = valid_ref.shape
@@ -439,8 +441,10 @@
         [jnp.where(first, sent, received), jnp.where(first, received, sent)], axis=1
     )
     valid_ref[...] = tiles[slots:]
+    nbr = tiles[:slots].astype(jnp.int32)
+    nbr_ref[...] = nbr
     for slot in range(slots):
-        chosen_ref[slot] = hot(group, tiles[slot : slot + 1].astype(jnp.int32)).astype(bf16)
+        chosen_ref[slot] = hot(group, nbr[slot : slot + 1]).astype(bf16)
     for layer in range(factors.shape[0]):
         prepare(
             edge_ref.at[layer],
@@ -521,59 +525,78 @@
     return jnp.take_along_axis(rows, index, axis=1)
 
 
-def first_is_below(region, near):
-    return lax.rem(jnp.where(near, region, region // 2), 2) == 0
+def sides_below(region, dom):
+    first = dom == 0
+    near = (lax.rem(region, 2) == 0) == first
+    far = (lax.rem(region // 2, 2) == 0) != first
+    return near, far
 
 
 def asked_columns(rim, side, region, dom, facts):
     own, below, above = facts
-    near = dom == 0
+    near_below, far_below = sides_below(region, dom)
     lane = iota((8, LANES), 1)
     base = 4 * rim
-    up = [jnp.where(near, mine, theirs) for mine, theirs in zip(own, above)]
-    down = [jnp.where(near, mine, theirs) for mine, theirs in zip(own, below)]
-    up_rims = jnp.where(lane < rim, up[0], moved(up[1], rim))
-    down_rims = jnp.where(lane < rim, moved(down[0], -rim), down[1])
-    up_sides = jnp.where(lane < base + side, above[0], moved(above[1], side))
-    down_sides = jnp.where(lane < base + side, moved(below[0], -side), below[1])
-    asked = []
-    for rims, sides in ((up_rims, up_sides), (down_rims, down_sides)):
-        sides = jnp.where((lane >= base) & near, sides, -1.0)
-        asked.append(jnp.where(lane < 2 * rim, rims, sides)[0:1].astype(jnp.int32))
-    first_below = first_is_below(region, near)
-    up, down = asked
-    return jnp.where(first_below, down, up), jnp.where(first_below, up, down)
-
-
-def answer_lanes(rim, side, dom, core, place):
+    rims = jnp.where(
+        near_below,
+        jnp.where(lane < rim, moved(own[0], -rim), own[1]),
+        jnp.where(lane < rim, own[0], moved(own[1], rim)),
+    )
+    beyond = jnp.where(
+        far_below,
+        jnp.where(lane < 3 * rim, moved(below[0], rim), moved(below[1], 2 * rim)),
+        jnp.where(lane < 3 * rim, moved(above[0], 2 * rim), moved(above[1], 3 * rim)),
+    )
+    sides = jnp.where(
+        near_below,
+        jnp.where(lane < base + side, moved(below[0], -side), below[1]),
+        jnp.where(lane < base + side, above[0], moved(above[1], side)),
+    )
+    asked = jnp.where(lane < 2 * rim, rims, jnp.where(lane < base, beyond, sides))
+    return asked[0:1].astype(jnp.int32)
+
+
+def answer_lanes(rim, side, region, dom, core, place):
+    near_below, far_below = sides_below(region, dom)
     lane = iota((1, LANES), 1)
     base = 4 * rim
-    near = dom == 0
     second = core == 1
+    skip = jnp.where(second, rim, 0)
     from_dom = (lane >= 2 * rim) & (lane < base)
+    below_rim = lane < rim
+    above_rim = (lane >= rim) & (lane < 2 * rim)
     low_place = (place >= base) & (place < base + side)
-    low = jnp.where(lane < rim, lane + jnp.where(second, rim, 0), -1)
-    high = jnp.where((lane >= rim) & (lane < 2 * rim), lane - jnp.where(second, 0, rim), -1)
-    near_low = jnp.where(
+    low = jnp.where(
         from_dom,
         jnp.where(low_place, place + jnp.where(second, 0, side), -1),
         jnp.where(
-            (lane >= base) & (lane < base + side), lane + jnp.where(second, side, 0), low
+            (lane >= base) & (lane < base + side),
+            lane + jnp.where(second, side, 0),
+            jnp.where(below_rim, lane + skip, -1),
         ),
     )
-    near_high = jnp.where(
+    high = jnp.where(
         from_dom,
         jnp.where(place >= base + side, place - jnp.where(second, side, 0), -1),
-        jnp.where(lane >= base + side, lane - jnp.where(second, 0, side), high),
-    )
-    return jnp.where(near, near_low, low), jnp.where(near, near_high, high)
-
-
-def coarse_layer(own, chosen, valid, factors, columns):
+        jnp.where(
+            lane >= base + side,
+            lane - jnp.where(second, 0, side),
+            jnp.where(above_rim, lane - rim + skip, -1),
+        ),
+    )
+    far_low = jnp.where(below_rim, lane + 2 * rim + skip, -1)
+    far_high = jnp.where(above_rim, lane + rim + skip, -1)
+    return jnp.where(near_below, low, high), jnp.where(far_below, far_low, far_high)
+
+
+def coarse_sources(own, factors):
+    return stacked_halves(times(factors[1], own))
+
+
+def coarse_layer(own, sources, chosen, valid, factors, columns):
     (term,) = own_products(factors, columns, (0,), own)
     (node_term,) = own_products(factors, columns, (3,), own)
-    stacked = stacked_halves(times(factors[1], own))
-    found = jnp.dot(stacked, chosen, preferred_element_type=f32)
+    found = jnp.dot(sources, chosen, preferred_element_type=f32)
     count = own.shape[1]
 
     def before(slot):
@@ -581,6 +604,10 @@
 
     gathered = edge_sum(before, valid, factors[2], columns[1])
     return node_step(own, node_term, gathered, factors, columns)
+
+
+def all_slots(chosen_ref):
+    return jnp.concatenate([chosen_ref[slot] for slot in range(chosen_ref.shape[0])], axis=1)
 
 
 def coarse_kernel(
@@ -590,19 +617,20 @@
     mine_ref,
     other_ref,
     chosen_ref,
+    nbr_ref,
     valid_ref,
     factors,
     columns,
-    group_ref,
-    out_ref,
-    first_ref,
-    second_ref,
-    rows_ref,
+    middle_ref,
+    sources_ref,
+    answer_ref,
 ):
     region, dom = lax.axis_index("region"), lax.axis_index("dom")
     facts = known_facts(group, rim, dom, mine_ref, other_ref)
-    asked = asked_columns(rim, side, region, dom, facts)
-    asked = jnp.concatenate(asked, axis=1) - region * group
+    asked = asked_columns(rim, side, region, dom, facts) - region * group
+    inside = (asked >= 0) & (asked < group)
+    nbr = pick_columns(nbr_ref[...], asked)
+    valid = pick_columns(valid_ref[...], asked)
     total = mine_ref[0:group, :] + other_ref[0:group, :]
     weight = [
         mine_ref[group + 8 * b : group + 8 * b + 1, :]
@@ -610,17 +638,17 @@
         for b in range(group // LANES)
     ]
     own = total.T / jnp.maximum(jnp.concatenate(weight, axis=1), 1.0)
-    chosen = jnp.concatenate([chosen_ref[slot] for slot in range(chosen_ref.shape[0])], axis=1)
-    valid = valid_ref[...]
-    own = coarse_layer(own, chosen, valid, factors.at[0], columns.at[0])
-    own = coarse_layer(own, chosen, valid, factors.at[1], columns.at[1])
-    group_ref[...] = own
-    answers = hot_gather(stacked_halves(own), asked)
-    first_ref[...] = answers[:, :LANES]
-    second_ref[...] = answers[:, LANES:]
-    rows_ref[...] = own.T
-    rows = out_ref.shape[0]
-    out_ref[...] = rows_ref[pl.ds(pl.multiple_of(dom * rows, rows), rows), :]
+    sources = coarse_sources(own, factors.at[0])
+    own = coarse_layer(
+        own, sources, all_slots(chosen_ref), valid_ref[...], factors.at[0], columns.at[0]
+    )
+    middle_ref[...] = own
+    sources = coarse_sources(own, factors.at[1])
+    sources_ref[...] = sources
+    chosen = hot(group, wide_row(nbr, 0, nbr.shape[0])).astype(bf16)
+    some = pick_columns(own, asked)
+    some = coarse_layer(some, sources, chosen, valid, factors.at[1], columns.at[1])
+    answer_ref[...] = jnp.where(inside, some, 0.0)
 
 
 def between_kernel(
@@ -632,25 +660,37 @@
     odd_mine,
     mine_ref,
     other_ref,
-    coarse_mine,
+    middle_ref,
+    sources_ref,
+    chosen_ref,
+    valid_ref,
+    factors,
+    columns,
     nbr_ref,
-    place_ref,
     parent_ref,
     share_ref,
     edge_ref,
-    node_ref,
-    bias_ref,
+    out_ref,
     own_ref,
     late_ref,
     partial_ref,
-    late_index,
     weight_ref,
     lanes_ref,
-    factors,
-    columns,
+    rows_ref,
+    semaphores,
 ):
-    last = edge_ref.shape[0] - 1
-    prepare(edge_ref.at[last], node_ref.at[last], bias_ref.at[last], factors, columns)
+    coarse = coarse_layer(
+        middle_ref[...],
+        sources_ref[...],
+        all_slots(chosen_ref),
+        valid_ref[...],
+        factors.at[1],
+        columns.at[1],
+    )
+    rows_ref[...] = coarse.T
+    rows = out_ref.shape[0]
+    start = pl.multiple_of(lax.axis_index("dom") * rows, rows)
+    copies = fetch(((rows_ref.at[pl.ds(start, rows)], out_ref),), semaphores)
     region = lax.axis_index("region")
     even = lax.rem(region, 2) == 0
     base = side + 8
@@ -677,29 +717,40 @@
     weight_ref[...] = jnp.concatenate([mine, theirs], axis=1) * 0.25
     places = [own_facts[1 - core][2:3].astype(jnp.int32) for core in range(2)]
     lanes = [
-        answer_lanes(rim, side, dom, core, jnp.where(core == 0, places[0], places[1]))
+        answer_lanes(
+            rim, side, region, dom, core, jnp.where(core == 0, places[0], places[1])
+        )
         for core in (dom, 1 - dom)
     ]
     for row in range(2):
         pair = jnp.concatenate([lanes[0][row], lanes[1][row]], axis=1)
         lanes_ref[8 * row : 8 * row + 8, :] = jnp.broadcast_to(pair, (8, 2 * LANES))
-    stacked = stacked_halves(coarse_mine[...])
+    stacked = stacked_halves(coarse)
     local = mine[0:1].astype(jnp.int32) - region * group
     late_ref[...] = outer + (mine[1:2] * 0.25) * hot_gather(stacked, local)
     share = share_ref[...].astype(f32) * 0.25
     own = fine_ref[...] + share * hot_gather(stacked, parent_ref[...] - region * group)
     own_ref[...] = own
-    stacked = stacked_halves(times(factors[1], own))
+    stacked = stacked_halves(times(halves(edge_ref[edge_ref.shape[0] - 1, 1]), own))
     for slot in range(nbr_ref.shape[0]):
         partial_ref[slot] = hot_gather(stacked, nbr_ref[slot : slot + 1, :])
+    for copy in copies:
+        copy.wait()
+
+
+def prepare_last_kernel(
+    token_ref, nbr_ref, place_ref, edge_ref, node_ref, bias_ref, late_index, factors, columns
+):
+    last = edge_ref.shape[0] - 1
+    prepare(edge_ref.at[last], node_ref.at[last], bias_ref.at[last], factors, columns)
     late_places(nbr_ref, place_ref, late_index)
 
 
 def side_kernel(weight_ref, lanes_ref, late_in, first_in, second_in, late_ref, back_ref):
-    first_below = first_is_below(lax.axis_index("region"), lax.axis_index("dom") == 0)
-    first, second = first_in[...], second_in[...]
-    low, high = jnp.where(first_below, first, second), jnp.where(first_below, second, first)
-    late = block_gather(low, lanes_ref[0:1, :]) + block_gather(high, lanes_ref[8:9, :])
+    first = lax.axis_index("dom") == 0
+    near = jnp.where(first, first_in[...], second_in[...])
+    far_rows = jnp.where(first, second_in[...], first_in[...])
+    late = block_gather(near, lanes_ref[0:1, :]) + block_gather(far_rows, lanes_ref[8:9, :])
     late = late * weight_ref[1:2, :]
     late_ref[...] = late_in[...] + late[:, :LANES]
     back_ref[...] = late[:, LANES:]
@@ -716,6 +767,8 @@
     factors,
     columns,
     out_ref,
+    rows_ref,
+    semaphores,
 ):
     late = late_in[...] + back_ref[...]
     own = own_ref[...] + block_gather(late, place_ref[0:1, :])
@@ -726,7 +779,16 @@
         return partial_ref[slot] + block_gather(block, late_index[slot : slot + 1, :]) + term
 
     gathered = edge_sum(before, valid_ref, factors[2], columns[1])
-    out_ref[...] = node_step(own, node_term, gathered, factors, columns).T
+    copies = []
+    for place in range(PARTS):
+        size = own.shape[1] // PARTS
+        part = slice(place * size, (place + 1) * size)
+        result = node_step(own[:, part], node_term[:, part], gathered[:, part], factors, columns)
+        rows_ref[part, :] = result.T
+        pair = (rows_ref.at[part], out_ref.at[part])
+        copies += fetch((pair,), semaphores.at[pl.ds(place, 1)])
+    for copy in copies:
+        copy.wait()
 
 
 def whole():
@@ -745,12 +807,12 @@
     return pl.BlockSpec(memory_space=pltpu.SMEM)
 
 
-def kernel_call(body, in_specs, outs, scratch=(), copies=0, flops=0):
+def kernel_call(body, in_specs, outs, scratch=(), copies=0, flops=0, sent=()):
     outs = [(out, f32) if isinstance(out[0], int) else out for out in outs]
     return pl.pallas_call(
         body,
         in_specs=in_specs,
-        out_specs=tuple(whole() for _ in outs),
+        out_specs=tuple(far() if place in sent else whole() for place in range(len(outs))),
         out_shape=tuple(jax.ShapeDtypeStruct(shape, kind) for shape, kind in outs),
         scratch_shapes=list(scratch) + [pltpu.SemaphoreType.DMA((copies,))] * (copies > 0),
         compiler_params=pltpu.CompilerParams(vmem_limit_bytes=VMEM_BYTES),
@@ -815,11 +877,11 @@
     def dom_swap(value):
         return swap(value, "dom", lambda d: d + 1, domains)
 
-    def both_swap(value, near, distant):
+    def both_swap(value, for_first, for_second):
         pairs = []
         for r in range(regions):
             for d in range(domains):
-                target = (near(r) if d == 0 else distant(r)) % regions
+                target = (for_first(r) if d == 0 else for_second(r)) % regions
                 pairs.append((r * domains + d, target * domains + d))
         return lax.ppermute(value, ("region", "dom"), pairs)
 
@@ -983,62 +1045,78 @@
     )(mine, even_mine, odd_mine)
     other = dom_swap(mine)
 
-    factors, columns, group_chosen, group_valid = kernel_call(
+    factors, columns, group_chosen, group_nbr, group_valid = kernel_call(
         functools.partial(prepare_kernel, rim),
         [whole()] * 6,
         [
             ((later - 1, 6, 2 * width, width), bf16),
             (later - 1, 4, width, LANES),
             ((slots, group, group), bf16),
+            ((slots, group), i32),
             (slots, group),
         ],
         flops=10**9,
     )(mine, dom_out, meta_dom, edge_later, node_later, bias_later)
 
-    coarse_group, coarse_out, first_out, second_out = kernel_call(
+    middle, sources, answers = kernel_call(
         functools.partial(coarse_kernel, rim, group, side),
-        [whole()] * 6,
-        [(width, group), (own_coarse, width), (width, LANES), (width, LANES)],
-        [pltpu.VMEM((group, width), f32)],
-    )(mine, other, group_chosen, group_valid, factors, columns)
-    first = both_swap(first_out, even_partner, even_two_partner)
-    second = both_swap(second_out, odd_partner, odd_two_partner)
-
-    own, late, partial, late_index, weight, lanes, factors, columns = kernel_call(
+        [whole()] * 7,
+        [(width, group), ((2 * width, group), bf16), (width, LANES)],
+    )(mine, other, group_chosen, group_nbr, group_valid, factors, columns)
+    first = both_swap(answers, even_partner, even_two_partner)
+    second = both_swap(answers, odd_two_partner, odd_partner)
+
+    coarse_out, own, late, partial, weight, lanes = kernel_call(
         functools.partial(between_kernel, rim, group, side),
-        [whole()] * 13,
+        [whole()] * 15,
         [
+            (own_coarse, width),
             columns_shape,
             (width, LANES),
             (slots, width, count),
-            fine_slots,
             (8, 2 * LANES),
             ((16, 2 * LANES), i32),
-            ((6, 2 * width, width), bf16),
-            (4, width, LANES),
         ],
-        flops=4 * 10**9,
+        [pltpu.VMEM((group, width), f32)],
+        copies=1,
+        flops=8 * 10**9,
+        sent=(0,),
     )(
         fine_one,
         even_mine,
         odd_mine,
         mine,
         other,
-        coarse_group,
+        middle,
+        sources,
+        group_chosen,
+        group_valid,
+        factors,
+        columns,
         nbr,
-        place,
         parents,
         shares,
         edge_later,
-        node_later,
-        bias_later,
     )
     late, back = kernel_call(
         side_kernel, [whole()] * 5, [(width, LANES), (width, LANES)]
     )(weight, lanes, late, first, second)
-    back = dom_swap(back)
-    (fine_out,) = kernel_call(last_kernel, [whole()] * 9, [(count, width)])(
-        own, late, back, partial, late_index, place, valid, factors, columns
+    back_here = dom_swap(back)
+    late_index, factors, columns = kernel_call(
+        prepare_last_kernel,
+        [whole()] * 6,
+        [fine_slots, ((6, 2 * width, width), bf16), (4, width, LANES)],
+        flops=10**9,
+    )(back, nbr, place, edge_later, node_later, bias_later)
+    (fine_out,) = kernel_call(
+        last_kernel,
+        [whole()] * 9,
+        [(count, width)],
+        [pltpu.VMEM((count, width), f32)],
+        copies=PARTS,
+        sent=(0,),
+    )(
+        own, late, back_here, partial, late_index, place, valid, factors, columns
     )
     return (fine_out, coarse_out)
 

time: 43.4 us -> 42.9 us (0.988)
  waiting for transfers between devices: 3.83 us -> 0.98 us
  Pallas kernels: 25.1 us -> 26.8 us
    pallas_call x1, Pallas kernels: 2.95 us -> 5.32 us  [body(): kernel_call(functools.partial(between_kernel, rim, group, side), [whole()...]
    ppermute x2, waiting for transfers between devices: 2 us -> 0.01 us  [both_swap(): return lax.ppermute(value, ('region', 'dom'), pairs)]
    pallas_call x1, Pallas kernels: 5.13 us -> 3.94 us  [body(): kernel_call(functools.partial(coarse_kernel, rim, group, side), [whole()]...]
    ppermute x7, waiting for transfers between devices: 1.83 us -> 0.97 us  [swap(): lax.ppermute(value, axis, [(source, partner(source) % count) for source i...]
    pallas_call x1 -> x2, Pallas kernels: 4.32 us -> 4.86 us  [the longest x1 4.35 us: body(): kernel_call(last_kernel, [whole()] * 9, [(count, width)], [pltpu.VMEM((co...]
  transfers between devices with their start and end apart: 9 -> 9, of which waited for: 4 -> 3; matrix products, arithmetic and copies ran while one was open for 0% -> 0% of each run, Pallas kernels for 28% -> 35%
where the time goes in v4:
time: 42.9 us; the launch traced here: 42.7 us
  Pallas kernels  26.8 us (62%)
  starting transfers between devices  14 us (33%)
  waiting for transfers between devices  0.98 us (2%)
  between operations  0.92 us (2%)
    ppermute x7, starting transfers between devices, swap(): lax.ppermute(value, axis, [(source, partner(source) % count) for source i...  10.8 us
    pallas_call x1, Pallas kernels, body(): kernel_call(functools.partial(between_kernel, rim, group, side), [whole()...  5.32 us
    pallas_call x1, Pallas kernels, body(): kernel_call(last_kernel, [whole()] * 9, [(count, width)], [pltpu.VMEM((co...  4.35 us
    pallas_call x1, Pallas kernels, body(): kernel_call(functools.partial(before_kernel, rim, group, side, regions),...  4.05 us
    pallas_call x1, Pallas kernels, body(): kernel_call(functools.partial(coarse_kernel, rim, group, side), [whole()]...  3.94 us
    pallas_call x1, Pallas kernels, body(): kernel_call(functools.partial(fine_kernel, rim, group), [whole()] * 12, [...  3.89 us
    ppermute x2, starting transfers between devices, both_swap(): return lax.ppermute(value, ('region', 'dom'), pairs)  3.23 us
    pallas_call x1, Pallas kernels, body(): kernel_call(first_body, [whole()] * 11, [(block_rows, width), (block_rows...  1.84 us
  transfers between devices with their start and end apart: 9, of which 3 were waited for; matrix products, arithmetic and copies ran while one was open for 0% of the time, Pallas kernels for 35%

profile of v4, /device:TPU:0, one launch (start us, length us, event | category | flops | bytes accessed | tf_op | source)
XLA Modules:
  0.0 42.7 jit_solution(2414854877219937004)
XLA Ops:
  0.6 1.3 %shard_map.122 = (f32[16,128]{1,0:T(8,128)S(1)}, f32[16,128]{1,0:T(8,128)S(1)}, f32[64,128]{1,0:T(8,128)S(1)}, s32[8,128]{1,0:T(8,128)S(1)}, f32[512,128]{1,0:T(...) custom-call(s32[4,16]{1,0:T(4,128)} %send_hbm.1, ...), custom_call_target="tpu_custom_call" | custom-call | bytes 4194304 | tf_op jit(solution)/shard_map/pallas_call | solution.py:904
  1.9 0.5 %collective-permute-start.2 = (f32[64,128]{1,0:T(8,128)S(1)}, f32[64,128]{1,0:T(8,128)S(1)}, u32[]{:S(2)}, u32[]{:S(2)}) collective-permute-start(f32[64,128]{1,0:T(8,128)S(1)} %get-tuple-element.78.sent_dom), channel_id=1, source_target_pairs={{0,1},{1,0},{2,3},{3,2},{4,5},{5,4},{6,7},{7,6},{8,9},{9,8},{10,11... | collective-permute-start | bytes 98312 | tf_op jit(solution)/shard_map/ppermute | solution.py:826
  2.4 6.6 %collective-permute-start = (f32[16,128]{1,0:T(8,128)S(1)}, f32[16,128]{1,0:T(8,128)S(1)}, u32[]{:S(2)}, u32[]{:S(2)}) collective-permute-start(f32[16,128]{1,0:T(8,128)S(1)} %get-tuple-element.76), channel_id=1, source_target_pairs={{0,30},{2,4},{4,2},{6,8},{8,6},{10,12},{12,10},{14,16},{16,14},{18... | collective-permute-start | bytes 24584 | tf_op jit(solution)/shard_map/ppermute | solution.py:826
  9.0 0.0 collective-permute-start.1
  9.0 4.0 %shard_map.123 = (f32[128,512]{1,0:T(8,128)S(1)}, f32[128,512]{1,0:T(8,128)S(1)}, f32[16,128,512]{2,1,0:T(8,128)S(1)}, f32[16,512]{1,0:T(8,128)S(1)}, bf16[6,256...) custom-call(f32[512,128]{1,0:T(8,128)S(1)} %get-tuple-element.55.sta, ...), custom_call_target="tpu_custom_call" | custom-call | flops 4000000000 | bytes 4194304 | tf_op jit(solution)/shard_map/pallas_call | solution.py:960
  13.0 0.0 collective-permute-done.refs_8_
  13.0 0.0 collective-permute-done.1.refs_9_
  13.0 0.0 collective-permute-done.2.refs_10_.meta_dom
  13.1 1.8 %shard_map.124 = (f32[64,128]{1,0:T(8,128)S(1)}, f32[64,128]{1,0:T(8,128)S(1)}, f32[32,128]{1,0:T(8,128)S(1)}, f32[128,128]{1,0:T(8,128)S(1)}) custom-call(f32[128,128]{1,0:T(8,128)S(1)} %get-tuple-element.70.refs_0_, f32[128,128]{1,0:T(8,128)S(1)} %get-tuple-element.71.refs_1_, f32[16,128,128]{2,1,0:T(8,128)S(1)} %get-tuple-element.72.refs_2_, ...), custom_call_target="tpu_custom_call" | custom-call | bytes 4194304 | tf_op jit(solution)/shard_map/pallas_call | solution.py:1002
  14.9 3.2 %collective-permute-start.3 = (f32[64,128]{1,0:T(8,128)S(1)}, f32[64,128]{1,0:T(8,128)S(1)}, u32[]{:S(2)}, u32[]{:S(2)}) collective-permute-start(f32[64,128]{1,0:T(8,128)S(1)} %get-tuple-element.82), channel_id=1, source_target_pairs={{0,30},{2,4},{4,2},{6,8},{8,6},{10,12},{12,10},{14,16},{16,14},{18... | collective-permute-start | bytes 98312 | tf_op jit(solution)/shard_map/ppermute | solution.py:826
  18.1 0.0 collective-permute-start.4
  18.1 3.9 %shard_map.125 = (f32[128,512]{1,0:T(8,128)S(1)}, f32[312,128]{1,0:T(8,128)S(1)}) custom-call(f32[128,512]{1,0:T(8,128)S(1)} %get-tuple-element.64.own_ref, f32[128,512]{1,0:T(8,128)S(1)} %get-tuple-element.65.node_term_ref, f32[16,128,512]{2,1,0:T(8,128)S(1)} %get-tuple-element.66.partial_ref, s32[16,512]{1,0:T(8,128)S(1)} %get-tuple-element.59.nbr_ref, ...), custom_call_target="tpu_custom_call" | custom-call | flops 4000000000 | bytes 4194304 | tf_op jit(solution)/shard_map/pallas_call | solution.py:1022
  22.0 0.5 %collective-permute-done.3.even_mine = f32[64,128]{1,0:T(8,128)S(1)} collective-permute-done((f32[64,128]{1,0:T(8,128)S(1)}, f32[64,128]{1,0:T(8,128)S(1)}, u32[]{:S(2)}, u32[]{:S(2)}) %collective-permute-start.3) | collective-permute-done | bytes 32800 | tf_op jit(solution)/shard_map/ppermute | solution.py:826
  22.5 0.0 collective-permute-done.4.odd_mine
  22.5 0.3 shard_map.126.token_ref.mine_ref
  22.7 0.1 collective-permute-start.5
  22.8 1.3 %shard_map.127 = (bf16[2,6,256,128]{3,2,1,0:T(8,128)(2,1)S(1)}, f32[2,4,128,128]{3,2,1,0:T(8,128)S(1)}, bf16[16,256,256]{2,1,0:T(8,128)(2,1)S(1)}, s32[16,256]{1,0:T(8,128)S(1)}, f32[16,256]{1,0:T(8,128)S(1)}) custom-call(f32[328,128]{1,0:T(8,128)S(1)} %shard_map.126.token_ref.mine_ref, f32[64,128]{1,0:T(8,128)S(1)} %get-tuple-element.78.sent_dom, ...), custom_call_target="tpu_custom_call" | custom-call | flops 1000000000 | bytes 4194304 | tf_op jit(solution)/shard_map/pallas_call | solution.py:1048
  24.1 0.1 collective-permute-done.5.other_ref
  24.2 3.9 %shard_map.128 = (f32[128,256]{1,0:T(8,128)S(1)}, bf16[256,256]{1,0:T(8,128)(2,1)S(1)}, f32[128,128]{1,0:T(8,128)S(1)}) custom-call(f32[328,128]{1,0:T(8,128)S(1)} %shard_map.126.token_ref.mine_ref, f32[328,128]{1,0:T(8,128)S(1)} %collective-permute-done.5.other_ref, bf16[16,256,256]{2,1,0:T(8,128)(2,1)S(1)} %get-tuple-element.88.chosen_ref, ...), custom_call_target="tpu_custom_call" | custom-call | bytes 4194304 | tf_op jit(solution)/shard_map/pallas_call | solution.py:1061
  28.2 3.2 %collective-permute-start.6 = (f32[128,128]{1,0:T(8,128)S(1)}, f32[128,128]{1,0:T(8,128)S(1)}, u32[]{:S(2)}, u32[]{:S(2)}) collective-permute-start(f32[128,128]{1,0:T(8,128)S(1)} %get-tuple-element.99), channel_id=1, source_target_pairs={{0,30},{1,29},{2,4},{3,31},{4,2},{5,9},{6,8},{7,11},{8,6},{9,5},{1... | collective-permute-start | bytes 196616 | tf_op jit(solution)/shard_map/ppermute | solution.py:886
  31.4 0.0 collective-permute-start.7
  31.4 5.3 %shard_map.129 = (f32[128,128]{1,0:T(8,128)}, f32[128,512]{1,0:T(8,128)S(1)}, f32[128,128]{1,0:T(8,128)S(1)}, f32[16,128,512]{2,1,0:T(8,128)S(1)}, f32[8,256]{1,0:T(8,128)S(1)}, /*index=5*/s32[16,256]{1,0:T(8,128)S(1)}) custom-call(f32[128,512]{1,0:T(8,128)S(1)} %get-tuple-element.81.fine_ref, f32[64,128]{1,0:T(8,128)S(1)} %collective-permute-done.3.even_mine, ...), custom_call_target="tpu_custom_call" | custom-call | flops 8000000000 | bytes 4194304 | tf_op jit(solution)/shard_map/pallas_call | solution.py:1069
  36.7 0.0 collective-permute-done.6.first_in
  36.7 0.0 collective-permute-done.7.second_in
  36.7 0.2 shard_map.130
  36.9 0.4 %collective-permute-start.8 = (f32[128,128]{1,0:T(8,128)S(1)}, f32[128,128]{1,0:T(8,128)S(1)}, u32[]{:S(2)}, u32[]{:S(2)}) collective-permute-start(f32[128,128]{1,0:T(8,128)S(1)} %get-tuple-element.101.token_ref), channel_id=1, source_target_pairs={{0,1},{1,0},{2,3},{3,2},{4,5},{5,4},{6,7},{7,6},{8,9},{9,8},{10,11... | collective-permute-start | bytes 196616 | tf_op jit(solution)/shard_map/ppermute | solution.py:826
  37.3 0.5 %shard_map.131 = (s32[16,512]{1,0:T(8,128)S(1)}, bf16[6,256,128]{2,1,0:T(8,128)(2,1)S(1)}, f32[4,128,128]{2,1,0:T(8,128)S(1)}) custom-call(f32[128,128]{1,0:T(8,128)S(1)} %get-tuple-element.101.token_ref, s32[16,512]{1,0:T(8,128)S(1)} %get-tuple-element.59.nbr_ref, s32[8,512]{1,0:T(8,128)S(1)} %get-tuple-element.103.place_ref, ...), custom_call_target="tpu_custom_call" | custom-call | flops 1000000000 | bytes 4194304 | tf_op jit(solution)/shard_map/pallas_call | solution.py:1105
  37.9 0.4 collective-permute-done.8.back_ref
  38.2 4.3 %shard_map.132 = f32[512,128]{1,0:T(8,128)} custom-call(f32[128,512]{1,0:T(8,128)S(1)} %get-tuple-element.95.own_ref, f32[128,128]{1,0:T(8,128)S(1)} %get-tuple-element.100.late_in, f32[128,128]{1,0:T(8,128)S(1)} %collective-permute-done.8.back_ref, f32[16,128,512]{2,1,0:T(8,128)S(1)} %get-tuple-element.102.partial_ref, ...), custom_call_target="tpu_custom_call" | custom-call | bytes 4194304 | tf_op jit(solution)/shard_map/pallas_call | solution.py:1111
Async XLA Ops:
  1.9 11.2 %collective-permute-start.2 = (f32[64,128]{1,0:T(8,128)S(1)}, f32[64,128]{1,0:T(8,128)S(1)}, u32[]{:S(2)}, u32[]{:S(2)}) collective-permute-start(f32[64,128]{1,0:T(8,128)S(1)} %get-tuple-element.78.sent_dom), channel_id=1, source_target_pairs={{0,1},{1,0},{2,3},{3,2},{4,5},{5,4},{6,7},{7,6},{8,9},{9,8},{10,11... | collective-permute-start | bytes 98312 | tf_op jit(solution)/shard_map/ppermute | solution.py:826
  2.4 10.6 %collective-permute-start = (f32[16,128]{1,0:T(8,128)S(1)}, f32[16,128]{1,0:T(8,128)S(1)}, u32[]{:S(2)}, u32[]{:S(2)}) collective-permute-start(f32[16,128]{1,0:T(8,128)S(1)} %get-tuple-element.76), channel_id=1, source_target_pairs={{0,30},{2,4},{4,2},{6,8},{8,6},{10,12},{12,10},{14,16},{16,14},{18... | collective-permute-start | bytes 24584 | tf_op jit(solution)/shard_map/ppermute | solution.py:826
  9.0 4.1 %collective-permute-start.1 = (f32[16,128]{1,0:T(8,128)S(1)}, f32[16,128]{1,0:T(8,128)S(1)}, u32[]{:S(2)}, u32[]{:S(2)}) collective-permute-start(f32[16,128]{1,0:T(8,128)S(1)} %get-tuple-element.77), channel_id=1, source_target_pairs={{0,2},{2,0},{4,6},{6,4},{8,10},{10,8},{12,14},{14,12},{16,18},{18,... | collective-permute-start | bytes 24584 | tf_op jit(solution)/shard_map/ppermute | solution.py:826
  14.9 7.6 %collective-permute-start.3 = (f32[64,128]{1,0:T(8,128)S(1)}, f32[64,128]{1,0:T(8,128)S(1)}, u32[]{:S(2)}, u32[]{:S(2)}) collective-permute-start(f32[64,128]{1,0:T(8,128)S(1)} %get-tuple-element.82), channel_id=1, source_target_pairs={{0,30},{2,4},{4,2},{6,8},{8,6},{10,12},{12,10},{14,16},{16,14},{18... | collective-permute-start | bytes 98312 | tf_op jit(solution)/shard_map/ppermute | solution.py:826
  18.1 4.4 %collective-permute-start.4 = (f32[64,128]{1,0:T(8,128)S(1)}, f32[64,128]{1,0:T(8,128)S(1)}, u32[]{:S(2)}, u32[]{:S(2)}) collective-permute-start(f32[64,128]{1,0:T(8,128)S(1)} %get-tuple-element.83), channel_id=1, source_target_pairs={{0,2},{2,0},{4,6},{6,4},{8,10},{10,8},{12,14},{14,12},{16,18},{18,... | collective-permute-start | bytes 98312 | tf_op jit(solution)/shard_map/ppermute | solution.py:826
  22.7 1.5 %collective-permute-start.5 = (f32[328,128]{1,0:T(8,128)S(1)}, f32[328,128]{1,0:T(8,128)S(1)}, u32[]{:S(2)}, u32[]{:S(2)}) collective-permute-start(f32[328,128]{1,0:T(8,128)S(1)} %shard_map.126.token_ref.mine_ref), channel_id=1, source_target_pairs={{0,1},{1,0},{2,3},{3,2},{4,5},{5,4},{6,7},{7,6},{8,9},{9,8},{10,11... | collective-permute-start | bytes 503816 | tf_op jit(solution)/shard_map/ppermute | solution.py:826
  28.2 8.6 %collective-permute-start.6 = (f32[128,128]{1,0:T(8,128)S(1)}, f32[128,128]{1,0:T(8,128)S(1)}, u32[]{:S(2)}, u32[]{:S(2)}) collective-permute-start(f32[128,128]{1,0:T(8,128)S(1)} %get-tuple-element.99), channel_id=1, source_target_pairs={{0,30},{1,29},{2,4},{3,31},{4,2},{5,9},{6,8},{7,11},{8,6},{9,5},{1... | collective-permute-start | bytes 196616 | tf_op jit(solution)/shard_map/ppermute | solution.py:886
  31.4 5.3 %collective-permute-start.7 = (f32[128,128]{1,0:T(8,128)S(1)}, f32[128,128]{1,0:T(8,128)S(1)}, u32[]{:S(2)}, u32[]{:S(2)}) collective-permute-start(f32[128,128]{1,0:T(8,128)S(1)} %get-tuple-element.99), channel_id=1, source_target_pairs={{0,4},{1,3},{2,6},{3,1},{4,0},{5,7},{6,2},{7,5},{8,12},{9,11},{10,... | collective-permute-start | bytes 196616 | tf_op jit(solution)/shard_map/ppermute | solution.py:886
  36.9 1.3 %collective-permute-start.8 = (f32[128,128]{1,0:T(8,128)S(1)}, f32[128,128]{1,0:T(8,128)S(1)}, u32[]{:S(2)}, u32[]{:S(2)}) collective-permute-start(f32[128,128]{1,0:T(8,128)S(1)} %get-tuple-element.101.token_ref), channel_id=1, source_target_pairs={{0,1},{1,0},{2,3},{3,2},{4,5},{5,4},{6,7},{7,6},{8,9},{9,8},{10,11... | collective-permute-start | bytes 196616 | tf_op jit(solution)/shard_map/ppermute | solution.py:826

commit v5 on v4

--- a/solution.py
+++ b/solution.py
@@ -12,6 +12,7 @@
 bf16 = jnp.bfloat16
 LANES = 128
 PARTS = 2
+REST = 4
 WIDE = 512
 VMEM_BYTES = 32 * 2**20
 
@@ -732,21 +733,36 @@
     own = fine_ref[...] + share * hot_gather(stacked, parent_ref[...] - region * group)
     own_ref[...] = own
     stacked = stacked_halves(times(halves(edge_ref[edge_ref.shape[0] - 1, 1]), own))
-    for slot in range(nbr_ref.shape[0]):
+    for slot in range(partial_ref.shape[0]):
         partial_ref[slot] = hot_gather(stacked, nbr_ref[slot : slot + 1, :])
     for copy in copies:
         copy.wait()
 
 
 def prepare_last_kernel(
-    token_ref, nbr_ref, place_ref, edge_ref, node_ref, bias_ref, late_index, factors, columns
+    token_ref,
+    own_ref,
+    nbr_ref,
+    place_ref,
+    edge_ref,
+    node_ref,
+    bias_ref,
+    late_index,
+    factors,
+    columns,
+    partial_ref,
 ):
     last = edge_ref.shape[0] - 1
     prepare(edge_ref.at[last], node_ref.at[last], bias_ref.at[last], factors, columns)
     late_places(nbr_ref, place_ref, late_index)
-
-
-def side_kernel(weight_ref, lanes_ref, late_in, first_in, second_in, late_ref, back_ref):
+    stacked = stacked_halves(times(factors[1], own_ref[...]))
+    left = nbr_ref.shape[0] - partial_ref.shape[0]
+    for slot in range(partial_ref.shape[0]):
+        row = left + slot
+        partial_ref[slot] = hot_gather(stacked, nbr_ref[row : row + 1, :])
+
+
+def side_kernel(weight_ref, lanes_ref, late_in, second_in, first_in, late_ref, back_ref):
     first = lax.axis_index("dom") == 0
     near = jnp.where(first, first_in[...], second_in[...])
     far_rows = jnp.where(first, second_in[...], first_in[...])
@@ -761,6 +777,7 @@
     late_in,
     back_ref,
     partial_ref,
+    partial_rest,
     late_index,
     place_ref,
     valid_ref,
@@ -775,8 +792,11 @@
     block = times(factors[1], late)
     term, node_term = own_products(factors, columns, (0, 3), own)
 
+    early = partial_ref.shape[0]
+
     def before(slot):
-        return partial_ref[slot] + block_gather(block, late_index[slot : slot + 1, :]) + term
+        partial = partial_ref[slot] if slot < early else partial_rest[slot - early]
+        return partial + block_gather(block, late_index[slot : slot + 1, :]) + term
 
     gathered = edge_sum(before, valid_ref, factors[2], columns[1])
     copies = []
@@ -1066,6 +1086,7 @@
     first = both_swap(answers, even_partner, even_two_partner)
     second = both_swap(answers, odd_two_partner, odd_partner)
 
+    rest = slots // REST
     coarse_out, own, late, partial, weight, lanes = kernel_call(
         functools.partial(between_kernel, rim, group, side),
         [whole()] * 15,
@@ -1073,7 +1094,7 @@
             (own_coarse, width),
             columns_shape,
             (width, LANES),
-            (slots, width, count),
+            (slots - rest, width, count),
             (8, 2 * LANES),
             ((16, 2 * LANES), i32),
         ],
@@ -1100,23 +1121,37 @@
     )
     late, back = kernel_call(
         side_kernel, [whole()] * 5, [(width, LANES), (width, LANES)]
-    )(weight, lanes, late, first, second)
+    )(weight, lanes, late, second, first)
     back_here = dom_swap(back)
-    late_index, factors, columns = kernel_call(
+    late_index, factors, columns, partial_rest = kernel_call(
         prepare_last_kernel,
-        [whole()] * 6,
-        [fine_slots, ((6, 2 * width, width), bf16), (4, width, LANES)],
+        [whole()] * 7,
+        [
+            fine_slots,
+            ((6, 2 * width, width), bf16),
+            (4, width, LANES),
+            (rest, width, count),
+        ],
         flops=10**9,
-    )(back, nbr, place, edge_later, node_later, bias_later)
+    )(back, own, nbr, place, edge_later, node_later, bias_later)
     (fine_out,) = kernel_call(
         last_kernel,
-        [whole()] * 9,
+        [whole()] * 10,
         [(count, width)],
         [pltpu.VMEM((count, width), f32)],
         copies=PARTS,
         sent=(0,),
     )(
-        own, late, back_here, partial, late_index, place, valid, factors, columns
+        own,
+        late,
+        back_here,
+        partial,
+        partial_rest,
+        late_index,
+        place,
+        valid,
+        factors,
+        columns,
     )
     return (fine_out, coarse_out)
 

time: 42.9 us -> 42.4 us (0.988)
    pallas_call x1, Pallas kernels: 5.32 us -> 4.75 us  [body(): kernel_call(functools.partial(between_kernel, rim, group, side), [whole()...]
    pallas_call x2, Pallas kernels: 4.86 us -> 5.31 us  [the longest x1 4.34 us: body(): kernel_call(last_kernel, [whole()] * 10, [(count, width)], [pltpu.VMEM((c...]
  transfers between devices with their start and end apart: 9 -> 9, of which waited for: 3 -> 4; matrix products, arithmetic and copies ran while one was open for 0% -> 0% of each run, Pallas kernels for 35% -> 35%
where the time goes in v5:
time: 42.4 us; the launch traced here: 42.3 us
  Pallas kernels  26.7 us (63%)
  starting transfers between devices  13.7 us (32%)
  waiting for transfers between devices  0.9 us (2%)
  between operations  0.9 us (2%)
    ppermute x7, starting transfers between devices, swap(): lax.ppermute(value, axis, [(source, partner(source) % count) for source i...  10.5 us
    pallas_call x1, Pallas kernels, body(): kernel_call(functools.partial(between_kernel, rim, group, side), [whole()...  4.75 us
    pallas_call x1, Pallas kernels, body(): kernel_call(last_kernel, [whole()] * 10, [(count, width)], [pltpu.VMEM((c...  4.34 us
    pallas_call x1, Pallas kernels, body(): kernel_call(functools.partial(before_kernel, rim, group, side, regions),...  4.05 us
    pallas_call x1, Pallas kernels, body(): kernel_call(functools.partial(coarse_kernel, rim, group, side), [whole()]...  3.94 us
    pallas_call x1, Pallas kernels, body(): kernel_call(functools.partial(fine_kernel, rim, group), [whole()] * 12, [...  3.9 us
    ppermute x2, starting transfers between devices, both_swap(): return lax.ppermute(value, ('region', 'dom'), pairs)  3.19 us
    pallas_call x1, Pallas kernels, body(): kernel_call(first_body, [whole()] * 11, [(block_rows, width), (block_rows...  1.83 us
  transfers between devices with their start and end apart: 9, of which 4 were waited for; matrix products, arithmetic and copies ran while one was open for 0% of the time, Pallas kernels for 35%

profile of v5, /device:TPU:0, one launch (start us, length us, event | category | flops | bytes accessed | tf_op | source)
XLA Modules:
  0.0 42.3 jit_solution(6605756354637167398)
XLA Ops:
  0.6 1.3 %shard_map.122 = (f32[16,128]{1,0:T(8,128)S(1)}, f32[16,128]{1,0:T(8,128)S(1)}, f32[64,128]{1,0:T(8,128)S(1)}, s32[8,128]{1,0:T(8,128)S(1)}, f32[512,128]{1,0:T(...) custom-call(s32[4,16]{1,0:T(4,128)} %send_hbm.1, ...), custom_call_target="tpu_custom_call" | custom-call | bytes 4194304 | tf_op jit(solution)/shard_map/pallas_call | solution.py:924
  1.9 7.0 %collective-permute-start = (f32[16,128]{1,0:T(8,128)S(1)}, f32[16,128]{1,0:T(8,128)S(1)}, u32[]{:S(2)}, u32[]{:S(2)}) collective-permute-start(f32[16,128]{1,0:T(8,128)S(1)} %get-tuple-element.77), channel_id=1, source_target_pairs={{0,30},{2,4},{4,2},{6,8},{8,6},{10,12},{12,10},{14,16},{16,14},{18... | collective-permute-start | bytes 24584 | tf_op jit(solution)/shard_map/ppermute | solution.py:846
  8.9 0.0 collective-permute-start.1
  8.9 0.0 collective-permute-start.2
  8.9 4.0 %shard_map.123 = (f32[128,512]{1,0:T(8,128)S(1)}, f32[128,512]{1,0:T(8,128)S(1)}, f32[16,128,512]{2,1,0:T(8,128)S(1)}, f32[16,512]{1,0:T(8,128)S(1)}, bf16[6,256...) custom-call(f32[512,128]{1,0:T(8,128)S(1)} %get-tuple-element.56.sta, ...), custom_call_target="tpu_custom_call" | custom-call | flops 4000000000 | bytes 4194304 | tf_op jit(solution)/shard_map/pallas_call | solution.py:980
  13.0 0.0 collective-permute-done.refs_8_
  13.0 0.0 collective-permute-done.1.refs_9_
  13.0 0.0 collective-permute-done.2.refs_10_.meta_dom
  13.0 1.8 %shard_map.124 = (f32[64,128]{1,0:T(8,128)S(1)}, f32[64,128]{1,0:T(8,128)S(1)}, f32[32,128]{1,0:T(8,128)S(1)}, f32[128,128]{1,0:T(8,128)S(1)}) custom-call(f32[128,128]{1,0:T(8,128)S(1)} %get-tuple-element.71.refs_0_, f32[128,128]{1,0:T(8,128)S(1)} %get-tuple-element.72.refs_1_, f32[16,128,128]{2,1,0:T(8,128)S(1)} %get-tuple-element.73.refs_2_, ...), custom_call_target="tpu_custom_call" | custom-call | bytes 4194304 | tf_op jit(solution)/shard_map/pallas_call | solution.py:1022
  14.8 3.2 %collective-permute-start.3 = (f32[64,128]{1,0:T(8,128)S(1)}, f32[64,128]{1,0:T(8,128)S(1)}, u32[]{:S(2)}, u32[]{:S(2)}) collective-permute-start(f32[64,128]{1,0:T(8,128)S(1)} %get-tuple-element.83), channel_id=1, source_target_pairs={{0,30},{2,4},{4,2},{6,8},{8,6},{10,12},{12,10},{14,16},{16,14},{18... | collective-permute-start | bytes 98312 | tf_op jit(solution)/shard_map/ppermute | solution.py:846
  18.0 0.0 collective-permute-start.4
  18.0 3.9 %shard_map.125 = (f32[128,512]{1,0:T(8,128)S(1)}, f32[312,128]{1,0:T(8,128)S(1)}) custom-call(f32[128,512]{1,0:T(8,128)S(1)} %get-tuple-element.65.own_ref, f32[128,512]{1,0:T(8,128)S(1)} %get-tuple-element.66.node_term_ref, f32[16,128,512]{2,1,0:T(8,128)S(1)} %get-tuple-element.67.partial_ref, s32[16,512]{1,0:T(8,128)S(1)} %get-tuple-element.60.nbr_ref, ...), custom_call_target="tpu_custom_call" | custom-call | flops 4000000000 | bytes 4194304 | tf_op jit(solution)/shard_map/pallas_call | solution.py:1042
  22.0 0.5 %collective-permute-done.3.even_mine = f32[64,128]{1,0:T(8,128)S(1)} collective-permute-done((f32[64,128]{1,0:T(8,128)S(1)}, f32[64,128]{1,0:T(8,128)S(1)}, u32[]{:S(2)}, u32[]{:S(2)}) %collective-permute-start.3) | collective-permute-done | bytes 32800 | tf_op jit(solution)/shard_map/ppermute | solution.py:846
  22.4 0.0 collective-permute-done.4.odd_mine
  22.4 0.3 shard_map.126.token_ref.mine_ref
  22.7 0.1 collective-permute-start.5
  22.8 1.3 %shard_map.127 = (bf16[2,6,256,128]{3,2,1,0:T(8,128)(2,1)S(1)}, f32[2,4,128,128]{3,2,1,0:T(8,128)S(1)}, bf16[16,256,256]{2,1,0:T(8,128)(2,1)S(1)}, s32[16,256]{1,0:T(8,128)S(1)}, f32[16,256]{1,0:T(8,128)S(1)}) custom-call(f32[328,128]{1,0:T(8,128)S(1)} %shard_map.126.token_ref.mine_ref, f32[64,128]{1,0:T(8,128)S(1)} %get-tuple-element.79.sent_dom, ...), custom_call_target="tpu_custom_call" | custom-call | flops 1000000000 | bytes 4194304 | tf_op jit(solution)/shard_map/pallas_call | solution.py:1068
  24.0 0.1 collective-permute-done.5.other_ref
  24.2 3.9 %shard_map.128 = (f32[128,256]{1,0:T(8,128)S(1)}, bf16[256,256]{1,0:T(8,128)(2,1)S(1)}, f32[128,128]{1,0:T(8,128)S(1)}) custom-call(f32[328,128]{1,0:T(8,128)S(1)} %shard_map.126.token_ref.mine_ref, f32[328,128]{1,0:T(8,128)S(1)} %collective-permute-done.5.other_ref, bf16[16,256,256]{2,1,0:T(8,128)(2,1)S(1)} %get-tuple-element.89.chosen_ref, ...), custom_call_target="tpu_custom_call" | custom-call | bytes 4194304 | tf_op jit(solution)/shard_map/pallas_call | solution.py:1081
  28.1 3.2 %collective-permute-start.7 = (f32[128,128]{1,0:T(8,128)S(1)}, f32[128,128]{1,0:T(8,128)S(1)}, u32[]{:S(2)}, u32[]{:S(2)}) collective-permute-start(f32[128,128]{1,0:T(8,128)S(1)} %get-tuple-element.100), channel_id=1, source_target_pairs={{0,30},{1,29},{2,4},{3,31},{4,2},{5,9},{6,8},{7,11},{8,6},{9,5},{1... | collective-permute-start | bytes 196616 | tf_op jit(solution)/shard_map/ppermute | solution.py:906
  31.3 0.0 collective-permute-start.6
  31.3 4.7 %shard_map.129 = (f32[128,128]{1,0:T(8,128)}, f32[128,512]{1,0:T(8,128)S(1)}, f32[128,128]{1,0:T(8,128)S(1)}, f32[12,128,512]{2,1,0:T(8,128)S(1)}, f32[8,256]{1,0:T(8,128)S(1)}, /*index=5*/s32[16,256]{1,0:T(8,128)S(1)}) custom-call(f32[128,512]{1,0:T(8,128)S(1)} %get-tuple-element.82.fine_ref, f32[64,128]{1,0:T(8,128)S(1)} %collective-permute-done.3.even_mine, ...), custom_call_target="tpu_custom_call" | custom-call | flops 8000000000 | bytes 4194304 | tf_op jit(solution)/shard_map/pallas_call | solution.py:1090
  36.1 0.2 collective-permute-done.7.first_in
  36.3 0.0 collective-permute-done.6.second_in
  36.3 0.2 shard_map.130
  36.4 0.3 collective-permute-start.8
  36.7 1.0 %shard_map.131 = (s32[16,512]{1,0:T(8,128)S(1)}, bf16[6,256,128]{2,1,0:T(8,128)(2,1)S(1)}, f32[4,128,128]{2,1,0:T(8,128)S(1)}, f32[4,128,512]{2,1,0:T(8,128)S(1)}) custom-call(f32[128,128]{1,0:T(8,128)S(1)} %get-tuple-element.102.token_ref, f32[128,512]{1,0:T(8,128)S(1)} %get-tuple-element.96.own_ref, s32[16,512]{1,0:T(8,128)S(1)} %get-tuple-element.60.nbr_ref, ...), custom_call_target="tpu_custom_call" | custom-call | flops 1000000000 | bytes 4194304 | tf_op jit(solution)/shard_map/pallas_call | solution.py:1126
  37.7 0.1 collective-permute-done.8.back_ref
  37.8 4.3 %shard_map.132 = f32[512,128]{1,0:T(8,128)} custom-call(f32[128,512]{1,0:T(8,128)S(1)} %get-tuple-element.96.own_ref, f32[128,128]{1,0:T(8,128)S(1)} %get-tuple-element.101.late_in, f32[128,128]{1,0:T(8,128)S(1)} %collective-permute-done.8.back_ref, f32[12,128,512]{2,1,0:T(8,128)S(1)} %get-tuple-element.103.partial_ref, ...), custom_call_target="tpu_custom_call" | custom-call | bytes 4194304 | tf_op jit(solution)/shard_map/pallas_call | solution.py:1137
Async XLA Ops:
  1.9 11.1 %collective-permute-start = (f32[16,128]{1,0:T(8,128)S(1)}, f32[16,128]{1,0:T(8,128)S(1)}, u32[]{:S(2)}, u32[]{:S(2)}) collective-permute-start(f32[16,128]{1,0:T(8,128)S(1)} %get-tuple-element.77), channel_id=1, source_target_pairs={{0,30},{2,4},{4,2},{6,8},{8,6},{10,12},{12,10},{14,16},{16,14},{18... | collective-permute-start | bytes 24584 | tf_op jit(solution)/shard_map/ppermute | solution.py:846
  8.9 4.1 %collective-permute-start.1 = (f32[16,128]{1,0:T(8,128)S(1)}, f32[16,128]{1,0:T(8,128)S(1)}, u32[]{:S(2)}, u32[]{:S(2)}) collective-permute-start(f32[16,128]{1,0:T(8,128)S(1)} %get-tuple-element.78), channel_id=1, source_target_pairs={{0,2},{2,0},{4,6},{6,4},{8,10},{10,8},{12,14},{14,12},{16,18},{18,... | collective-permute-start | bytes 24584 | tf_op jit(solution)/shard_map/ppermute | solution.py:846
  8.9 4.1 %collective-permute-start.2 = (f32[64,128]{1,0:T(8,128)S(1)}, f32[64,128]{1,0:T(8,128)S(1)}, u32[]{:S(2)}, u32[]{:S(2)}) collective-permute-start(f32[64,128]{1,0:T(8,128)S(1)} %get-tuple-element.79.sent_dom), channel_id=1, source_target_pairs={{0,1},{1,0},{2,3},{3,2},{4,5},{5,4},{6,7},{7,6},{8,9},{9,8},{10,11... | collective-permute-start | bytes 98312 | tf_op jit(solution)/shard_map/ppermute | solution.py:846
  14.8 7.6 %collective-permute-start.3 = (f32[64,128]{1,0:T(8,128)S(1)}, f32[64,128]{1,0:T(8,128)S(1)}, u32[]{:S(2)}, u32[]{:S(2)}) collective-permute-start(f32[64,128]{1,0:T(8,128)S(1)} %get-tuple-element.83), channel_id=1, source_target_pairs={{0,30},{2,4},{4,2},{6,8},{8,6},{10,12},{12,10},{14,16},{16,14},{18... | collective-permute-start | bytes 98312 | tf_op jit(solution)/shard_map/ppermute | solution.py:846
  18.0 4.4 %collective-permute-start.4 = (f32[64,128]{1,0:T(8,128)S(1)}, f32[64,128]{1,0:T(8,128)S(1)}, u32[]{:S(2)}, u32[]{:S(2)}) collective-permute-start(f32[64,128]{1,0:T(8,128)S(1)} %get-tuple-element.84), channel_id=1, source_target_pairs={{0,2},{2,0},{4,6},{6,4},{8,10},{10,8},{12,14},{14,12},{16,18},{18,... | collective-permute-start | bytes 98312 | tf_op jit(solution)/shard_map/ppermute | solution.py:846
  22.7 1.5 %collective-permute-start.5 = (f32[328,128]{1,0:T(8,128)S(1)}, f32[328,128]{1,0:T(8,128)S(1)}, u32[]{:S(2)}, u32[]{:S(2)}) collective-permute-start(f32[328,128]{1,0:T(8,128)S(1)} %shard_map.126.token_ref.mine_ref), channel_id=1, source_target_pairs={{0,1},{1,0},{2,3},{3,2},{4,5},{5,4},{6,7},{7,6},{8,9},{9,8},{10,11... | collective-permute-start | bytes 503816 | tf_op jit(solution)/shard_map/ppermute | solution.py:846
  28.1 8.2 %collective-permute-start.7 = (f32[128,128]{1,0:T(8,128)S(1)}, f32[128,128]{1,0:T(8,128)S(1)}, u32[]{:S(2)}, u32[]{:S(2)}) collective-permute-start(f32[128,128]{1,0:T(8,128)S(1)} %get-tuple-element.100), channel_id=1, source_target_pairs={{0,30},{1,29},{2,4},{3,31},{4,2},{5,9},{6,8},{7,11},{8,6},{9,5},{1... | collective-permute-start | bytes 196616 | tf_op jit(solution)/shard_map/ppermute | solution.py:906
  31.3 5.0 %collective-permute-start.6 = (f32[128,128]{1,0:T(8,128)S(1)}, f32[128,128]{1,0:T(8,128)S(1)}, u32[]{:S(2)}, u32[]{:S(2)}) collective-permute-start(f32[128,128]{1,0:T(8,128)S(1)} %get-tuple-element.100), channel_id=1, source_target_pairs={{0,4},{1,3},{2,6},{3,1},{4,0},{5,7},{6,2},{7,5},{8,12},{9,11},{10,... | collective-permute-start | bytes 196616 | tf_op jit(solution)/shard_map/ppermute | solution.py:906
  36.4 1.3 %collective-permute-start.8 = (f32[128,128]{1,0:T(8,128)S(1)}, f32[128,128]{1,0:T(8,128)S(1)}, u32[]{:S(2)}, u32[]{:S(2)}) collective-permute-start(f32[128,128]{1,0:T(8,128)S(1)} %get-tuple-element.102.token_ref), channel_id=1, source_target_pairs={{0,1},{1,0},{2,3},{3,2},{4,5},{5,4},{6,7},{7,6},{8,9},{9,8},{10,11... | collective-permute-start | bytes 196616 | tf_op jit(solution)/shard_map/ppermute | solution.py:846

commit v6 on v5

--- a/solution.py
+++ b/solution.py
@@ -12,7 +12,7 @@
 bf16 = jnp.bfloat16
 LANES = 128
 PARTS = 2
-REST = 4
+REST = 3
 WIDE = 512
 VMEM_BYTES = 32 * 2**20
 
@@ -362,7 +362,6 @@
         out[0:side, :] = jnp.where(is_low, low, high)
         out[side : side + 8, :] = facts_ref[...]
         out[side + 8 : side + 8 + rim, :] = jnp.where(is_low, down, up)
-        out[side + 8 + rim :, :] = jnp.zeros((out.shape[0] - side - 8 - rim, LANES), f32)
 
 
 def fine_kernel(
@@ -624,7 +623,8 @@
     columns,
     middle_ref,
     sources_ref,
-    answer_ref,
+    first_ref,
+    second_ref,
 ):
     region, dom = lax.axis_index("region"), lax.axis_index("dom")
     facts = known_facts(group, rim, dom, mine_ref, other_ref)
@@ -649,7 +649,12 @@
     chosen = hot(group, wide_row(nbr, 0, nbr.shape[0])).astype(bf16)
     some = pick_columns(own, asked)
     some = coarse_layer(some, sources, chosen, valid, factors.at[1], columns.at[1])
-    answer_ref[...] = jnp.where(inside, some, 0.0)
+    rows = jnp.where(inside, some, 0.0).T
+    near = jnp.concatenate([rows[: 2 * rim], rows[4 * rim :]], axis=0)
+    beyond = rows[2 * rim : 2 * rim + near.shape[0]]
+    first = dom == 0
+    first_ref[...] = jnp.where(first, near, beyond)
+    second_ref[...] = jnp.where(first, beyond, near)
 
 
 def between_kernel(
@@ -762,11 +767,13 @@
         partial_ref[slot] = hot_gather(stacked, nbr_ref[row : row + 1, :])
 
 
-def side_kernel(weight_ref, lanes_ref, late_in, second_in, first_in, late_ref, back_ref):
+def side_kernel(rim, weight_ref, lanes_ref, late_in, first_in, second_in, late_ref, back_ref):
     first = lax.axis_index("dom") == 0
     near = jnp.where(first, first_in[...], second_in[...])
-    far_rows = jnp.where(first, second_in[...], first_in[...])
-    late = block_gather(near, lanes_ref[0:1, :]) + block_gather(far_rows, lanes_ref[8:9, :])
+    beyond = jnp.where(first, second_in[...], first_in[...])
+    rims = [near[: 2 * rim], beyond[: 2 * rim], near[2 * rim :]]
+    came = jnp.concatenate(rims, axis=0).T
+    late = block_gather(came, lanes_ref[0:1, :]) + block_gather(came, lanes_ref[8:9, :])
     late = late * weight_ref[1:2, :]
     late_ref[...] = late_in[...] + late[:, :LANES]
     back_ref[...] = late[:, LANES:]
@@ -1013,7 +1020,7 @@
         *weights,
     )
 
-    block_rows = side + 8 + rim + 8
+    block_rows = side + 8 + rim
     dom_rows = group + 8 * (group // LANES) + 2 * rim + 8
 
     def first_body(*refs):
@@ -1078,13 +1085,19 @@
         flops=10**9,
     )(mine, dom_out, meta_dom, edge_later, node_later, bias_later)
 
-    middle, sources, answers = kernel_call(
+    near_rows = 2 * rim + 2 * side
+    middle, sources, first_out, second_out = kernel_call(
         functools.partial(coarse_kernel, rim, group, side),
         [whole()] * 7,
-        [(width, group), ((2 * width, group), bf16), (width, LANES)],
+        [
+            (width, group),
+            ((2 * width, group), bf16),
+            (near_rows, width),
+            (near_rows, width),
+        ],
     )(mine, other, group_chosen, group_nbr, group_valid, factors, columns)
-    first = both_swap(answers, even_partner, even_two_partner)
-    second = both_swap(answers, odd_two_partner, odd_partner)
+    first = both_swap(first_out, even_partner, even_two_partner)
+    second = both_swap(second_out, odd_two_partner, odd_partner)
 
     rest = slots // REST
     coarse_out, own, late, partial, weight, lanes = kernel_call(
@@ -1120,8 +1133,8 @@
         edge_later,
     )
     late, back = kernel_call(
-        side_kernel, [whole()] * 5, [(width, LANES), (width, LANES)]
-    )(weight, lanes, late, second, first)
+        functools.partial(side_kernel, rim), [whole()] * 5, [(width, LANES), (width, LANES)]
+    )(weight, lanes, late, first, second)
     back_here = dom_swap(back)
     late_index, factors, columns, partial_rest = kernel_call(
         prepare_last_kernel,

time: 42.4 us -> 42.6 us (level)
  transfers between devices with their start and end apart: 9 -> 9, of which waited for: 4 -> 2; matrix products, arithmetic and copies ran while one was open for 0% -> 0% of each run, Pallas kernels for 35% -> 35%
where the time goes in v6:
time: 42.6 us; the launch traced here: 42.4 us
  Pallas kernels  27 us (63%)
  starting transfers between devices  14 us (33%)
  between operations  0.91 us (2%)
  waiting for transfers between devices  0.55 us (1%)
    ppermute x7, starting transfers between devices, swap(): lax.ppermute(value, axis, [(source, partner(source) % count) for source i...  10.7 us
    pallas_call x1, Pallas kernels, body(): kernel_call(functools.partial(between_kernel, rim, group, side), [whole()...  4.62 us
    pallas_call x1, Pallas kernels, body(): kernel_call(last_kernel, [whole()] * 10, [(count, width)], [pltpu.VMEM((c...  4.28 us
    pallas_call x1, Pallas kernels, body(): kernel_call(functools.partial(coarse_kernel, rim, group, side), [whole()]...  4.11 us
    pallas_call x1, Pallas kernels, body(): kernel_call(functools.partial(before_kernel, rim, group, side, regions),...  4.05 us
    pallas_call x1, Pallas kernels, body(): kernel_call(functools.partial(fine_kernel, rim, group), [whole()] * 12, [...  3.91 us
    ppermute x2, starting transfers between devices, both_swap(): return lax.ppermute(value, ('region', 'dom'), pairs)  3.23 us
    pallas_call x1, Pallas kernels, body(): kernel_call(first_body, [whole()] * 11, [(block_rows, width), (block_rows...  1.84 us
  transfers between devices with their start and end apart: 9, of which 2 were waited for; matrix products, arithmetic and copies ran while one was open for 0% of the time, Pallas kernels for 35%

profile of v6, /device:TPU:0, one launch (start us, length us, event | category | flops | bytes accessed | tf_op | source)
XLA Modules:
  0.0 42.4 jit_solution(9826324763155850976)
XLA Ops:
  0.6 1.3 %shard_map.122 = (f32[16,128]{1,0:T(8,128)S(1)}, f32[16,128]{1,0:T(8,128)S(1)}, f32[64,128]{1,0:T(8,128)S(1)}, s32[8,128]{1,0:T(8,128)S(1)}, f32[512,128]{1,0:T(...) custom-call(s32[4,16]{1,0:T(4,128)} %send_hbm.1, ...), custom_call_target="tpu_custom_call" | custom-call | bytes 4194304 | tf_op jit(solution)/shard_map/pallas_call | solution.py:931
  1.9 7.0 %collective-permute-start = (f32[16,128]{1,0:T(8,128)S(1)}, f32[16,128]{1,0:T(8,128)S(1)}, u32[]{:S(2)}, u32[]{:S(2)}) collective-permute-start(f32[16,128]{1,0:T(8,128)S(1)} %get-tuple-element.78), channel_id=1, source_target_pairs={{0,30},{2,4},{4,2},{6,8},{8,6},{10,12},{12,10},{14,16},{16,14},{18... | collective-permute-start | bytes 24584 | tf_op jit(solution)/shard_map/ppermute | solution.py:853
  8.9 0.0 collective-permute-start.1
  8.9 0.0 collective-permute-start.2
  8.9 4.0 %shard_map.123 = (f32[128,512]{1,0:T(8,128)S(1)}, f32[128,512]{1,0:T(8,128)S(1)}, f32[16,128,512]{2,1,0:T(8,128)S(1)}, f32[16,512]{1,0:T(8,128)S(1)}, bf16[6,256...) custom-call(f32[512,128]{1,0:T(8,128)S(1)} %get-tuple-element.57.sta, ...), custom_call_target="tpu_custom_call" | custom-call | flops 4000000000 | bytes 4194304 | tf_op jit(solution)/shard_map/pallas_call | solution.py:987
  12.9 0.0 collective-permute-done.refs_8_
  13.0 0.0 collective-permute-done.1.refs_9_
  13.0 0.0 collective-permute-done.2.refs_10_.meta_dom
  13.0 1.8 %shard_map.124 = (f32[56,128]{1,0:T(8,128)S(1)}, f32[56,128]{1,0:T(8,128)S(1)}, f32[32,128]{1,0:T(8,128)S(1)}, f32[128,128]{1,0:T(8,128)S(1)}) custom-call(f32[128,128]{1,0:T(8,128)S(1)} %get-tuple-element.72.refs_0_, f32[128,128]{1,0:T(8,128)S(1)} %get-tuple-element.73.refs_1_, f32[16,128,128]{2,1,0:T(8,128)S(1)} %get-tuple-element.74.refs_2_, ...), custom_call_target="tpu_custom_call" | custom-call | bytes 4194304 | tf_op jit(solution)/shard_map/pallas_call | solution.py:1029
  14.8 3.2 %collective-permute-start.3 = (f32[56,128]{1,0:T(8,128)S(1)}, f32[56,128]{1,0:T(8,128)S(1)}, u32[]{:S(2)}, u32[]{:S(2)}) collective-permute-start(f32[56,128]{1,0:T(8,128)S(1)} %get-tuple-element.84), channel_id=1, source_target_pairs={{0,30},{2,4},{4,2},{6,8},{8,6},{10,12},{12,10},{14,16},{16,14},{18... | collective-permute-start | bytes 86024 | tf_op jit(solution)/shard_map/ppermute | solution.py:853
  18.0 0.0 collective-permute-start.4
  18.0 3.9 %shard_map.125 = (f32[128,512]{1,0:T(8,128)S(1)}, f32[312,128]{1,0:T(8,128)S(1)}) custom-call(f32[128,512]{1,0:T(8,128)S(1)} %get-tuple-element.66.own_ref, f32[128,512]{1,0:T(8,128)S(1)} %get-tuple-element.67.node_term_ref, f32[16,128,512]{2,1,0:T(8,128)S(1)} %get-tuple-element.68.partial_ref, s32[16,512]{1,0:T(8,128)S(1)} %get-tuple-element.61.nbr_ref, ...), custom_call_target="tpu_custom_call" | custom-call | flops 4000000000 | bytes 4194304 | tf_op jit(solution)/shard_map/pallas_call | solution.py:1049
  22.0 0.4 collective-permute-done.3.even_mine
  22.4 0.0 collective-permute-done.4.odd_mine
  22.4 0.3 shard_map.126.token_ref.mine_ref
  22.6 0.1 collective-permute-start.5
  22.7 1.3 %shard_map.127 = (bf16[2,6,256,128]{3,2,1,0:T(8,128)(2,1)S(1)}, f32[2,4,128,128]{3,2,1,0:T(8,128)S(1)}, bf16[16,256,256]{2,1,0:T(8,128)(2,1)S(1)}, s32[16,256]{1,0:T(8,128)S(1)}, f32[16,256]{1,0:T(8,128)S(1)}) custom-call(f32[328,128]{1,0:T(8,128)S(1)} %shard_map.126.token_ref.mine_ref, f32[64,128]{1,0:T(8,128)S(1)} %get-tuple-element.80.sent_dom, ...), custom_call_target="tpu_custom_call" | custom-call | flops 1000000000 | bytes 4194304 | tf_op jit(solution)/shard_map/pallas_call | solution.py:1075
  24.0 0.1 collective-permute-done.5.other_ref
  24.1 4.1 %shard_map.128 = (f32[128,256]{1,0:T(8,128)S(1)}, bf16[256,256]{1,0:T(8,128)(2,1)S(1)}, f32[96,128]{1,0:T(8,128)S(1)}, f32[96,128]{1,0:T(8,128)S(1)}) custom-call(f32[328,128]{1,0:T(8,128)S(1)} %shard_map.126.token_ref.mine_ref, f32[328,128]{1,0:T(8,128)S(1)} %collective-permute-done.5.other_ref, bf16[16,256,256]{2,1,0:T(8,128)(2,1)S(1)} %get-tuple-element.90.chosen_ref, ...), custom_call_target="tpu_custom_call" | custom-call | bytes 4194304 | tf_op jit(solution)/shard_map/pallas_call | solution.py:1089
  28.2 3.2 %collective-permute-start.6 = (f32[96,128]{1,0:T(8,128)S(1)}, f32[96,128]{1,0:T(8,128)S(1)}, u32[]{:S(2)}, u32[]{:S(2)}) collective-permute-start(f32[96,128]{1,0:T(8,128)S(1)} %get-tuple-element.101), channel_id=1, source_target_pairs={{0,30},{1,29},{2,4},{3,31},{4,2},{5,9},{6,8},{7,11},{8,6},{9,5},{1... | collective-permute-start | bytes 147464 | tf_op jit(solution)/shard_map/ppermute | solution.py:913
  31.4 0.0 collective-permute-start.7
  31.4 4.6 %shard_map.129 = (f32[128,128]{1,0:T(8,128)}, f32[128,512]{1,0:T(8,128)S(1)}, f32[128,128]{1,0:T(8,128)S(1)}, f32[11,128,512]{2,1,0:T(8,128)S(1)}, f32[8,256]{1,0:T(8,128)S(1)}, /*index=5*/s32[16,256]{1,0:T(8,128)S(1)}) custom-call(f32[128,512]{1,0:T(8,128)S(1)} %get-tuple-element.83.fine_ref, f32[56,128]{1,0:T(8,128)S(1)} %collective-permute-done.3.even_mine, ...), custom_call_target="tpu_custom_call" | custom-call | flops 8000000000 | bytes 4194304 | tf_op jit(solution)/shard_map/pallas_call | solution.py:1103
  36.1 0.0 collective-permute-done.6.first_in
  36.1 0.0 collective-permute-done.7.second_in
  36.1 0.3 shard_map.130
  36.4 0.4 %collective-permute-start.8 = (f32[128,128]{1,0:T(8,128)S(1)}, f32[128,128]{1,0:T(8,128)S(1)}, u32[]{:S(2)}, u32[]{:S(2)}) collective-permute-start(f32[128,128]{1,0:T(8,128)S(1)} %get-tuple-element.104.token_ref), channel_id=1, source_target_pairs={{0,1},{1,0},{2,3},{3,2},{4,5},{5,4},{6,7},{7,6},{8,9},{9,8},{10,11... | collective-permute-start | bytes 196616 | tf_op jit(solution)/shard_map/ppermute | solution.py:853
  36.9 1.1 %shard_map.131 = (s32[16,512]{1,0:T(8,128)S(1)}, bf16[6,256,128]{2,1,0:T(8,128)(2,1)S(1)}, f32[4,128,128]{2,1,0:T(8,128)S(1)}, f32[5,128,512]{2,1,0:T(8,128)S(1)}) custom-call(f32[128,128]{1,0:T(8,128)S(1)} %get-tuple-element.104.token_ref, f32[128,512]{1,0:T(8,128)S(1)} %get-tuple-element.97.own_ref, s32[16,512]{1,0:T(8,128)S(1)} %get-tuple-element.61.nbr_ref, ...), custom_call_target="tpu_custom_call" | custom-call | flops 1000000000 | bytes 4194304 | tf_op jit(solution)/shard_map/pallas_call | solution.py:1139
  38.0 0.0 collective-permute-done.8.back_ref
  38.0 4.3 %shard_map.132 = f32[512,128]{1,0:T(8,128)} custom-call(f32[128,512]{1,0:T(8,128)S(1)} %get-tuple-element.97.own_ref, f32[128,128]{1,0:T(8,128)S(1)} %get-tuple-element.103.late_in, f32[128,128]{1,0:T(8,128)S(1)} %collective-permute-done.8.back_ref, f32[11,128,512]{2,1,0:T(8,128)S(1)} %get-tuple-element.105.partial_ref, ...), custom_call_target="tpu_custom_call" | custom-call | bytes 4194304 | tf_op jit(solution)/shard_map/pallas_call | solution.py:1150
Async XLA Ops:
  1.9 11.1 %collective-permute-start = (f32[16,128]{1,0:T(8,128)S(1)}, f32[16,128]{1,0:T(8,128)S(1)}, u32[]{:S(2)}, u32[]{:S(2)}) collective-permute-start(f32[16,128]{1,0:T(8,128)S(1)} %get-tuple-element.78), channel_id=1, source_target_pairs={{0,30},{2,4},{4,2},{6,8},{8,6},{10,12},{12,10},{14,16},{16,14},{18... | collective-permute-start | bytes 24584 | tf_op jit(solution)/shard_map/ppermute | solution.py:853
  8.9 4.1 %collective-permute-start.1 = (f32[16,128]{1,0:T(8,128)S(1)}, f32[16,128]{1,0:T(8,128)S(1)}, u32[]{:S(2)}, u32[]{:S(2)}) collective-permute-start(f32[16,128]{1,0:T(8,128)S(1)} %get-tuple-element.79), channel_id=1, source_target_pairs={{0,2},{2,0},{4,6},{6,4},{8,10},{10,8},{12,14},{14,12},{16,18},{18,... | collective-permute-start | bytes 24584 | tf_op jit(solution)/shard_map/ppermute | solution.py:853
  8.9 4.1 %collective-permute-start.2 = (f32[64,128]{1,0:T(8,128)S(1)}, f32[64,128]{1,0:T(8,128)S(1)}, u32[]{:S(2)}, u32[]{:S(2)}) collective-permute-start(f32[64,128]{1,0:T(8,128)S(1)} %get-tuple-element.80.sent_dom), channel_id=1, source_target_pairs={{0,1},{1,0},{2,3},{3,2},{4,5},{5,4},{6,7},{7,6},{8,9},{9,8},{10,11... | collective-permute-start | bytes 98312 | tf_op jit(solution)/shard_map/ppermute | solution.py:853
  14.8 7.5 %collective-permute-start.3 = (f32[56,128]{1,0:T(8,128)S(1)}, f32[56,128]{1,0:T(8,128)S(1)}, u32[]{:S(2)}, u32[]{:S(2)}) collective-permute-start(f32[56,128]{1,0:T(8,128)S(1)} %get-tuple-element.84), channel_id=1, source_target_pairs={{0,30},{2,4},{4,2},{6,8},{8,6},{10,12},{12,10},{14,16},{16,14},{18... | collective-permute-start | bytes 86024 | tf_op jit(solution)/shard_map/ppermute | solution.py:853
  18.0 4.3 %collective-permute-start.4 = (f32[56,128]{1,0:T(8,128)S(1)}, f32[56,128]{1,0:T(8,128)S(1)}, u32[]{:S(2)}, u32[]{:S(2)}) collective-permute-start(f32[56,128]{1,0:T(8,128)S(1)} %get-tuple-element.85), channel_id=1, source_target_pairs={{0,2},{2,0},{4,6},{6,4},{8,10},{10,8},{12,14},{14,12},{16,18},{18,... | collective-permute-start | bytes 86024 | tf_op jit(solution)/shard_map/ppermute | solution.py:853
  22.6 1.5 %collective-permute-start.5 = (f32[328,128]{1,0:T(8,128)S(1)}, f32[328,128]{1,0:T(8,128)S(1)}, u32[]{:S(2)}, u32[]{:S(2)}) collective-permute-start(f32[328,128]{1,0:T(8,128)S(1)} %shard_map.126.token_ref.mine_ref), channel_id=1, source_target_pairs={{0,1},{1,0},{2,3},{3,2},{4,5},{5,4},{6,7},{7,6},{8,9},{9,8},{10,11... | collective-permute-start | bytes 503816 | tf_op jit(solution)/shard_map/ppermute | solution.py:853
  28.2 7.9 %collective-permute-start.6 = (f32[96,128]{1,0:T(8,128)S(1)}, f32[96,128]{1,0:T(8,128)S(1)}, u32[]{:S(2)}, u32[]{:S(2)}) collective-permute-start(f32[96,128]{1,0:T(8,128)S(1)} %get-tuple-element.101), channel_id=1, source_target_pairs={{0,30},{1,29},{2,4},{3,31},{4,2},{5,9},{6,8},{7,11},{8,6},{9,5},{1... | collective-permute-start | bytes 147464 | tf_op jit(solution)/shard_map/ppermute | solution.py:913
  31.4 4.7 %collective-permute-start.7 = (f32[96,128]{1,0:T(8,128)S(1)}, f32[96,128]{1,0:T(8,128)S(1)}, u32[]{:S(2)}, u32[]{:S(2)}) collective-permute-start(f32[96,128]{1,0:T(8,128)S(1)} %get-tuple-element.102), channel_id=1, source_target_pairs={{0,4},{1,3},{2,6},{3,1},{4,0},{5,7},{6,2},{7,5},{8,12},{9,11},{10,... | collective-permute-start | bytes 147464 | tf_op jit(solution)/shard_map/ppermute | solution.py:913
  36.4 1.6 %collective-permute-start.8 = (f32[128,128]{1,0:T(8,128)S(1)}, f32[128,128]{1,0:T(8,128)S(1)}, u32[]{:S(2)}, u32[]{:S(2)}) collective-permute-start(f32[128,128]{1,0:T(8,128)S(1)} %get-tuple-element.104.token_ref), channel_id=1, source_target_pairs={{0,1},{1,0},{2,3},{3,2},{4,5},{5,4},{6,7},{7,6},{8,9},{9,8},{10,11... | collective-permute-start | bytes 196616 | tf_op jit(solution)/shard_map/ppermute | solution.py:853
